TPU v7x, 128 devices: a whole 4x4x4 slice. The times are simulated.
128 devices in a mesh: section: 16 (over x_lo, z, core), expert: 8 (over y, x_hi).
Axes of the slice: x: 4 (x_hi: 2, x_lo: 2; x = x_hi * 2 + x_lo), y: 4, z: 4, core: 2. Of those that a mesh axis runs over, the one named last changes fastest.
Arguments:
- acts: bfloat16 [16, 512, 6144], P('section', 'expert'), may hold values from -6 to 6
- norm_gain: float32 [16, 6144], P('section'), may hold values from 0.1 to 1.9
- w_gate: bfloat16 [16, 8, 6144, 640], P('section', 'expert'), may hold values from -0.078125 to 0.078125
- w_up: bfloat16 [16, 8, 6144, 640], P('section', 'expert'), may hold values from -0.078125 to 0.078125
- w_down: bfloat16 [16, 8, 640, 6144], P('section', 'expert'), may hold values from -0.25 to 0.25
- routes: int32 [4, 16, 512, 4], P(None, 'section', 'expert'), may hold values from 0 to 7, all different within a row; in each aligned block of 64 rows (0 to 63, 64 to 127, ..., all dimensions but the last counted through in order) at most 48 rows name the same one
- gates: float32 [4, 16, 512, 4], P(None, 'section', 'expert'), may hold values from 0.2 to 1
Outputs:
- final_acts: bfloat16 [16, 512, 6144], P('section', 'expert')
Inputs may be any that keep to these rules, and one draw needn't show every extreme that they name: `routes`: each row names 4 different experts. Within the rows of one device for one tick no expert is named by more than 48 rows, a bound that some block reaches.
All inputs are finite; a program needn't handle non-finite values.
Results may differ from a plain program's by a relative error of at most 0.02.
Values may be sent and summed in bfloat16 or wider, within the bound.
No kernel may reach another device: no remote copies, remote signals or barrier semaphores. Data moves between devices by JAX's collectives and lax.ppermute only.
A program may use at most 128 MiB of HBM per device.

v0:
```python
import jax
import jax.numpy as jnp
from jax import lax
from jax.sharding import PartitionSpec as P

TICKS = 4
CAP = 48


def shifted(value, axis, by):
    size = lax.axis_size(axis)
    return lax.ppermute(value, axis, [(i, (i + by) % size) for i in range(size)])


def normalize(rows, gain):
    values = rows.astype(jnp.float32)
    meansq = jnp.mean(values * values, axis=-1, keepdims=True)
    return (values * lax.rsqrt(meansq + 1e-05) * gain[None, :]).astype(jnp.bfloat16)


def slot_targets(route, experts, slots):
    tok_rows, chosen = route.shape
    flat = route.reshape(tok_rows * chosen)
    onehot = (flat[:, None] == jnp.arange(experts, dtype=jnp.int32)[None, :]).astype(jnp.int32)
    before = jnp.cumsum(onehot, axis=0) - onehot
    position = jnp.sum(before * onehot, axis=1)
    return (flat * slots + position).reshape(tok_rows, chosen)


def body(acts, norm_gain, w_gate, w_up, w_down, routes, gates):
    groups = lax.axis_size("expert")
    exp_dev = w_gate.shape[1]
    experts = groups * exp_dev
    slots = CAP
    width = acts.shape[2]
    state = acts[0]
    gain = norm_gain[0]
    for tick in range(TICKS):
        normed = normalize(state, gain)
        route = routes[tick, 0]
        gate = gates[tick, 0]
        target = slot_targets(route, experts, slots)
        slot_rows = experts * slots
        slot_ids = jnp.arange(slot_rows, dtype=jnp.int32)
        placer = jnp.sum(
            (slot_ids[:, None, None] == target[None, :, :]).astype(jnp.bfloat16), axis=2
        )
        packed = jnp.dot(placer, normed, preferred_element_type=jnp.float32).astype(jnp.bfloat16)
        packed = packed.reshape(groups, exp_dev, slots, width)
        received = lax.all_to_all(packed, "expert", split_axis=0, concat_axis=2, tiled=True)
        inputs = received[0]
        gated = jnp.einsum("erd,edf->erf", inputs, w_gate[0], preferred_element_type=jnp.float32)
        upper = jnp.einsum("erd,edf->erf", inputs, w_up[0], preferred_element_type=jnp.float32)
        hidden = (jax.nn.silu(gated) * upper).astype(jnp.bfloat16)
        output = jnp.einsum(
            "erf,efd->erd", hidden, w_down[0], preferred_element_type=jnp.float32
        ).astype(jnp.bfloat16)
        output = output.reshape(1, exp_dev, groups * slots, width)
        returned = lax.all_to_all(output, "expert", split_axis=2, concat_axis=0, tiled=True)
        returned = returned.reshape(slot_rows, width)
        mixed = state.astype(jnp.float32)
        for pick in range(route.shape[1]):
            selector = (target[:, pick][:, None] == slot_ids[None, :]).astype(jnp.bfloat16)
            chosen_rows = jnp.dot(selector, returned, preferred_element_type=jnp.float32)
            mixed = mixed + gate[:, pick][:, None] * chosen_rows
        state = mixed.astype(jnp.bfloat16)
        state = shifted(state, "section", 1)
    return state[None]


def solution(mesh):
    return jax.shard_map(
        body,
        mesh=mesh,
        in_specs=(
            P("section", "expert", None),
            P("section", None),
            P("section", "expert", None, None),
            P("section", "expert", None, None),
            P("section", "expert", None, None),
            P(None, "section", "expert", None),
            P(None, "section", "expert", None),
        ),
        out_specs=P("section", "expert", None),
        check_vma=False,
    )
```

profile of v0, /device:TPU:2, one launch (start us, length us, event | category | flops | bytes accessed | tf_op | source)
XLA Modules:
  0.0 911.7 jit_solution(11628334221994587278)
XLA Ops:
  0.0 1.3 fusion.189
  2.9 1.4 fusion.77
  4.3 2.7 convolution_convert_fusion.7
  7.1 63.3 %all_to_all.32 = bf16[8,1,48,6144]{3,2,1,0:T(8,128)(2,1)S(1)} all-to-all(bf16[8,1,48,6144]{3,2,1,0:T(8,128)(2,1)S(1)} %bitcast.261), channel_id=1, replica_groups=mesh['section'=16,'expert'=8] {'expert'}, dimensions={0} | all-to-all | bytes 9437184 | tf_op jit(solution)/shard_map/all_to_all | solution.py:50
  70.4 2.1 copy-done.1
  72.5 3.8 fusion.18
  76.3 18.8 %fusion.20 = bf16[1,1,384,6144]{3,2,1,0:T(8,128)(2,1)} fusion(bf16[1,1,640,6144]{3,2,1,0:T(8,128)(2,1)} %param.11, bf16[384,6144]{1,0:T(8,128)(2,1)} %bitcast.266, bf16[1,1,6144,640]{3,2,1,0:T(8,128)(2,1)} %param.10, f32[384,640]{1,0:T(8,128)S(1)} %fusion.18), kind=kOutput, calls=%fused_computation.28 | convolution fusion | flops 6043631616 | bytes 26148864 | tf_op jit(solution)/shard_map/erf,efd->erd/dot_general | solution.py:55
  95.1 9.6 %copy.75 = bf16[1,1,384,6144]{3,1,0,2:T(2,128)(2,1)} copy(bf16[1,1,384,6144]{3,2,1,0:T(8,128)(2,1)} %fusion.20) | data formatting | bytes 9437184 | tf_op jit(solution)/shard_map/reshape | solution.py:58
  105.3 30.2 %reduce.44 = bf16[384,6144]{1,0:T(8,128)(2,1)} reduce(bf16[384,1,1,6144]{3,2,1,0:T(2,128)(2,1)} %bitcast.253, bf16[]{:T(256)} %broadcast.189), dimensions={1,2}, to_apply=%bitcast.252.reduce_sub_computation | reduce | bytes 9437186
  135.5 8.2 reshape.384
  143.7 4.7 all-to-all-start.1
  149.5 54.5 %all-to-all-done.1 = bf16[8,2,147456]{2,1,0:T(2,128)(2,1)} async-done(((bf16[8,2,147456]{2,1,0:T(2,128)(2,1)}), bf16[8,2,147456]{2,1,0:T(2,128)(2,1)}, u32[]{:S(2)}, u32[]{:S(2)}) %all-to-all-start.1) | async-done | bytes 4718624 | tf_op jit(solution)/shard_map/all_to_all | solution.py:59
  204.0 9.3 %reshape.385 = bf16[384,1,1,6144]{3,2,1,0:T(2,128)(2,1)} reshape(bf16[8,2,147456]{2,1,0:T(2,128)(2,1)} %all-to-all-done.1) | data formatting | bytes 9437184
  213.4 6.5 copy.60
  219.8 1.0 convolution_multiply_fusion.13
  221.8 1.0 convolution_multiply_fusion.12
  222.9 1.4 fusion.51
  225.7 12.2 %collective-permute-done = bf16[64,6144]{1,0:T(8,128)(2,1)S(1)} collective-permute-done((bf16[64,6144]{1,0:T(8,128)(2,1)S(1)}, bf16[64,6144]{1,0:T(8,128)(2,1)S(1)}, u32[]{:S(2)}, u32[]{:S(2)}) %collective-permute-start) | collective-permute-done | bytes 786464 | tf_op jit(solution)/shard_map/ppermute | solution.py:12
  238.2 1.4 convolution_convert_fusion.5
  239.7 57.3 %all_to_all.33 = bf16[8,1,48,6144]{3,2,1,0:T(8,128)(2,1)S(1)} all-to-all(bf16[8,1,48,6144]{3,2,1,0:T(8,128)(2,1)S(1)} %bitcast.262), channel_id=1, replica_groups=mesh['section'=16,'expert'=8] {'expert'}, dimensions={0} | all-to-all | bytes 9437184 | tf_op jit(solution)/shard_map/all_to_all | solution.py:50
  297.0 2.1 copy-done.2
  299.2 3.8 fusion.16
  303.0 18.8 %fusion.23 = bf16[1,1,384,6144]{3,2,1,0:T(8,128)(2,1)} fusion(bf16[1,1,640,6144]{3,2,1,0:T(8,128)(2,1)} %param.11, bf16[384,6144]{1,0:T(8,128)(2,1)} %bitcast.268, bf16[1,1,6144,640]{3,2,1,0:T(8,128)(2,1)} %param.10, f32[384,640]{1,0:T(8,128)S(1)} %fusion.16), kind=kOutput, calls=%fused_computation.29 | convolution fusion | flops 6043631616 | bytes 26148864 | tf_op jit(solution)/shard_map/erf,efd->erd/dot_general | solution.py:55
  321.8 9.6 %copy.74 = bf16[1,1,384,6144]{3,1,0,2:T(2,128)(2,1)} copy(bf16[1,1,384,6144]{3,2,1,0:T(8,128)(2,1)} %fusion.23) | data formatting | bytes 9437184 | tf_op jit(solution)/shard_map/reshape | solution.py:58
  331.4 30.1 %reduce.45 = bf16[384,6144]{1,0:T(8,128)(2,1)} reduce(bf16[384,1,1,6144]{3,2,1,0:T(2,128)(2,1)} %bitcast.256, bf16[]{:T(256)} %broadcast.189), dimensions={1,2}, to_apply=%bitcast.251.reduce_sub_computation | reduce | bytes 9437186
  361.4 8.2 reshape.386
  369.6 4.6 all-to-all-start.3
  374.8 53.0 %all-to-all-done.3 = bf16[8,2,147456]{2,1,0:T(2,128)(2,1)} async-done(((bf16[8,2,147456]{2,1,0:T(2,128)(2,1)}), bf16[8,2,147456]{2,1,0:T(2,128)(2,1)}, u32[]{:S(2)}, u32[]{:S(2)}) %all-to-all-start.3) | async-done | bytes 4718624 | tf_op jit(solution)/shard_map/all_to_all | solution.py:59
  427.7 9.3 %reshape.387 = bf16[384,1,1,6144]{3,2,1,0:T(2,128)(2,1)} reshape(bf16[8,2,147456]{2,1,0:T(2,128)(2,1)} %all-to-all-done.3) | data formatting | bytes 9437184
  437.1 6.5 copy.61
  446.5 1.4 fusion.50
  449.2 12.2 %collective-permute-done.1 = bf16[64,6144]{1,0:T(8,128)(2,1)S(1)} collective-permute-done((bf16[64,6144]{1,0:T(8,128)(2,1)S(1)}, bf16[64,6144]{1,0:T(8,128)(2,1)S(1)}, u32[]{:S(2)}, u32[]{:S(2)}) %collective-permute-start.1) | collective-permute-done | bytes 786464 | tf_op jit(solution)/shard_map/ppermute | solution.py:12
  461.8 1.5 convolution_convert_fusion.3
  463.2 60.4 %all_to_all.34 = bf16[8,1,48,6144]{3,2,1,0:T(8,128)(2,1)S(1)} all-to-all(bf16[8,1,48,6144]{3,2,1,0:T(8,128)(2,1)S(1)} %bitcast.263), channel_id=1, replica_groups=mesh['section'=16,'expert'=8] {'expert'}, dimensions={0} | all-to-all | bytes 9437184 | tf_op jit(solution)/shard_map/all_to_all | solution.py:50
  523.6 2.1 copy-done.3
  525.7 3.8 fusion.14
  529.5 18.8 %fusion.26 = bf16[1,1,384,6144]{3,2,1,0:T(8,128)(2,1)} fusion(bf16[1,1,640,6144]{3,2,1,0:T(8,128)(2,1)} %param.11, bf16[384,6144]{1,0:T(8,128)(2,1)} %bitcast.270, bf16[1,1,6144,640]{3,2,1,0:T(8,128)(2,1)} %param.10, f32[384,640]{1,0:T(8,128)S(1)} %fusion.14), kind=kOutput, calls=%fused_computation.30 | convolution fusion | flops 6043631616 | bytes 26148864 | tf_op jit(solution)/shard_map/erf,efd->erd/dot_general | solution.py:55
  548.3 9.6 %copy.73 = bf16[1,1,384,6144]{3,1,0,2:T(2,128)(2,1)} copy(bf16[1,1,384,6144]{3,2,1,0:T(8,128)(2,1)} %fusion.26) | data formatting | bytes 9437184 | tf_op jit(solution)/shard_map/reshape | solution.py:58
  557.9 30.0 %reduce.46 = bf16[384,6144]{1,0:T(8,128)(2,1)} reduce(bf16[384,1,1,6144]{3,2,1,0:T(2,128)(2,1)} %bitcast.258, bf16[]{:T(256)} %broadcast.189), dimensions={1,2}, to_apply=%bitcast.250.reduce_sub_computation | reduce | bytes 9437186
  587.9 8.2 reshape.388
  596.1 4.7 all-to-all-start.5
  601.4 55.8 %all-to-all-done.5 = bf16[8,2,147456]{2,1,0:T(2,128)(2,1)} async-done(((bf16[8,2,147456]{2,1,0:T(2,128)(2,1)}), bf16[8,2,147456]{2,1,0:T(2,128)(2,1)}, u32[]{:S(2)}, u32[]{:S(2)}) %all-to-all-start.5) | async-done | bytes 4718624 | tf_op jit(solution)/shard_map/all_to_all | solution.py:59
  657.2 9.3 %reshape.389 = bf16[384,1,1,6144]{3,2,1,0:T(2,128)(2,1)} reshape(bf16[8,2,147456]{2,1,0:T(2,128)(2,1)} %all-to-all-done.5) | data formatting | bytes 9437184
  666.5 6.5 copy.62
  673.0 1.0 convolution_multiply_fusion.5
  674.0 1.0 convolution_multiply_fusion.6
  675.9 1.4 fusion.49
  678.7 12.2 %collective-permute-done.2 = bf16[64,6144]{1,0:T(8,128)(2,1)S(1)} collective-permute-done((bf16[64,6144]{1,0:T(8,128)(2,1)S(1)}, bf16[64,6144]{1,0:T(8,128)(2,1)S(1)}, u32[]{:S(2)}, u32[]{:S(2)}) %collective-permute-start.2) | collective-permute-done | bytes 786464 | tf_op jit(solution)/shard_map/ppermute | solution.py:12
  691.2 1.5 convolution_convert_fusion.1
  692.7 55.0 %all_to_all.35 = bf16[8,1,48,6144]{3,2,1,0:T(8,128)(2,1)S(1)} all-to-all(bf16[8,1,48,6144]{3,2,1,0:T(8,128)(2,1)S(1)} %bitcast.264), channel_id=1, replica_groups=mesh['section'=16,'expert'=8] {'expert'}, dimensions={0} | all-to-all | bytes 9437184 | tf_op jit(solution)/shard_map/all_to_all | solution.py:50
  747.7 2.1 copy-done.4
  749.9 3.8 fusion.12
  753.7 18.8 %fusion.29 = bf16[1,1,384,6144]{3,2,1,0:T(8,128)(2,1)} fusion(bf16[1,1,640,6144]{3,2,1,0:T(8,128)(2,1)} %param.11, bf16[384,6144]{1,0:T(8,128)(2,1)} %bitcast.272, bf16[1,1,6144,640]{3,2,1,0:T(8,128)(2,1)} %param.10, f32[384,640]{1,0:T(8,128)S(1)} %fusion.12), kind=kOutput, calls=%fused_computation.31 | convolution fusion | flops 6043631616 | bytes 26148864 | tf_op jit(solution)/shard_map/erf,efd->erd/dot_general | solution.py:55
  772.5 9.6 %copy.72 = bf16[1,1,384,6144]{3,1,0,2:T(2,128)(2,1)} copy(bf16[1,1,384,6144]{3,2,1,0:T(8,128)(2,1)} %fusion.29) | data formatting | bytes 9437184 | tf_op jit(solution)/shard_map/reshape | solution.py:58
  782.0 30.1 %reduce.47 = bf16[384,6144]{1,0:T(8,128)(2,1)} reduce(bf16[384,1,1,6144]{3,2,1,0:T(2,128)(2,1)} %bitcast.254, bf16[]{:T(256)} %broadcast.189), dimensions={1,2}, to_apply=%bitcast.249.reduce_sub_computation | reduce | bytes 9437186
  812.2 8.2 reshape.390
  820.3 4.7 all-to-all-start.7
  825.3 50.7 %all-to-all-done.7 = bf16[8,2,147456]{2,1,0:T(2,128)(2,1)} async-done(((bf16[8,2,147456]{2,1,0:T(2,128)(2,1)}), bf16[8,2,147456]{2,1,0:T(2,128)(2,1)}, u32[]{:S(2)}, u32[]{:S(2)}) %all-to-all-start.7) | async-done | bytes 4718624 | tf_op jit(solution)/shard_map/all_to_all | solution.py:59
  876.0 9.3 %reshape.391 = bf16[384,1,1,6144]{3,2,1,0:T(2,128)(2,1)} reshape(bf16[8,2,147456]{2,1,0:T(2,128)(2,1)} %all-to-all-done.7) | data formatting | bytes 9437184
  885.3 6.5 copy.63
  891.8 1.0 convolution_multiply_fusion.1
  892.8 1.0 convolution_multiply_fusion.2
  894.7 1.4 fusion.48
  896.2 14.2 %collective-permute-done.3 = bf16[64,6144]{1,0:T(8,128)(2,1)S(1)} collective-permute-done((bf16[64,6144]{1,0:T(8,128)(2,1)S(1)}, bf16[64,6144]{1,0:T(8,128)(2,1)S(1)}, u32[]{:S(2)}, u32[]{:S(2)}) %collective-permute-start.3) | collective-permute-done | bytes 786464 | tf_op jit(solution)/shard_map/ppermute | solution.py:12
  (114 shorter events, 16.3 us)
Async XLA Ops:
  4.3 68.2 %slice-start = ((s8[7864320]{0:T(1024)(128)(4,1)}), s8[4194304]{0:T(1024)(128)(4,1)S(1)}, s32[]{:S(2)}) async-start(s8[7864320]{0:T(1024)(128)(4,1)} %bitcast.278), calls=%async_computation.8 | async-start | bytes 8388608
  7.1 65.5 %slice-start.1 = ((s8[7864320]{0:T(1024)(128)(4,1)}), s8[3670016]{0:T(1024)(128)(4,1)S(1)}, s32[]{:S(2)}) async-start(s8[7864320]{0:T(1024)(128)(4,1)} %bitcast.278), calls=%async_computation.9 | async-start | bytes 7340032
  70.4 2.1 copy-start.1
  143.7 5.3 copy-start.6
  143.7 60.4 %all-to-all-start.1 = ((bf16[8,2,147456]{2,1,0:T(2,128)(2,1)}), bf16[8,2,147456]{2,1,0:T(2,128)(2,1)}, u32[]{:S(2)}, u32[]{:S(2)}) async-start(bf16[8,2,147456]{2,1,0:T(2,128)(2,1)} %reshape.384), calls=%async_computation.1 | async-start | bytes 9437184 | tf_op jit(solution)/shard_map/all_to_all | solution.py:59
  221.8 1.1 copy-start
  222.9 15.3 %copy-start.5 = (f32[1,6144]{1,0:T(1,128)S(1)}, f32[1,6144]{1,0:T(1,128)}, u32[]{:S(2)}) copy-start(f32[1,6144]{1,0:T(1,128)} %param.8) | copy-start | bytes 73732
  224.3 13.6 %collective-permute-start = (bf16[64,6144]{1,0:T(8,128)(2,1)S(1)}, bf16[64,6144]{1,0:T(8,128)(2,1)S(1)}, u32[]{:S(2)}, u32[]{:S(2)}) collective-permute-start(bf16[64,6144]{1,0:T(8,128)(2,1)S(1)} %fusion.51), channel_id=1, source_target_pairs={{0,8},{8,16},{16,24},{24,32},{32,40},{40,48},{48,56},{56,64},{64,7... | collective-permute-start | bytes 2359304 | tf_op jit(solution)/shard_map/ppermute | solution.py:12
  238.2 60.9 %slice-start.2 = ((s8[7864320]{0:T(1024)(128)(4,1)}), s8[4194304]{0:T(1024)(128)(4,1)S(1)}, s32[]{:S(2)}) async-start(s8[7864320]{0:T(1024)(128)(4,1)} %bitcast.280), calls=%async_computation.10 | async-start | bytes 8388608
  239.7 59.5 %slice-start.3 = ((s8[7864320]{0:T(1024)(128)(4,1)}), s8[3670016]{0:T(1024)(128)(4,1)S(1)}, s32[]{:S(2)}) async-start(s8[7864320]{0:T(1024)(128)(4,1)} %bitcast.280), calls=%async_computation.11 | async-start | bytes 7340032
  297.0 2.1 copy-start.2
  369.6 58.1 %all-to-all-start.3 = ((bf16[8,2,147456]{2,1,0:T(2,128)(2,1)}), bf16[8,2,147456]{2,1,0:T(2,128)(2,1)}, u32[]{:S(2)}, u32[]{:S(2)}) async-start(bf16[8,2,147456]{2,1,0:T(2,128)(2,1)} %reshape.386), calls=%async_computation.3 | async-start | bytes 9437184 | tf_op jit(solution)/shard_map/all_to_all | solution.py:59
  447.9 13.6 %collective-permute-start.1 = (bf16[64,6144]{1,0:T(8,128)(2,1)S(1)}, bf16[64,6144]{1,0:T(8,128)(2,1)S(1)}, u32[]{:S(2)}, u32[]{:S(2)}) collective-permute-start(bf16[64,6144]{1,0:T(8,128)(2,1)S(1)} %fusion.50), channel_id=1, source_target_pairs={{0,8},{8,16},{16,24},{24,32},{32,40},{40,48},{48,56},{56,64},{64,7... | collective-permute-start | bytes 2359304 | tf_op jit(solution)/shard_map/ppermute | solution.py:12
  461.7 64.0 %slice-start.4 = ((s8[7864320]{0:T(1024)(128)(4,1)}), s8[4194304]{0:T(1024)(128)(4,1)S(1)}, s32[]{:S(2)}) async-start(s8[7864320]{0:T(1024)(128)(4,1)} %bitcast.282), calls=%async_computation.12 | async-start | bytes 8388608
  463.2 62.5 %slice-start.5 = ((s8[7864320]{0:T(1024)(128)(4,1)}), s8[3670016]{0:T(1024)(128)(4,1)S(1)}, s32[]{:S(2)}) async-start(s8[7864320]{0:T(1024)(128)(4,1)} %bitcast.282), calls=%async_computation.13 | async-start | bytes 7340032
  523.6 2.1 copy-start.3
  596.1 4.7 copy-start.7
  596.1 61.1 %all-to-all-start.5 = ((bf16[8,2,147456]{2,1,0:T(2,128)(2,1)}), bf16[8,2,147456]{2,1,0:T(2,128)(2,1)}, u32[]{:S(2)}, u32[]{:S(2)}) async-start(bf16[8,2,147456]{2,1,0:T(2,128)(2,1)} %reshape.388), calls=%async_computation.5 | async-start | bytes 9437184 | tf_op jit(solution)/shard_map/all_to_all | solution.py:59
  677.4 13.6 %collective-permute-start.2 = (bf16[64,6144]{1,0:T(8,128)(2,1)S(1)}, bf16[64,6144]{1,0:T(8,128)(2,1)S(1)}, u32[]{:S(2)}, u32[]{:S(2)}) collective-permute-start(bf16[64,6144]{1,0:T(8,128)(2,1)S(1)} %fusion.49), channel_id=1, source_target_pairs={{0,8},{8,16},{16,24},{24,32},{32,40},{40,48},{48,56},{56,64},{64,7... | collective-permute-start | bytes 2359304 | tf_op jit(solution)/shard_map/ppermute | solution.py:12
  691.2 58.6 %slice-start.6 = ((s8[7864320]{0:T(1024)(128)(4,1)}), s8[4194304]{0:T(1024)(128)(4,1)S(1)}, s32[]{:S(2)}) async-start(s8[7864320]{0:T(1024)(128)(4,1)} %bitcast.284), calls=%async_computation.14 | async-start | bytes 8388608
  692.7 57.2 %slice-start.7 = ((s8[7864320]{0:T(1024)(128)(4,1)}), s8[3670016]{0:T(1024)(128)(4,1)S(1)}, s32[]{:S(2)}) async-start(s8[7864320]{0:T(1024)(128)(4,1)} %bitcast.284), calls=%async_computation.15 | async-start | bytes 7340032
  747.7 2.1 copy-start.4
  820.3 5.0 copy-start.8
  820.3 55.6 %all-to-all-start.7 = ((bf16[8,2,147456]{2,1,0:T(2,128)(2,1)}), bf16[8,2,147456]{2,1,0:T(2,128)(2,1)}, u32[]{:S(2)}, u32[]{:S(2)}) async-start(bf16[8,2,147456]{2,1,0:T(2,128)(2,1)} %reshape.390), calls=%async_computation.7 | async-start | bytes 9437184 | tf_op jit(solution)/shard_map/all_to_all | solution.py:59
  896.1 14.3 %collective-permute-start.3 = (bf16[64,6144]{1,0:T(8,128)(2,1)S(1)}, bf16[64,6144]{1,0:T(8,128)(2,1)S(1)}, u32[]{:S(2)}, u32[]{:S(2)}) collective-permute-start(bf16[64,6144]{1,0:T(8,128)(2,1)S(1)} %fusion.48), channel_id=1, source_target_pairs={{0,8},{8,16},{16,24},{24,32},{32,40},{40,48},{48,56},{56,64},{64,7... | collective-permute-start | bytes 2359304 | tf_op jit(solution)/shard_map/ppermute | solution.py:12
where the time goes:
time: 924 us; the launch traced here: 912 us
  waiting for transfers between devices  265 us (29%)
  blocking collectives  236 us (26%)
  local copies, waits for them, and re-layouts  150 us (16%)
  other arithmetic  126 us (14%)
  matrix products  115 us (12%)
  starting transfers between devices  19 us (2%)
    all_to_all x4, blocking collectives, body(): lax.all_to_all(packed, 'expert', split_axis=0, concat_axis=2, tiled=True)  236 us
    all_to_all x4, waiting for transfers between devices, body(): lax.all_to_all(output, 'expert', split_axis=2, concat_axis=0, tiled=True)  214 us
    unnamed x8, other arithmetic  120 us
    unnamed x52, local copies, waits for them, and re-layouts  106 us
    dot_general x4, matrix products, body(): jnp.einsum('erf,efd->erd', hidden, w_down[0], preferred_element_type=jnp....  75.2 us
    ppermute x4, waiting for transfers between devices, shifted(): lax.ppermute(value, axis, [(i, (i + by) % size) for i in range(size)])  50.9 us
    reshape x4, local copies, waits for them, and re-layouts, body(): output = output.reshape(1, exp_dev, groups * slots, width)  38.3 us
    all_to_all x4, starting transfers between devices, body(): lax.all_to_all(output, 'expert', split_axis=2, concat_axis=0, tiled=True)  18.7 us
  transfers between devices with their start and end apart: 8, of which 8 were waited for; matrix products, arithmetic and copies ran while one was open for 1% of the time, Pallas kernels for 0%

commit v1 on v0

v1 whole, which is shorter than its diff:
```python
import functools

import jax
import jax.numpy as jnp
from jax import lax
from jax.experimental import pallas as pl
from jax.experimental.pallas import tpu as pltpu
from jax.sharding import PartitionSpec as P

TICKS = 4
STREAMS = 1
FIRST = 3584
DEEP = 1024
WIDE = 1024
RINGS = [[0, 2, 4, 6], [1, 3, 5, 7]]


def relayed(value):
    return lax.ppermute(value, "section", [(i, (i + 1) % 16) for i in range(16)])


def relayed_across(value):
    pairs = [(s * 8 + e, ((s + 1) % 16) * 8 + (e ^ 1)) for s in range(16) for e in range(8)]
    return lax.ppermute(value, ("section", "expert"), pairs)


def across(value):
    return lax.ppermute(value, "expert", [(i, i ^ 1) for i in range(8)])


def upward(value):
    return lax.ppermute(value, "expert", [(i, (i + 2) % 8) for i in range(8)])


def downward(value):
    return lax.ppermute(value, "expert", [(i, (i - 2) % 8) for i in range(8)])


def plus(*terms):
    total = terms[0].astype(jnp.float32)
    for term in terms[1:]:
        total = total + term.astype(jnp.float32)
    return total


def normalize(first, second, gain):
    split = first.shape[1]
    one, two = first.astype(jnp.float32), second.astype(jnp.float32)
    total = jnp.sum(one * one, axis=-1, keepdims=True) + jnp.sum(two * two, axis=-1, keepdims=True)
    scale = lax.rsqrt(total / gain.shape[0] + 1e-05)
    one = (one * scale * gain[None, :split]).astype(jnp.bfloat16)
    two = (two * scale * gain[None, split:]).astype(jnp.bfloat16)
    return one, two


def gather(first, second):
    half = first.shape[1] // 2
    near = lax.all_gather(second, "expert", axis=0, axis_index_groups=RINGS)
    other = across(first)
    own_l = jnp.concatenate([first[:, :half], other[:, :half]], axis=0)
    own_r = jnp.concatenate([first[:, half:], other[:, half:]], axis=0)
    below_l, above_r = upward(own_l), downward(own_r)
    below_r, above_l = upward(own_r), downward(own_l)
    opp_l, opp_r = upward(below_l), downward(above_r)
    far = across(near)
    return (own_l, own_r, below_l, below_r, above_l, above_r, opp_l, opp_r), (near, far)


def scatter_sum(pieces, near, far, rows):
    own_l, own_r, below_l, below_r, above_l, above_r, opp_l, opp_r = pieces
    other = across(far)
    arrived_l, arrived_r = upward(opp_l), downward(opp_r)
    sum_r, sum_l = upward(above_r), downward(below_l)
    both = plus(near, other).astype(jnp.bfloat16)
    second = lax.psum_scatter(both, "expert", scatter_dimension=0, axis_index_groups=RINGS)
    above_l = plus(above_l, arrived_l).astype(jnp.bfloat16)
    below_r = plus(below_r, arrived_r).astype(jnp.bfloat16)
    top_l, low_r = upward(above_l), downward(below_r)
    left = plus(own_l, sum_l, top_l)
    right = plus(own_r, sum_r, low_r)
    return jnp.concatenate([left, right], axis=1), second


def mlp_kernel(split, rows, me_ref, weight_ref, gate_ref, up_ref, down_ref, *refs):
    pieces, (near, far) = refs[:8], refs[8:10]
    out_pieces, (out_near, out_far) = refs[10:18], refs[18:20]
    inputs, gated, upper, hidden = refs[20:]
    step = pl.program_id(0)
    half = split // 2
    width = inputs.shape[1]
    deep_steps = width // DEEP
    wide_steps = width // WIDE
    high, low = me_ref[0] // 2, me_ref[0] % 2

    def place(dy, dx):
        slot = lax.rem(high + dy, 4) * 2 + lax.rem(low + dx, 2)
        return pl.ds(pl.multiple_of(slot * rows, rows), rows)

    turns = (0, 3, 1, 2)

    @pl.when(step == 0)
    def _():
        for at in range(8):
            dy, side = turns[at // 2], at % 2
            for dx in range(2):
                inputs[place(dy, dx), side * half : (side + 1) * half] = pieces[at][dx * rows : (dx + 1) * rows, :]
        for y in range(4):
            for dx, source in ((0, near), (1, far)):
                slot = 2 * y + lax.rem(low + dx, 2)
                inputs[pl.ds(pl.multiple_of(slot * rows, rows), rows), split:] = source[y]
        gated[...] = jnp.zeros_like(gated)
        upper[...] = jnp.zeros_like(upper)

    @pl.when(step < deep_steps)
    def _():
        block = inputs[:, pl.ds(pl.multiple_of(step * DEEP, DEEP), DEEP)]
        gated[...] += jnp.dot(block, gate_ref[...], preferred_element_type=jnp.float32)
        upper[...] += jnp.dot(block, up_ref[...], preferred_element_type=jnp.float32)

    @pl.when(step == deep_steps - 1)
    def _():
        value = gated[...]
        hidden[...] = (value / (1.0 + jnp.exp(-value)) * upper[...]).astype(jnp.bfloat16)

    @pl.when(step >= deep_steps)
    def _():
        at = step - deep_steps
        output = jnp.dot(hidden[...], down_ref[...], preferred_element_type=jnp.float32)
        output = (output * weight_ref[...]).astype(jnp.bfloat16)
        inputs[:, pl.ds(pl.multiple_of(at * WIDE, WIDE), WIDE)] = output

    @pl.when(step == deep_steps + wide_steps - 1)
    def _():
        for at in range(8):
            dy, side = turns[at // 2], at % 2
            for dx in range(2):
                out_pieces[at][dx * rows : (dx + 1) * rows, :] = inputs[place(dy, dx), side * half : (side + 1) * half]
        for y in range(4):
            for dx, target in ((0, out_near), (1, out_far)):
                slot = 2 * y + lax.rem(low + dx, 2)
                target[y] = inputs[pl.ds(pl.multiple_of(slot * rows, rows), rows), split:]


def expert(me, weight, gate_w, up_w, down_w, pieces, near, far):
    width, inner = gate_w.shape
    rows = near.shape[1]
    total = rows * 8
    split = pieces[0].shape[1] * 2
    deep_steps, wide_steps = width // DEEP, width // WIDE
    whole = pl.BlockSpec(memory_space=pltpu.VMEM)
    shapes = [jax.ShapeDtypeStruct(p.shape, jnp.bfloat16) for p in (*pieces, near, far)]
    outs = pl.pallas_call(
        functools.partial(mlp_kernel, split, rows),
        grid=(deep_steps + wide_steps,),
        in_specs=[
            pl.BlockSpec(memory_space=pltpu.SMEM),
            whole,
            pl.BlockSpec((DEEP, inner), lambda i: (jnp.minimum(i, deep_steps - 1), 0)),
            pl.BlockSpec((DEEP, inner), lambda i: (jnp.minimum(i, deep_steps - 1), 0)),
            pl.BlockSpec((inner, WIDE), lambda i: (0, jnp.maximum(i - deep_steps, 0))),
        ]
        + [whole] * 10,
        out_specs=[whole] * 10,
        out_shape=shapes,
        scratch_shapes=[
            pltpu.VMEM((total, width), jnp.bfloat16),
            pltpu.VMEM((total, inner), jnp.float32),
            pltpu.VMEM((total, inner), jnp.float32),
            pltpu.VMEM((total, inner), jnp.bfloat16),
        ],
        compiler_params=pltpu.CompilerParams(
            dimension_semantics=("arbitrary",), vmem_limit_bytes=44 * 1024 * 1024
        ),
        cost_estimate=pl.CostEstimate(
            flops=6 * total * width * inner,
            bytes_accessed=6 * width * inner + 4 * total * width,
            transcendentals=total * inner,
        ),
        name="expert_mlp",
    )(me, weight, gate_w, up_w, down_w, *pieces, near, far)
    return outs[:8], outs[8], outs[9]


def body(acts, norm_gain, w_gate, w_up, w_down, routes, gates):
    gain = norm_gain[0]
    gate_w, up_w, down_w = w_gate[0, 0], w_up[0, 0], w_down[0, 0]
    tok_rows = acts.shape[1]
    rows = tok_rows // STREAMS
    me = lax.axis_index("expert")
    ids = jnp.arange(8, dtype=jnp.int32)
    chosen = (routes[:, 0, :, :, None] == ids).astype(jnp.float32)
    weights = jnp.sum(gates[:, 0, :, :, None] * chosen, axis=2)
    weights = jnp.transpose(weights, (2, 0, 1)).reshape(8, TICKS * tok_rows)
    weights = lax.all_to_all(weights, "expert", split_axis=0, concat_axis=0, tiled=True)
    weights = weights.reshape(8, TICKS, tok_rows)
    me = jnp.reshape(me, (1,)).astype(jnp.int32)
    states = [
        (acts[0, i * rows : (i + 1) * rows, :FIRST], acts[0, i * rows : (i + 1) * rows, FIRST:])
        for i in range(STREAMS)
    ]
    for tick in range(TICKS):
        done = []
        for stream, (first, second) in enumerate(states):
            pieces, (near, far) = gather(*normalize(first, second, gain))
            weight = weights[:, tick, stream * rows : (stream + 1) * rows].reshape(8 * rows, 1)
            pieces, near, far = expert(me, weight, gate_w, up_w, down_w, pieces, near, far)
            sums, more = scatter_sum(pieces, near, far, rows)
            kept = relayed((first.astype(jnp.float32) + sums[:rows]).astype(jnp.bfloat16))
            sent = relayed_across(sums[rows:].astype(jnp.bfloat16))
            second = relayed(plus(second, more).astype(jnp.bfloat16))
            done.append((plus(kept, sent).astype(jnp.bfloat16), second))
        states = done
    return jnp.concatenate([jnp.concatenate(state, axis=1) for state in states], axis=0)[None]


def solution(mesh):
    return jax.shard_map(
        body,
        mesh=mesh,
        in_specs=(
            P("section", "expert", None),
            P("section", None),
            P("section", "expert", None, None),
            P("section", "expert", None, None),
            P("section", "expert", None, None),
            P(None, "section", "expert", None),
            P(None, "section", "expert", None),
        ),
        out_specs=P("section", "expert", None),
        check_vma=False,
    )
```

time: 924 us -> 671 us (0.73)
  blocking collectives: 236 us -> 0 us
  matrix products: 115 us -> 0 us
  waiting for transfers between devices: 265 us -> 380 us
  local copies, waits for them, and re-layouts: 150 us -> 36.6 us
  Pallas kernels: 0 us -> 95.8 us
  other arithmetic: 126 us -> 31.9 us
  starting transfers between devices: 19 us -> 99.3 us
  between operations: 1.04 us -> 14.6 us
    ppermute x4 -> x72, waiting for transfers between devices: 50.9 us -> 293 us  [the longest x12 93.3 us: across(): return lax.ppermute(value, 'expert', [(i, i ^ 1) for i in range(8)])]
    all_to_all x4 -> x0, blocking collectives: 236 us -> none  [body(): lax.all_to_all(packed, 'expert', split_axis=0, concat_axis=2, tiled=True)]
    all_to_all x4 -> x1, waiting for transfers between devices: 214 us -> 11.5 us  [body(): lax.all_to_all(weights, 'expert', split_axis=0, concat_axis=0, tiled=True)]
    unnamed x8 -> x0, other arithmetic: 120 us -> none
    dot_general x28 -> x0, matrix products: 115 us -> none  [the longest x4 75.2 us: body(): jnp.einsum('erf,efd->erd', hidden, w_down[0], preferred_element_type=jnp....]
    pallas_call x0 -> x4, Pallas kernels: none -> 95.8 us  [expert(): pl.pallas_call(functools.partial(mlp_kernel, split, rows), grid=(deep_ste...]
    ppermute x4 -> x72, starting transfers between devices: 0.3 us -> 93.6 us  [the longest x24 47 us: downward(): return lax.ppermute(value, 'expert', [(i, (i - 2) % 8) for i in range(8)])]
    unnamed x52 -> x118, local copies, waits for them, and re-layouts: 106 us -> 34 us
  transfers between devices with their start and end apart: 8 -> 81, of which waited for: 8 -> 51; matrix products, arithmetic and copies ran while one was open for 1% -> 4% of each run, Pallas kernels for 0% -> 0%
where the time goes in v1:
time: 671 us; the launch traced here: 659 us
  waiting for transfers between devices  380 us (57%)
  starting transfers between devices  99.3 us (15%)
  Pallas kernels  95.8 us (14%)
  local copies, waits for them, and re-layouts  36.6 us (5%)
  other arithmetic  31.9 us (5%)
  between operations  14.6 us (2%)
    pallas_call x4, Pallas kernels, expert(): pl.pallas_call(functools.partial(mlp_kernel, split, rows), grid=(deep_ste...  95.8 us
    ppermute x12, waiting for transfers between devices, across(): return lax.ppermute(value, 'expert', [(i, i ^ 1) for i in range(8)])  93.3 us
    ppermute x24, waiting for transfers between devices, downward(): return lax.ppermute(value, 'expert', [(i, (i - 2) % 8) for i in range(8)])  83.2 us
    ppermute x24, waiting for transfers between devices, upward(): return lax.ppermute(value, 'expert', [(i, (i + 2) % 8) for i in range(8)])  71.1 us
    all_gather x4, waiting for transfers between devices, gather(): near = lax.all_gather(second, 'expert', axis=0, axis_index_groups=RINGS)  52.6 us
    ppermute x24, starting transfers between devices, downward(): return lax.ppermute(value, 'expert', [(i, (i - 2) % 8) for i in range(8)])  47 us
    unnamed x118, local copies, waits for them, and re-layouts  34 us
    ppermute x8, waiting for transfers between devices, relayed(): lax.ppermute(value, 'section', [(i, (i + 1) % 16) for i in range(16)])  29.6 us
  transfers between devices with their start and end apart: 81, of which 51 were waited for; matrix products, arithmetic and copies ran while one was open for 4% of the time, Pallas kernels for 0%

profile of v1, /device:TPU:2, one launch (start us, length us, event | category | flops | bytes accessed | tf_op | source)
XLA Modules:
  0.0 658.5 jit_solution(5270942486515004481)
XLA Ops:
  11.9 2.2 collective-permute-start
  14.1 11.6 %collective-permute-done = bf16[64,3584]{1,0:T(8,128)(2,1)S(1)} collective-permute-done((bf16[64,3584]{1,0:T(8,128)(2,1)S(1)}, bf16[64,3584]{1,0:T(8,128)(2,1)S(1)}, u32[]{:S(2)}, u32[]{:S(2)}) %collective-permute-start) | collective-permute-done | bytes 458784 | tf_op jit(solution)/shard_map/ppermute | solution.py:28
  25.7 13.3 %all-gather.8.cloned.1.call-done.refs_8_ = bf16[4,64,2560]{2,1,0:T(8,128)(2,1)} async-done(((bf16[1,64,2560]{2,1,0:T(8,128)(2,1)}), bf16[4,64,2560]{2,1,0:T(8,128)(2,1)}) %all-gather.8.cloned.1.call-update) | async-done | bytes 1310736 | tf_op jit(solution)/shard_map/all_gather | solution.py:58
  43.9 2.7 collective-permute-start.3
  46.6 8.1 %collective-permute-done.4.refs_5_ = bf16[128,1792]{1,0:T(8,128)(2,1)S(1)} collective-permute-done((bf16[128,1792]{1,0:T(8,128)(2,1)S(1)}, bf16[128,1792]{1,0:T(8,128)(2,1)S(1)}, u32[]{:S(2)}, u32[]{:S(2)}) %collective-permute-start.4) | collective-permute-done | bytes 458784 | tf_op jit(solution)/shard_map/ppermute | solution.py:36
  54.7 3.0 collective-permute-start.6
  58.5 5.4 all-to-all-start
  63.9 11.5 %all-to-all-done = f32[8,1,256]{2,1,0:T(1,128)S(1)} async-done(((f32[8,1,256]{2,1,0:T(1,128)}), f32[8,1,256]{2,1,0:T(1,128)S(1)}, u32[]{:S(2)}, u32[]{:S(2)}) %all-to-all-start) | async-done | bytes 8224 | tf_op jit(solution)/shard_map/all_to_all | solution.py:194
  81.3 24.2 %expert_mlp.4 = (bf16[128,1792]{1,0:T(8,128)(2,1)S(1)}, bf16[128,1792]{1,0:T(8,128)(2,1)S(1)}, bf16[128,1792]{1,0:T(8,128)(2,1)}, bf16[128,1792]{1,0:T(8,128)(2,...) custom-call(s32[1]{0:T(128)} %bitcast.1.me_ref, ...), custom_call_target="tpu_custom_call" | custom-call | flops 12079595520 | bytes 36175872 | tf_op jit(solution)/shard_map/expert_mlp/pallas_call | solution.py:152
  107.0 3.2 collective-permute-start.8
  112.2 9.4 %collective-permute-done.9 = bf16[128,1792]{1,0:T(8,128)(2,1)S(1)} collective-permute-done((bf16[128,1792]{1,0:T(8,128)(2,1)S(1)}, bf16[128,1792]{1,0:T(8,128)(2,1)S(1)}, u32[]{:S(2)}, u32[]{:S(2)}) %collective-permute-start.9) | collective-permute-done | bytes 458784 | tf_op jit(solution)/shard_map/ppermute | solution.py:32
  122.5 13.2 %collective-permute-done.16 = bf16[4,64,2560]{2,1,0:T(8,128)(2,1)S(1)} collective-permute-done((bf16[4,64,2560]{2,1,0:T(8,128)(2,1)S(1)}, bf16[4,64,2560]{2,1,0:T(8,128)(2,1)S(1)}, u32[]{:S(2)}, u32[]{:S(2)}) %collective-permute-start.16) | collective-permute-done | bytes 1310752 | tf_op jit(solution)/shard_map/ppermute | solution.py:28
  138.1 10.9 %collective-permute-done.13 = bf16[128,1792]{1,0:T(8,128)(2,1)S(1)} collective-permute-done((bf16[128,1792]{1,0:T(8,128)(2,1)S(1)}, bf16[128,1792]{1,0:T(8,128)(2,1)S(1)}, u32[]{:S(2)}, u32[]{:S(2)}) %collective-permute-start.13) | collective-permute-done | bytes 458784 | tf_op jit(solution)/shard_map/ppermute | solution.py:36
  151.2 8.5 %reduce-scatter.5.cloned.1.call-done = bf16[1,64,2560]{2,1,0:T(8,128)(2,1)} async-done(((bf16[4,64,2560]{2,1,0:T(8,128)(2,1)}), bf16[1,64,2560]{2,1,0:T(8,128)(2,1)}) %reduce-scatter.5.cloned.1.call-update) | async-done | bytes 327696 | tf_op jit(solution)/shard_map/reduce_scatter | solution.py:75
  162.8 4.6 collective-permute-done.15
  167.6 2.5 collective-permute-done.17
  173.6 9.0 %collective-permute-done.18 = bf16[64,3584]{1,0:T(8,128)(2,1)S(1)} collective-permute-done((bf16[64,3584]{1,0:T(8,128)(2,1)S(1)}, bf16[64,3584]{1,0:T(8,128)(2,1)S(1)}, u32[]{:S(2)}, u32[]{:S(2)}) %collective-permute-start.18) | collective-permute-done | bytes 458784 | tf_op jit(solution)/shard_map/ppermute | solution.py:28
  182.6 11.7 %all-gather.10.cloned.1.call-done = bf16[256,2560]{1,0:T(8,128)(2,1)} async-done(((bf16[64,2560]{1,0:T(8,128)(2,1)}), bf16[256,2560]{1,0:T(8,128)(2,1)}) %all-gather.10.cloned.1.call-update) | async-done | bytes 1310736 | tf_op jit(solution)/shard_map/all_gather | solution.py:58
  199.2 2.7 collective-permute-start.21
  201.9 8.1 %collective-permute-done.22.refs_5_ = bf16[128,1792]{1,0:T(8,128)(2,1)S(1)} collective-permute-done((bf16[128,1792]{1,0:T(8,128)(2,1)S(1)}, bf16[128,1792]{1,0:T(8,128)(2,1)S(1)}, u32[]{:S(2)}, u32[]{:S(2)}) %collective-permute-start.22) | collective-permute-done | bytes 458784 | tf_op jit(solution)/shard_map/ppermute | solution.py:36
  210.0 3.0 collective-permute-start.24
  214.7 8.2 %collective-permute-done.20.refs_3_ = bf16[128,1792]{1,0:T(8,128)(2,1)S(1)} collective-permute-done((bf16[128,1792]{1,0:T(8,128)(2,1)S(1)}, bf16[128,1792]{1,0:T(8,128)(2,1)S(1)}, u32[]{:S(2)}, u32[]{:S(2)}) %collective-permute-start.20) | collective-permute-done | bytes 458784 | tf_op jit(solution)/shard_map/ppermute | solution.py:32
  224.4 2.6 collective-permute-done.24.refs_7_
  227.8 2.9 collective-permute-done.23.refs_6_
  235.8 23.9 %expert_mlp.5 = (bf16[128,1792]{1,0:T(8,128)(2,1)S(1)}, bf16[128,1792]{1,0:T(8,128)(2,1)S(1)}, bf16[128,1792]{1,0:T(8,128)(2,1)S(1)}, bf16[128,1792]{1,0:T(8,128...) custom-call(s32[1]{0:T(128)} %bitcast.1.me_ref, ...), custom_call_target="tpu_custom_call" | custom-call | flops 12079595520 | bytes 36175872 | tf_op jit(solution)/shard_map/expert_mlp/pallas_call | solution.py:152
  261.1 3.2 collective-permute-start.26
  266.4 9.4 %collective-permute-done.27 = bf16[128,1792]{1,0:T(8,128)(2,1)S(1)} collective-permute-done((bf16[128,1792]{1,0:T(8,128)(2,1)S(1)}, bf16[128,1792]{1,0:T(8,128)(2,1)S(1)}, u32[]{:S(2)}, u32[]{:S(2)}) %collective-permute-start.27) | collective-permute-done | bytes 458784 | tf_op jit(solution)/shard_map/ppermute | solution.py:32
  276.6 13.2 %collective-permute-done.34 = bf16[4,64,2560]{2,1,0:T(8,128)(2,1)S(1)} collective-permute-done((bf16[4,64,2560]{2,1,0:T(8,128)(2,1)S(1)}, bf16[4,64,2560]{2,1,0:T(8,128)(2,1)S(1)}, u32[]{:S(2)}, u32[]{:S(2)}) %collective-permute-start.34) | collective-permute-done | bytes 1310752 | tf_op jit(solution)/shard_map/ppermute | solution.py:28
  294.8 10.7 %collective-permute-done.31 = bf16[128,1792]{1,0:T(8,128)(2,1)S(1)} collective-permute-done((bf16[128,1792]{1,0:T(8,128)(2,1)S(1)}, bf16[128,1792]{1,0:T(8,128)(2,1)S(1)}, u32[]{:S(2)}, u32[]{:S(2)}) %collective-permute-start.31) | collective-permute-done | bytes 458784 | tf_op jit(solution)/shard_map/ppermute | solution.py:36
  305.8 8.9 %collective-permute-start.32 = (bf16[64,3584]{1,0:T(8,128)(2,1)S(1)}, bf16[64,3584]{1,0:T(8,128)(2,1)S(1)}, u32[]{:S(2)}, u32[]{:S(2)}) collective-permute-start(bf16[64,3584]{1,0:T(8,128)(2,1)S(1)} %fusion.3), channel_id=1, source_target_pairs={{0,8},{8,16},{16,24},{24,32},{32,40},{40,48},{48,56},{56,64},{64,7... | collective-permute-start | bytes 1376264 | tf_op jit(solution)/shard_map/ppermute | solution.py:19
  317.7 11.3 %collective-permute-done.32 = bf16[64,3584]{1,0:T(8,128)(2,1)S(1)} collective-permute-done((bf16[64,3584]{1,0:T(8,128)(2,1)S(1)}, bf16[64,3584]{1,0:T(8,128)(2,1)S(1)}, u32[]{:S(2)}, u32[]{:S(2)}) %collective-permute-start.32) | collective-permute-done | bytes 458784 | tf_op jit(solution)/shard_map/ppermute | solution.py:19
  330.6 3.2 collective-permute-done.35
  336.2 10.3 %collective-permute-done.36 = bf16[64,3584]{1,0:T(8,128)(2,1)S(1)} collective-permute-done((bf16[64,3584]{1,0:T(8,128)(2,1)S(1)}, bf16[64,3584]{1,0:T(8,128)(2,1)S(1)}, u32[]{:S(2)}, u32[]{:S(2)}) %collective-permute-start.36) | collective-permute-done | bytes 458784 | tf_op jit(solution)/shard_map/ppermute | solution.py:28
  346.5 14.1 %all-gather.12.cloned.1.call-done = bf16[256,2560]{1,0:T(8,128)(2,1)} async-done(((bf16[64,2560]{1,0:T(8,128)(2,1)}), bf16[256,2560]{1,0:T(8,128)(2,1)}) %all-gather.12.cloned.1.call-update) | async-done | bytes 1310736 | tf_op jit(solution)/shard_map/all_gather | solution.py:58
  365.4 2.7 collective-permute-start.39
  368.1 8.1 %collective-permute-done.40.refs_5_ = bf16[128,1792]{1,0:T(8,128)(2,1)S(1)} collective-permute-done((bf16[128,1792]{1,0:T(8,128)(2,1)S(1)}, bf16[128,1792]{1,0:T(8,128)(2,1)S(1)}, u32[]{:S(2)}, u32[]{:S(2)}) %collective-permute-start.40) | collective-permute-done | bytes 458784 | tf_op jit(solution)/shard_map/ppermute | solution.py:36
  376.2 3.0 collective-permute-start.42
  381.0 8.2 %collective-permute-done.38.refs_3_ = bf16[128,1792]{1,0:T(8,128)(2,1)S(1)} collective-permute-done((bf16[128,1792]{1,0:T(8,128)(2,1)S(1)}, bf16[128,1792]{1,0:T(8,128)(2,1)S(1)}, u32[]{:S(2)}, u32[]{:S(2)}) %collective-permute-start.38) | collective-permute-done | bytes 458784 | tf_op jit(solution)/shard_map/ppermute | solution.py:32
  390.7 2.6 collective-permute-done.42.refs_7_
  394.1 2.9 collective-permute-done.41.refs_6_
  402.0 23.9 %expert_mlp.6 = (bf16[128,1792]{1,0:T(8,128)(2,1)S(1)}, bf16[128,1792]{1,0:T(8,128)(2,1)S(1)}, bf16[128,1792]{1,0:T(8,128)(2,1)S(1)}, bf16[128,1792]{1,0:T(8,128...) custom-call(s32[1]{0:T(128)} %bitcast.1.me_ref, ...), custom_call_target="tpu_custom_call" | custom-call | flops 12079595520 | bytes 36175872 | tf_op jit(solution)/shard_map/expert_mlp/pallas_call | solution.py:152
  427.4 3.2 collective-permute-start.44
  432.6 9.4 %collective-permute-done.45 = bf16[128,1792]{1,0:T(8,128)(2,1)S(1)} collective-permute-done((bf16[128,1792]{1,0:T(8,128)(2,1)S(1)}, bf16[128,1792]{1,0:T(8,128)(2,1)S(1)}, u32[]{:S(2)}, u32[]{:S(2)}) %collective-permute-start.45) | collective-permute-done | bytes 458784 | tf_op jit(solution)/shard_map/ppermute | solution.py:32
  442.9 13.2 %collective-permute-done.52 = bf16[4,64,2560]{2,1,0:T(8,128)(2,1)S(1)} collective-permute-done((bf16[4,64,2560]{2,1,0:T(8,128)(2,1)S(1)}, bf16[4,64,2560]{2,1,0:T(8,128)(2,1)S(1)}, u32[]{:S(2)}, u32[]{:S(2)}) %collective-permute-start.52) | collective-permute-done | bytes 1310752 | tf_op jit(solution)/shard_map/ppermute | solution.py:28
  461.0 10.7 %collective-permute-done.49 = bf16[128,1792]{1,0:T(8,128)(2,1)S(1)} collective-permute-done((bf16[128,1792]{1,0:T(8,128)(2,1)S(1)}, bf16[128,1792]{1,0:T(8,128)(2,1)S(1)}, u32[]{:S(2)}, u32[]{:S(2)}) %collective-permute-start.49) | collective-permute-done | bytes 458784 | tf_op jit(solution)/shard_map/ppermute | solution.py:36
  474.1 7.1 %reduce-scatter.9.cloned.1.call-done = bf16[1,64,2560]{2,1,0:T(8,128)(2,1)} async-done(((bf16[4,64,2560]{2,1,0:T(8,128)(2,1)}), bf16[1,64,2560]{2,1,0:T(8,128)(2,1)}) %reduce-scatter.9.cloned.1.call-update) | async-done | bytes 327696 | tf_op jit(solution)/shard_map/reduce_scatter | solution.py:75
  482.3 3.8 collective-permute-done.50
  486.1 4.9 collective-permute-done.51
  495.0 9.8 %collective-permute-done.54 = bf16[64,3584]{1,0:T(8,128)(2,1)S(1)} collective-permute-done((bf16[64,3584]{1,0:T(8,128)(2,1)S(1)}, bf16[64,3584]{1,0:T(8,128)(2,1)S(1)}, u32[]{:S(2)}, u32[]{:S(2)}) %collective-permute-start.54) | collective-permute-done | bytes 458784 | tf_op jit(solution)/shard_map/ppermute | solution.py:28
  504.8 13.4 %all-gather.14.cloned.1.call-done = bf16[256,2560]{1,0:T(8,128)(2,1)} async-done(((bf16[64,2560]{1,0:T(8,128)(2,1)}), bf16[256,2560]{1,0:T(8,128)(2,1)}) %all-gather.14.cloned.1.call-update) | async-done | bytes 1310736 | tf_op jit(solution)/shard_map/all_gather | solution.py:58
  523.1 2.7 collective-permute-start.57
  525.8 8.1 %collective-permute-done.58.refs_5_ = bf16[128,1792]{1,0:T(8,128)(2,1)S(1)} collective-permute-done((bf16[128,1792]{1,0:T(8,128)(2,1)S(1)}, bf16[128,1792]{1,0:T(8,128)(2,1)S(1)}, u32[]{:S(2)}, u32[]{:S(2)}) %collective-permute-start.58) | collective-permute-done | bytes 458784 | tf_op jit(solution)/shard_map/ppermute | solution.py:36
  533.9 3.0 collective-permute-start.60
  538.6 8.2 %collective-permute-done.56.refs_3_ = bf16[128,1792]{1,0:T(8,128)(2,1)S(1)} collective-permute-done((bf16[128,1792]{1,0:T(8,128)(2,1)S(1)}, bf16[128,1792]{1,0:T(8,128)(2,1)S(1)}, u32[]{:S(2)}, u32[]{:S(2)}) %collective-permute-start.56) | collective-permute-done | bytes 458784 | tf_op jit(solution)/shard_map/ppermute | solution.py:32
  548.3 2.6 collective-permute-done.60.refs_7_
  551.7 2.9 collective-permute-done.59.refs_6_
  559.7 23.9 %expert_mlp.7 = (bf16[128,1792]{1,0:T(8,128)(2,1)S(1)}, bf16[128,1792]{1,0:T(8,128)(2,1)S(1)}, bf16[128,1792]{1,0:T(8,128)(2,1)S(1)}, bf16[128,1792]{1,0:T(8,128...) custom-call(s32[1]{0:T(128)} %bitcast.1.me_ref, ...), custom_call_target="tpu_custom_call" | custom-call | flops 12079595520 | bytes 36175872 | tf_op jit(solution)/shard_map/expert_mlp/pallas_call | solution.py:152
  585.0 3.2 collective-permute-start.62
  590.3 9.4 %collective-permute-done.63 = bf16[128,1792]{1,0:T(8,128)(2,1)S(1)} collective-permute-done((bf16[128,1792]{1,0:T(8,128)(2,1)S(1)}, bf16[128,1792]{1,0:T(8,128)(2,1)S(1)}, u32[]{:S(2)}, u32[]{:S(2)}) %collective-permute-start.63) | collective-permute-done | bytes 458784 | tf_op jit(solution)/shard_map/ppermute | solution.py:32
  600.6 13.2 %collective-permute-done.70 = bf16[4,64,2560]{2,1,0:T(8,128)(2,1)S(1)} collective-permute-done((bf16[4,64,2560]{2,1,0:T(8,128)(2,1)S(1)}, bf16[4,64,2560]{2,1,0:T(8,128)(2,1)S(1)}, u32[]{:S(2)}, u32[]{:S(2)}) %collective-permute-start.70) | collective-permute-done | bytes 1310752 | tf_op jit(solution)/shard_map/ppermute | solution.py:28
  618.7 10.6 %collective-permute-done.67 = bf16[128,1792]{1,0:T(8,128)(2,1)S(1)} collective-permute-done((bf16[128,1792]{1,0:T(8,128)(2,1)S(1)}, bf16[128,1792]{1,0:T(8,128)(2,1)S(1)}, u32[]{:S(2)}, u32[]{:S(2)}) %collective-permute-start.67) | collective-permute-done | bytes 458784 | tf_op jit(solution)/shard_map/ppermute | solution.py:36
  631.5 7.4 %reduce-scatter.11.cloned.1.call-done = bf16[1,64,2560]{2,1,0:T(8,128)(2,1)} async-done(((bf16[4,64,2560]{2,1,0:T(8,128)(2,1)}), bf16[1,64,2560]{2,1,0:T(8,128)(2,1)}) %reduce-scatter.11.cloned.1.call-update) | async-done | bytes 327696 | tf_op jit(solution)/shard_map/reduce_scatter | solution.py:75
  640.0 3.5 collective-permute-done.68
  643.5 5.1 collective-permute-done.69
  (310 shorter events, 122.9 us)
Async XLA Ops:
  6.5 32.5 %all-gather.8.cloned.1.call-start = ((), (), s32[]{:S(2)}) async-start(), calls=%async_computation.5 | async-start | bytes 1638400 | tf_op jit(solution)/shard_map/all_gather | solution.py:58
  39.1 39.2 %collective-permute-start.7 = (bf16[4,64,2560]{2,1,0:T(8,128)(2,1)}, bf16[4,64,2560]{2,1,0:T(8,128)(2,1)}, u32[]{:S(2)}, u32[]{:S(2)}) collective-permute-start(bf16[4,64,2560]{2,1,0:T(8,128)(2,1)} %all-gather.8.cloned.1.call-done.refs_8_), channel_id=1, source_target_pairs={{0,1},{1,0},{2,3},{3,2},{4,5},{5,4},{6,7},{7,6},{8,9},{9,8},{10,11... | collective-permute-start | bytes 3932168 | tf_op jit(solution)/shard_map/ppermute | solution.py:28
  43.0 14.7 %collective-permute-start.1 = (bf16[128,1792]{1,0:T(8,128)(2,1)S(1)}, bf16[128,1792]{1,0:T(8,128)(2,1)S(1)}, u32[]{:S(2)}, u32[]{:S(2)}) collective-permute-start(bf16[128,1792]{1,0:T(8,128)(2,1)S(1)} %pad_maximum_fusion.4.refs_0_), channel_id=1, source_target_pairs={{0,2},{1,3},{2,4},{3,5},{4,6},{5,7},{6,0},{7,1},{8,10},{9,11},{10,... | collective-permute-start | bytes 1376264 | tf_op jit(solution)/shard_map/ppermute | solution.py:32
  43.4 32.5 %collective-permute-start.2 = (bf16[128,1792]{1,0:T(8,128)(2,1)S(1)}, bf16[128,1792]{1,0:T(8,128)(2,1)S(1)}, u32[]{:S(2)}, u32[]{:S(2)}) collective-permute-start(bf16[128,1792]{1,0:T(8,128)(2,1)S(1)} %pad_maximum_fusion.5.refs_1_), channel_id=1, source_target_pairs={{0,2},{1,3},{2,4},{3,5},{4,6},{5,7},{6,0},{7,1},{8,10},{9,11},{10,... | collective-permute-start | bytes 1376264 | tf_op jit(solution)/shard_map/ppermute | solution.py:32
  43.9 32.7 %collective-permute-start.3 = (bf16[128,1792]{1,0:T(8,128)(2,1)S(1)}, bf16[128,1792]{1,0:T(8,128)(2,1)S(1)}, u32[]{:S(2)}, u32[]{:S(2)}) collective-permute-start(bf16[128,1792]{1,0:T(8,128)(2,1)S(1)} %pad_maximum_fusion.4.refs_0_), channel_id=1, source_target_pairs={{0,6},{1,7},{2,0},{3,1},{4,2},{5,3},{6,4},{7,5},{8,14},{9,15},{10,... | collective-permute-start | bytes 1376264 | tf_op jit(solution)/shard_map/ppermute | solution.py:36
  54.7 22.7 %collective-permute-start.6 = (bf16[128,1792]{1,0:T(8,128)(2,1)S(1)}, bf16[128,1792]{1,0:T(8,128)(2,1)S(1)}, u32[]{:S(2)}, u32[]{:S(2)}) collective-permute-start(bf16[128,1792]{1,0:T(8,128)(2,1)S(1)} %collective-permute-done.4.refs_5_), channel_id=1, source_target_pairs={{0,6},{1,7},{2,0},{3,1},{4,2},{5,3},{6,4},{7,5},{8,14},{9,15},{10,... | collective-permute-start | bytes 1376264 | tf_op jit(solution)/shard_map/ppermute | solution.py:36
  57.8 20.4 %collective-permute-start.5 = (bf16[128,1792]{1,0:T(8,128)(2,1)S(1)}, bf16[128,1792]{1,0:T(8,128)(2,1)}, u32[]{:S(2)}, u32[]{:S(2)}) collective-permute-start(bf16[128,1792]{1,0:T(8,128)(2,1)S(1)} %collective-permute-done.1.refs_2_), channel_id=1, source_target_pairs={{0,2},{1,3},{2,4},{3,5},{4,6},{5,7},{6,0},{7,1},{8,10},{9,11},{10,... | collective-permute-start | bytes 1376264 | tf_op jit(solution)/shard_map/ppermute | solution.py:32
  58.5 17.0 %all-to-all-start = ((f32[8,1,256]{2,1,0:T(1,128)}), f32[8,1,256]{2,1,0:T(1,128)S(1)}, u32[]{:S(2)}, u32[]{:S(2)}) async-start(f32[8,1,256]{2,1,0:T(1,128)} %all_to_all.8), calls=%async_computation | async-start | bytes 16384 | tf_op jit(solution)/shard_map/all_to_all | solution.py:194
  63.9 95.8 %reduce-scatter.5.cloned.1.call-start = ((), (), s32[]{:S(2)}) async-start(), calls=%async_computation.6 | async-start | bytes 1638400 | tf_op jit(solution)/shard_map/reduce_scatter | solution.py:75
  105.5 30.2 %collective-permute-start.16 = (bf16[4,64,2560]{2,1,0:T(8,128)(2,1)S(1)}, bf16[4,64,2560]{2,1,0:T(8,128)(2,1)S(1)}, u32[]{:S(2)}, u32[]{:S(2)}) collective-permute-start(bf16[4,64,2560]{2,1,0:T(8,128)(2,1)S(1)} %get-tuple-element.54), channel_id=1, source_target_pairs={{0,1},{1,0},{2,3},{3,2},{4,5},{5,4},{6,7},{7,6},{8,9},{9,8},{10,11... | collective-permute-start | bytes 3932168 | tf_op jit(solution)/shard_map/ppermute | solution.py:28
  107.0 14.7 %collective-permute-start.9 = (bf16[128,1792]{1,0:T(8,128)(2,1)S(1)}, bf16[128,1792]{1,0:T(8,128)(2,1)S(1)}, u32[]{:S(2)}, u32[]{:S(2)}) collective-permute-start(bf16[128,1792]{1,0:T(8,128)(2,1)S(1)} %get-tuple-element.48), channel_id=1, source_target_pairs={{0,2},{1,3},{2,4},{3,5},{4,6},{5,7},{6,0},{7,1},{8,10},{9,11},{10,... | collective-permute-start | bytes 1376264 | tf_op jit(solution)/shard_map/ppermute | solution.py:32
  107.0 30.7 %collective-permute-start.8 = (bf16[128,1792]{1,0:T(8,128)(2,1)}, bf16[128,1792]{1,0:T(8,128)(2,1)S(1)}, u32[]{:S(2)}, u32[]{:S(2)}) collective-permute-start(bf16[128,1792]{1,0:T(8,128)(2,1)} %get-tuple-element.46), channel_id=1, source_target_pairs={{0,6},{1,7},{2,0},{3,1},{4,2},{5,3},{6,4},{7,5},{8,14},{9,15},{10,... | collective-permute-start | bytes 1376264 | tf_op jit(solution)/shard_map/ppermute | solution.py:36
  110.2 26.9 %collective-permute-start.12 = (bf16[128,1792]{1,0:T(8,128)(2,1)}, bf16[128,1792]{1,0:T(8,128)(2,1)S(1)}, u32[]{:S(2)}, u32[]{:S(2)}) collective-permute-start(bf16[128,1792]{1,0:T(8,128)(2,1)} %get-tuple-element.52), channel_id=1, source_target_pairs={{0,6},{1,7},{2,0},{3,1},{4,2},{5,3},{6,4},{7,5},{8,14},{9,15},{10,... | collective-permute-start | bytes 1376264 | tf_op jit(solution)/shard_map/ppermute | solution.py:36
  110.2 27.9 %collective-permute-start.11 = (bf16[128,1792]{1,0:T(8,128)(2,1)}, bf16[128,1792]{1,0:T(8,128)(2,1)S(1)}, u32[]{:S(2)}, u32[]{:S(2)}) collective-permute-start(bf16[128,1792]{1,0:T(8,128)(2,1)} %get-tuple-element.50), channel_id=1, source_target_pairs={{0,2},{1,3},{2,4},{3,5},{4,6},{5,7},{6,0},{7,1},{8,10},{9,11},{10,... | collective-permute-start | bytes 1376264 | tf_op jit(solution)/shard_map/ppermute | solution.py:32
  122.5 15.4 %collective-permute-start.10 = (bf16[128,1792]{1,0:T(8,128)(2,1)}, bf16[128,1792]{1,0:T(8,128)(2,1)S(1)}, u32[]{:S(2)}, u32[]{:S(2)}) collective-permute-start(bf16[128,1792]{1,0:T(8,128)(2,1)} %add_convert_fusion.15), channel_id=1, source_target_pairs={{0,2},{1,3},{2,4},{3,5},{4,6},{5,7},{6,0},{7,1},{8,10},{9,11},{10,... | collective-permute-start | bytes 1376264 | tf_op jit(solution)/shard_map/ppermute | solution.py:32
  137.1 57.3 %all-gather.10.cloned.1.call-start = ((), (), s32[]{:S(2)}) async-start(), calls=%async_computation.10 | async-start | bytes 1638400 | tf_op jit(solution)/shard_map/all_gather | solution.py:58
  149.4 18.0 %collective-permute-start.15 = (bf16[64,3584]{1,0:T(8,128)(2,1)S(1)}, bf16[64,3584]{1,0:T(8,128)(2,1)S(1)}, u32[]{:S(2)}, u32[]{:S(2)}) collective-permute-start(bf16[64,3584]{1,0:T(8,128)(2,1)S(1)} %fusion.23), channel_id=1, source_target_pairs={{0,9},{1,8},{2,11},{3,10},{4,13},{5,12},{6,15},{7,14},{8,17},{9,16... | collective-permute-start | bytes 1376264 | tf_op jit(solution)/shard_map/ppermute | solution.py:24
  171.8 144.7 %reduce-scatter.7.cloned.1.call-start = ((), (), s32[]{:S(2)}) async-start(), calls=%async_computation.7 | async-start | bytes 1638400 | tf_op jit(solution)/shard_map/reduce_scatter | solution.py:75
  194.3 36.4 %collective-permute-start.25 = (bf16[4,64,2560]{2,1,0:T(8,128)(2,1)}, bf16[4,64,2560]{2,1,0:T(8,128)(2,1)}, u32[]{:S(2)}, u32[]{:S(2)}) collective-permute-start(bf16[4,64,2560]{2,1,0:T(8,128)(2,1)} %bitcast.45), channel_id=1, source_target_pairs={{0,1},{1,0},{2,3},{3,2},{4,5},{5,4},{6,7},{7,6},{8,9},{9,8},{10,11... | collective-permute-start | bytes 3932168 | tf_op jit(solution)/shard_map/ppermute | solution.py:28
  198.3 15.4 %collective-permute-start.19 = (bf16[128,1792]{1,0:T(8,128)(2,1)S(1)}, bf16[128,1792]{1,0:T(8,128)(2,1)S(1)}, u32[]{:S(2)}, u32[]{:S(2)}) collective-permute-start(bf16[128,1792]{1,0:T(8,128)(2,1)S(1)} %pad_maximum_fusion.6.refs_0_), channel_id=1, source_target_pairs={{0,2},{1,3},{2,4},{3,5},{4,6},{5,7},{6,0},{7,1},{8,10},{9,11},{10,... | collective-permute-start | bytes 1376264 | tf_op jit(solution)/shard_map/ppermute | solution.py:32
  198.6 24.2 %collective-permute-start.20 = (bf16[128,1792]{1,0:T(8,128)(2,1)S(1)}, bf16[128,1792]{1,0:T(8,128)(2,1)S(1)}, u32[]{:S(2)}, u32[]{:S(2)}) collective-permute-start(bf16[128,1792]{1,0:T(8,128)(2,1)S(1)} %pad_maximum_fusion.7.refs_1_), channel_id=1, source_target_pairs={{0,2},{1,3},{2,4},{3,5},{4,6},{5,7},{6,0},{7,1},{8,10},{9,11},{10,... | collective-permute-start | bytes 1376264 | tf_op jit(solution)/shard_map/ppermute | solution.py:32
  199.2 24.5 %collective-permute-start.21 = (bf16[128,1792]{1,0:T(8,128)(2,1)S(1)}, bf16[128,1792]{1,0:T(8,128)(2,1)S(1)}, u32[]{:S(2)}, u32[]{:S(2)}) collective-permute-start(bf16[128,1792]{1,0:T(8,128)(2,1)S(1)} %pad_maximum_fusion.6.refs_0_), channel_id=1, source_target_pairs={{0,6},{1,7},{2,0},{3,1},{4,2},{5,3},{6,4},{7,5},{8,14},{9,15},{10,... | collective-permute-start | bytes 1376264 | tf_op jit(solution)/shard_map/ppermute | solution.py:36
  210.0 17.1 %collective-permute-start.24 = (bf16[128,1792]{1,0:T(8,128)(2,1)S(1)}, bf16[128,1792]{1,0:T(8,128)(2,1)S(1)}, u32[]{:S(2)}, u32[]{:S(2)}) collective-permute-start(bf16[128,1792]{1,0:T(8,128)(2,1)S(1)} %collective-permute-done.22.refs_5_), channel_id=1, source_target_pairs={{0,6},{1,7},{2,0},{3,1},{4,2},{5,3},{6,4},{7,5},{8,14},{9,15},{10,... | collective-permute-start | bytes 1376264 | tf_op jit(solution)/shard_map/ppermute | solution.py:36
  213.7 17.0 %collective-permute-start.23 = (bf16[128,1792]{1,0:T(8,128)(2,1)S(1)}, bf16[128,1792]{1,0:T(8,128)(2,1)}, u32[]{:S(2)}, u32[]{:S(2)}) collective-permute-start(bf16[128,1792]{1,0:T(8,128)(2,1)S(1)} %collective-permute-done.19.refs_2_), channel_id=1, source_target_pairs={{0,2},{1,3},{2,4},{3,5},{4,6},{5,7},{6,0},{7,1},{8,10},{9,11},{10,... | collective-permute-start | bytes 1376264 | tf_op jit(solution)/shard_map/ppermute | solution.py:32
  259.7 30.2 %collective-permute-start.34 = (bf16[4,64,2560]{2,1,0:T(8,128)(2,1)S(1)}, bf16[4,64,2560]{2,1,0:T(8,128)(2,1)S(1)}, u32[]{:S(2)}, u32[]{:S(2)}) collective-permute-start(bf16[4,64,2560]{2,1,0:T(8,128)(2,1)S(1)} %get-tuple-element.64), channel_id=1, source_target_pairs={{0,1},{1,0},{2,3},{3,2},{4,5},{5,4},{6,7},{7,6},{8,9},{9,8},{10,11... | collective-permute-start | bytes 3932168 | tf_op jit(solution)/shard_map/ppermute | solution.py:28
  261.1 14.7 %collective-permute-start.27 = (bf16[128,1792]{1,0:T(8,128)(2,1)S(1)}, bf16[128,1792]{1,0:T(8,128)(2,1)S(1)}, u32[]{:S(2)}, u32[]{:S(2)}) collective-permute-start(bf16[128,1792]{1,0:T(8,128)(2,1)S(1)} %get-tuple-element.58), channel_id=1, source_target_pairs={{0,2},{1,3},{2,4},{3,5},{4,6},{5,7},{6,0},{7,1},{8,10},{9,11},{10,... | collective-permute-start | bytes 1376264 | tf_op jit(solution)/shard_map/ppermute | solution.py:32
  261.1 32.5 %collective-permute-start.26 = (bf16[128,1792]{1,0:T(8,128)(2,1)S(1)}, bf16[128,1792]{1,0:T(8,128)(2,1)S(1)}, u32[]{:S(2)}, u32[]{:S(2)}) collective-permute-start(bf16[128,1792]{1,0:T(8,128)(2,1)S(1)} %get-tuple-element.56), channel_id=1, source_target_pairs={{0,6},{1,7},{2,0},{3,1},{4,2},{5,3},{6,4},{7,5},{8,14},{9,15},{10,... | collective-permute-start | bytes 1376264 | tf_op jit(solution)/shard_map/ppermute | solution.py:36
  264.3 26.9 %collective-permute-start.30 = (bf16[128,1792]{1,0:T(8,128)(2,1)}, bf16[128,1792]{1,0:T(8,128)(2,1)}, u32[]{:S(2)}, u32[]{:S(2)}) collective-permute-start(bf16[128,1792]{1,0:T(8,128)(2,1)} %get-tuple-element.62), channel_id=1, source_target_pairs={{0,6},{1,7},{2,0},{3,1},{4,2},{5,3},{6,4},{7,5},{8,14},{9,15},{10,... | collective-permute-start | bytes 1376264 | tf_op jit(solution)/shard_map/ppermute | solution.py:36
  264.4 30.4 %collective-permute-start.29 = (bf16[128,1792]{1,0:T(8,128)(2,1)S(1)}, bf16[128,1792]{1,0:T(8,128)(2,1)S(1)}, u32[]{:S(2)}, u32[]{:S(2)}) collective-permute-start(bf16[128,1792]{1,0:T(8,128)(2,1)S(1)} %get-tuple-element.60), channel_id=1, source_target_pairs={{0,2},{1,3},{2,4},{3,5},{4,6},{5,7},{6,0},{7,1},{8,10},{9,11},{10,... | collective-permute-start | bytes 1376264 | tf_op jit(solution)/shard_map/ppermute | solution.py:32
  276.6 17.0 %collective-permute-start.28 = (bf16[128,1792]{1,0:T(8,128)(2,1)}, bf16[128,1792]{1,0:T(8,128)(2,1)}, u32[]{:S(2)}, u32[]{:S(2)}) collective-permute-start(bf16[128,1792]{1,0:T(8,128)(2,1)} %add_convert_fusion.12), channel_id=1, source_target_pairs={{0,2},{1,3},{2,4},{3,5},{4,6},{5,7},{6,0},{7,1},{8,10},{9,11},{10,... | collective-permute-start | bytes 1376264 | tf_op jit(solution)/shard_map/ppermute | solution.py:32
  291.2 69.4 %all-gather.12.cloned.1.call-start = ((), (), s32[]{:S(2)}) async-start(), calls=%async_computation.11 | async-start | bytes 1638400 | tf_op jit(solution)/shard_map/all_gather | solution.py:58
  305.8 23.1 %collective-permute-start.32 = (bf16[64,3584]{1,0:T(8,128)(2,1)S(1)}, bf16[64,3584]{1,0:T(8,128)(2,1)S(1)}, u32[]{:S(2)}, u32[]{:S(2)}) collective-permute-start(bf16[64,3584]{1,0:T(8,128)(2,1)S(1)} %fusion.3), channel_id=1, source_target_pairs={{0,8},{8,16},{16,24},{24,32},{32,40},{40,48},{48,56},{56,64},{64,7... | collective-permute-start | bytes 1376264 | tf_op jit(solution)/shard_map/ppermute | solution.py:19
  314.8 15.5 %collective-permute-start.33 = (bf16[64,3584]{1,0:T(8,128)(2,1)S(1)}, bf16[64,3584]{1,0:T(8,128)(2,1)S(1)}, u32[]{:S(2)}, u32[]{:S(2)}) collective-permute-start(bf16[64,3584]{1,0:T(8,128)(2,1)S(1)} %fusion.22), channel_id=1, source_target_pairs={{0,9},{1,8},{2,11},{3,10},{4,13},{5,12},{6,15},{7,14},{8,17},{9,16... | collective-permute-start | bytes 1376264 | tf_op jit(solution)/shard_map/ppermute | solution.py:24
  317.5 16.2 %collective-permute-start.35 = (bf16[64,2560]{1,0:T(8,128)(2,1)S(1)}, bf16[64,2560]{1,0:T(8,128)(2,1)S(1)}, u32[]{:S(2)}, u32[]{:S(2)}) collective-permute-start(bf16[64,2560]{1,0:T(8,128)(2,1)S(1)} %fusion.31), channel_id=1, source_target_pairs={{0,8},{8,16},{16,24},{24,32},{32,40},{40,48},{48,56},{56,64},{64,7... | collective-permute-start | bytes 983048 | tf_op jit(solution)/shard_map/ppermute | solution.py:19
  335.4 145.8 %reduce-scatter.9.cloned.1.call-start = ((), (), s32[]{:S(2)}) async-start(), calls=%async_computation.8 | async-start | bytes 1638400 | tf_op jit(solution)/shard_map/reduce_scatter | solution.py:75
  360.6 36.4 %collective-permute-start.43 = (bf16[4,64,2560]{2,1,0:T(8,128)(2,1)}, bf16[4,64,2560]{2,1,0:T(8,128)(2,1)}, u32[]{:S(2)}, u32[]{:S(2)}) collective-permute-start(bf16[4,64,2560]{2,1,0:T(8,128)(2,1)} %bitcast.47), channel_id=1, source_target_pairs={{0,1},{1,0},{2,3},{3,2},{4,5},{5,4},{6,7},{7,6},{8,9},{9,8},{10,11... | collective-permute-start | bytes 3932168 | tf_op jit(solution)/shard_map/ppermute | solution.py:28
  364.6 15.4 %collective-permute-start.37 = (bf16[128,1792]{1,0:T(8,128)(2,1)S(1)}, bf16[128,1792]{1,0:T(8,128)(2,1)S(1)}, u32[]{:S(2)}, u32[]{:S(2)}) collective-permute-start(bf16[128,1792]{1,0:T(8,128)(2,1)S(1)} %pad_maximum_fusion.8.refs_0_), channel_id=1, source_target_pairs={{0,2},{1,3},{2,4},{3,5},{4,6},{5,7},{6,0},{7,1},{8,10},{9,11},{10,... | collective-permute-start | bytes 1376264 | tf_op jit(solution)/shard_map/ppermute | solution.py:32
  364.9 24.2 %collective-permute-start.38 = (bf16[128,1792]{1,0:T(8,128)(2,1)S(1)}, bf16[128,1792]{1,0:T(8,128)(2,1)S(1)}, u32[]{:S(2)}, u32[]{:S(2)}) collective-permute-start(bf16[128,1792]{1,0:T(8,128)(2,1)S(1)} %pad_maximum_fusion.9.refs_1_), channel_id=1, source_target_pairs={{0,2},{1,3},{2,4},{3,5},{4,6},{5,7},{6,0},{7,1},{8,10},{9,11},{10,... | collective-permute-start | bytes 1376264 | tf_op jit(solution)/shard_map/ppermute | solution.py:32
  365.4 24.5 %collective-permute-start.39 = (bf16[128,1792]{1,0:T(8,128)(2,1)S(1)}, bf16[128,1792]{1,0:T(8,128)(2,1)S(1)}, u32[]{:S(2)}, u32[]{:S(2)}) collective-permute-start(bf16[128,1792]{1,0:T(8,128)(2,1)S(1)} %pad_maximum_fusion.8.refs_0_), channel_id=1, source_target_pairs={{0,6},{1,7},{2,0},{3,1},{4,2},{5,3},{6,4},{7,5},{8,14},{9,15},{10,... | collective-permute-start | bytes 1376264 | tf_op jit(solution)/shard_map/ppermute | solution.py:36
  376.2 17.1 %collective-permute-start.42 = (bf16[128,1792]{1,0:T(8,128)(2,1)S(1)}, bf16[128,1792]{1,0:T(8,128)(2,1)S(1)}, u32[]{:S(2)}, u32[]{:S(2)}) collective-permute-start(bf16[128,1792]{1,0:T(8,128)(2,1)S(1)} %collective-permute-done.40.refs_5_), channel_id=1, source_target_pairs={{0,6},{1,7},{2,0},{3,1},{4,2},{5,3},{6,4},{7,5},{8,14},{9,15},{10,... | collective-permute-start | bytes 1376264 | tf_op jit(solution)/shard_map/ppermute | solution.py:36
  380.0 17.0 %collective-permute-start.41 = (bf16[128,1792]{1,0:T(8,128)(2,1)S(1)}, bf16[128,1792]{1,0:T(8,128)(2,1)}, u32[]{:S(2)}, u32[]{:S(2)}) collective-permute-start(bf16[128,1792]{1,0:T(8,128)(2,1)S(1)} %collective-permute-done.37.refs_2_), channel_id=1, source_target_pairs={{0,2},{1,3},{2,4},{3,5},{4,6},{5,7},{6,0},{7,1},{8,10},{9,11},{10,... | collective-permute-start | bytes 1376264 | tf_op jit(solution)/shard_map/ppermute | solution.py:32
  425.9 30.2 %collective-permute-start.52 = (bf16[4,64,2560]{2,1,0:T(8,128)(2,1)S(1)}, bf16[4,64,2560]{2,1,0:T(8,128)(2,1)S(1)}, u32[]{:S(2)}, u32[]{:S(2)}) collective-permute-start(bf16[4,64,2560]{2,1,0:T(8,128)(2,1)S(1)} %get-tuple-element.74), channel_id=1, source_target_pairs={{0,1},{1,0},{2,3},{3,2},{4,5},{5,4},{6,7},{7,6},{8,9},{9,8},{10,11... | collective-permute-start | bytes 3932168 | tf_op jit(solution)/shard_map/ppermute | solution.py:28
  427.4 14.7 %collective-permute-start.45 = (bf16[128,1792]{1,0:T(8,128)(2,1)S(1)}, bf16[128,1792]{1,0:T(8,128)(2,1)S(1)}, u32[]{:S(2)}, u32[]{:S(2)}) collective-permute-start(bf16[128,1792]{1,0:T(8,128)(2,1)S(1)} %get-tuple-element.68), channel_id=1, source_target_pairs={{0,2},{1,3},{2,4},{3,5},{4,6},{5,7},{6,0},{7,1},{8,10},{9,11},{10,... | collective-permute-start | bytes 1376264 | tf_op jit(solution)/shard_map/ppermute | solution.py:32
  427.4 32.5 %collective-permute-start.44 = (bf16[128,1792]{1,0:T(8,128)(2,1)S(1)}, bf16[128,1792]{1,0:T(8,128)(2,1)S(1)}, u32[]{:S(2)}, u32[]{:S(2)}) collective-permute-start(bf16[128,1792]{1,0:T(8,128)(2,1)S(1)} %get-tuple-element.66), channel_id=1, source_target_pairs={{0,6},{1,7},{2,0},{3,1},{4,2},{5,3},{6,4},{7,5},{8,14},{9,15},{10,... | collective-permute-start | bytes 1376264 | tf_op jit(solution)/shard_map/ppermute | solution.py:36
  430.6 26.9 %collective-permute-start.48 = (bf16[128,1792]{1,0:T(8,128)(2,1)}, bf16[128,1792]{1,0:T(8,128)(2,1)}, u32[]{:S(2)}, u32[]{:S(2)}) collective-permute-start(bf16[128,1792]{1,0:T(8,128)(2,1)} %get-tuple-element.72), channel_id=1, source_target_pairs={{0,6},{1,7},{2,0},{3,1},{4,2},{5,3},{6,4},{7,5},{8,14},{9,15},{10,... | collective-permute-start | bytes 1376264 | tf_op jit(solution)/shard_map/ppermute | solution.py:36
  430.6 30.4 %collective-permute-start.47 = (bf16[128,1792]{1,0:T(8,128)(2,1)S(1)}, bf16[128,1792]{1,0:T(8,128)(2,1)S(1)}, u32[]{:S(2)}, u32[]{:S(2)}) collective-permute-start(bf16[128,1792]{1,0:T(8,128)(2,1)S(1)} %get-tuple-element.70), channel_id=1, source_target_pairs={{0,2},{1,3},{2,4},{3,5},{4,6},{5,7},{6,0},{7,1},{8,10},{9,11},{10,... | collective-permute-start | bytes 1376264 | tf_op jit(solution)/shard_map/ppermute | solution.py:32
  442.9 17.0 %collective-permute-start.46 = (bf16[128,1792]{1,0:T(8,128)(2,1)}, bf16[128,1792]{1,0:T(8,128)(2,1)}, u32[]{:S(2)}, u32[]{:S(2)}) collective-permute-start(bf16[128,1792]{1,0:T(8,128)(2,1)} %add_convert_fusion.9), channel_id=1, source_target_pairs={{0,2},{1,3},{2,4},{3,5},{4,6},{5,7},{6,0},{7,1},{8,10},{9,11},{10,... | collective-permute-start | bytes 1376264 | tf_op jit(solution)/shard_map/ppermute | solution.py:32
  457.5 60.8 %all-gather.14.cloned.1.call-start = ((), (), s32[]{:S(2)}) async-start(), calls=%async_computation.12 | async-start | bytes 1638400 | tf_op jit(solution)/shard_map/all_gather | solution.py:58
  472.1 14.1 %collective-permute-start.50 = (bf16[64,3584]{1,0:T(8,128)(2,1)S(1)}, bf16[64,3584]{1,0:T(8,128)(2,1)S(1)}, u32[]{:S(2)}, u32[]{:S(2)}) collective-permute-start(bf16[64,3584]{1,0:T(8,128)(2,1)S(1)} %fusion.7), channel_id=1, source_target_pairs={{0,8},{8,16},{16,24},{24,32},{32,40},{40,48},{48,56},{56,64},{64,7... | collective-permute-start | bytes 1376264 | tf_op jit(solution)/shard_map/ppermute | solution.py:19
  472.4 18.6 %collective-permute-start.51 = (bf16[64,3584]{1,0:T(8,128)(2,1)S(1)}, bf16[64,3584]{1,0:T(8,128)(2,1)S(1)}, u32[]{:S(2)}, u32[]{:S(2)}) collective-permute-start(bf16[64,3584]{1,0:T(8,128)(2,1)S(1)} %fusion.21), channel_id=1, source_target_pairs={{0,9},{1,8},{2,11},{3,10},{4,13},{5,12},{6,15},{7,14},{8,17},{9,16... | collective-permute-start | bytes 1376264 | tf_op jit(solution)/shard_map/ppermute | solution.py:24
  494.5 144.4 %reduce-scatter.11.cloned.1.call-start = ((), (), s32[]{:S(2)}) async-start(), calls=%async_computation.9 | async-start | bytes 1638400 | tf_op jit(solution)/shard_map/reduce_scatter | solution.py:75
  518.2 36.4 %collective-permute-start.61 = (bf16[4,64,2560]{2,1,0:T(8,128)(2,1)}, bf16[4,64,2560]{2,1,0:T(8,128)(2,1)}, u32[]{:S(2)}, u32[]{:S(2)}) collective-permute-start(bf16[4,64,2560]{2,1,0:T(8,128)(2,1)} %bitcast.43), channel_id=1, source_target_pairs={{0,1},{1,0},{2,3},{3,2},{4,5},{5,4},{6,7},{7,6},{8,9},{9,8},{10,11... | collective-permute-start | bytes 3932168 | tf_op jit(solution)/shard_map/ppermute | solution.py:28
  522.2 15.4 %collective-permute-start.55 = (bf16[128,1792]{1,0:T(8,128)(2,1)S(1)}, bf16[128,1792]{1,0:T(8,128)(2,1)S(1)}, u32[]{:S(2)}, u32[]{:S(2)}) collective-permute-start(bf16[128,1792]{1,0:T(8,128)(2,1)S(1)} %pad_maximum_fusion.10.refs_0_), channel_id=1, source_target_pairs={{0,2},{1,3},{2,4},{3,5},{4,6},{5,7},{6,0},{7,1},{8,10},{9,11},{10,... | collective-permute-start | bytes 1376264 | tf_op jit(solution)/shard_map/ppermute | solution.py:32
  522.6 24.2 %collective-permute-start.56 = (bf16[128,1792]{1,0:T(8,128)(2,1)S(1)}, bf16[128,1792]{1,0:T(8,128)(2,1)S(1)}, u32[]{:S(2)}, u32[]{:S(2)}) collective-permute-start(bf16[128,1792]{1,0:T(8,128)(2,1)S(1)} %pad_maximum_fusion.11.refs_1_), channel_id=1, source_target_pairs={{0,2},{1,3},{2,4},{3,5},{4,6},{5,7},{6,0},{7,1},{8,10},{9,11},{10,... | collective-permute-start | bytes 1376264 | tf_op jit(solution)/shard_map/ppermute | solution.py:32
  523.1 24.5 %collective-permute-start.57 = (bf16[128,1792]{1,0:T(8,128)(2,1)S(1)}, bf16[128,1792]{1,0:T(8,128)(2,1)S(1)}, u32[]{:S(2)}, u32[]{:S(2)}) collective-permute-start(bf16[128,1792]{1,0:T(8,128)(2,1)S(1)} %pad_maximum_fusion.10.refs_0_), channel_id=1, source_target_pairs={{0,6},{1,7},{2,0},{3,1},{4,2},{5,3},{6,4},{7,5},{8,14},{9,15},{10,... | collective-permute-start | bytes 1376264 | tf_op jit(solution)/shard_map/ppermute | solution.py:36
  533.9 17.1 %collective-permute-start.60 = (bf16[128,1792]{1,0:T(8,128)(2,1)S(1)}, bf16[128,1792]{1,0:T(8,128)(2,1)S(1)}, u32[]{:S(2)}, u32[]{:S(2)}) collective-permute-start(bf16[128,1792]{1,0:T(8,128)(2,1)S(1)} %collective-permute-done.58.refs_5_), channel_id=1, source_target_pairs={{0,6},{1,7},{2,0},{3,1},{4,2},{5,3},{6,4},{7,5},{8,14},{9,15},{10,... | collective-permute-start | bytes 1376264 | tf_op jit(solution)/shard_map/ppermute | solution.py:36
  537.6 17.0 %collective-permute-start.59 = (bf16[128,1792]{1,0:T(8,128)(2,1)S(1)}, bf16[128,1792]{1,0:T(8,128)(2,1)}, u32[]{:S(2)}, u32[]{:S(2)}) collective-permute-start(bf16[128,1792]{1,0:T(8,128)(2,1)S(1)} %collective-permute-done.55.refs_2_), channel_id=1, source_target_pairs={{0,2},{1,3},{2,4},{3,5},{4,6},{5,7},{6,0},{7,1},{8,10},{9,11},{10,... | collective-permute-start | bytes 1376264 | tf_op jit(solution)/shard_map/ppermute | solution.py:32
  583.6 30.2 %collective-permute-start.70 = (bf16[4,64,2560]{2,1,0:T(8,128)(2,1)S(1)}, bf16[4,64,2560]{2,1,0:T(8,128)(2,1)S(1)}, u32[]{:S(2)}, u32[]{:S(2)}) collective-permute-start(bf16[4,64,2560]{2,1,0:T(8,128)(2,1)S(1)} %get-tuple-element.84), channel_id=1, source_target_pairs={{0,1},{1,0},{2,3},{3,2},{4,5},{5,4},{6,7},{7,6},{8,9},{9,8},{10,11... | collective-permute-start | bytes 3932168 | tf_op jit(solution)/shard_map/ppermute | solution.py:28
  585.0 14.7 %collective-permute-start.63 = (bf16[128,1792]{1,0:T(8,128)(2,1)S(1)}, bf16[128,1792]{1,0:T(8,128)(2,1)S(1)}, u32[]{:S(2)}, u32[]{:S(2)}) collective-permute-start(bf16[128,1792]{1,0:T(8,128)(2,1)S(1)} %get-tuple-element.78), channel_id=1, source_target_pairs={{0,2},{1,3},{2,4},{3,5},{4,6},{5,7},{6,0},{7,1},{8,10},{9,11},{10,... | collective-permute-start | bytes 1376264 | tf_op jit(solution)/shard_map/ppermute | solution.py:32
  585.0 32.4 %collective-permute-start.62 = (bf16[128,1792]{1,0:T(8,128)(2,1)S(1)}, bf16[128,1792]{1,0:T(8,128)(2,1)S(1)}, u32[]{:S(2)}, u32[]{:S(2)}) collective-permute-start(bf16[128,1792]{1,0:T(8,128)(2,1)S(1)} %get-tuple-element.76), channel_id=1, source_target_pairs={{0,6},{1,7},{2,0},{3,1},{4,2},{5,3},{6,4},{7,5},{8,14},{9,15},{10,... | collective-permute-start | bytes 1376264 | tf_op jit(solution)/shard_map/ppermute | solution.py:36
  588.3 26.9 %collective-permute-start.66 = (bf16[128,1792]{1,0:T(8,128)(2,1)}, bf16[128,1792]{1,0:T(8,128)(2,1)}, u32[]{:S(2)}, u32[]{:S(2)}) collective-permute-start(bf16[128,1792]{1,0:T(8,128)(2,1)} %get-tuple-element.82), channel_id=1, source_target_pairs={{0,6},{1,7},{2,0},{3,1},{4,2},{5,3},{6,4},{7,5},{8,14},{9,15},{10,... | collective-permute-start | bytes 1376264 | tf_op jit(solution)/shard_map/ppermute | solution.py:36
  588.3 30.4 %collective-permute-start.65 = (bf16[128,1792]{1,0:T(8,128)(2,1)S(1)}, bf16[128,1792]{1,0:T(8,128)(2,1)S(1)}, u32[]{:S(2)}, u32[]{:S(2)}) collective-permute-start(bf16[128,1792]{1,0:T(8,128)(2,1)S(1)} %get-tuple-element.80), channel_id=1, source_target_pairs={{0,2},{1,3},{2,4},{3,5},{4,6},{5,7},{6,0},{7,1},{8,10},{9,11},{10,... | collective-permute-start | bytes 1376264 | tf_op jit(solution)/shard_map/ppermute | solution.py:32
  600.6 16.9 %collective-permute-start.64 = (bf16[128,1792]{1,0:T(8,128)(2,1)}, bf16[128,1792]{1,0:T(8,128)(2,1)}, u32[]{:S(2)}, u32[]{:S(2)}) collective-permute-start(bf16[128,1792]{1,0:T(8,128)(2,1)} %add_convert_fusion.6), channel_id=1, source_target_pairs={{0,2},{1,3},{2,4},{3,5},{4,6},{5,7},{6,0},{7,1},{8,10},{9,11},{10,... | collective-permute-start | bytes 1376264 | tf_op jit(solution)/shard_map/ppermute | solution.py:32
  629.8 18.8 %collective-permute-start.69 = (bf16[64,3584]{1,0:T(8,128)(2,1)S(1)}, bf16[64,3584]{1,0:T(8,128)(2,1)S(1)}, u32[]{:S(2)}, u32[]{:S(2)}) collective-permute-start(bf16[64,3584]{1,0:T(8,128)(2,1)S(1)} %fusion.20), channel_id=1, source_target_pairs={{0,9},{1,8},{2,11},{3,10},{4,13},{5,12},{6,15},{7,14},{8,17},{9,16... | collective-permute-start | bytes 1376264 | tf_op jit(solution)/shard_map/ppermute | solution.py:24
  (76 other events, 483.4 us)
Sparse Core Ops, SparseCore 0:
  11.7 27.2 all-gather.7
  137.2 22.4 reduce-scatter.4
  171.9 22.3 all-gather.9
  291.3 23.5 reduce-scatter.6
  335.5 25.0 all-gather.11
  457.6 23.5 reduce-scatter.8
  494.6 23.6 all-gather.13
  615.3 23.5 reduce-scatter.10

commit v2 on v0

v2 whole, which is shorter than its diff:
```python
import functools

import jax
import jax.numpy as jnp
from jax import lax
from jax.experimental import pallas as pl
from jax.experimental.pallas import tpu as pltpu
from jax.sharding import PartitionSpec as P

TICKS = 4
FIRST = 4096
DEEP = 1024
WIDE = 2048
SLOTS = 4
RINGS = [[0, 2, 4, 6], [1, 3, 5, 7]]
LIMIT = 38


def relayed(value, turn):
    pairs = []
    for s in range(16):
        for e in range(8):
            target = e ^ 1 if turn is None else (e + turn) % 8
            pairs.append((s * 8 + e, (s + 1) % 16 * 8 + target))
    return lax.ppermute(value, ("section", "expert"), pairs)


def across(value):
    return lax.ppermute(value, "expert", [(i, i ^ 1) for i in range(8)])


def upward(value):
    return lax.ppermute(value, "expert", [(i, (i + 2) % 8) for i in range(8)])


def downward(value):
    return lax.ppermute(value, "expert", [(i, (i - 2) % 8) for i in range(8)])


def plus(*terms):
    total = terms[0].astype(jnp.float32)
    for term in terms[1:]:
        total = total + term.astype(jnp.float32)
    return total


def normalize(first, second, gain):
    split = first.shape[1]
    one, two = first.astype(jnp.float32), second.astype(jnp.float32)
    total = jnp.sum(one * one, axis=-1, keepdims=True) + jnp.sum(two * two, axis=-1, keepdims=True)
    scale = lax.rsqrt(total / gain.shape[0] + 1e-05)
    one = (one * scale * gain[None, :split]).astype(jnp.bfloat16)
    two = (two * scale * gain[None, split:]).astype(jnp.bfloat16)
    return one, two


def thirds(weights):
    high = lax.reduce_precision(weights, 8, 7)
    rest = weights - high
    middle = lax.reduce_precision(rest, 8, 7)
    parts = jnp.concatenate([high, middle, rest - middle], axis=1)
    return jnp.pad(parts, ((0, 0), (0, 128 - parts.shape[1]))).astype(jnp.bfloat16)


def whole_again(parts):
    size = TICKS * 8
    high, middle, low = (parts[:, i * size : (i + 1) * size].astype(jnp.float32) for i in range(3))
    return high + (middle + low)


def gather(first, second):
    half, quarter = first.shape[1] // 2, second.shape[1] // 256 * 128
    other = across(first)
    below, above = upward(second), downward(second)
    own_l = jnp.concatenate([first[:, :half], other[:, :half]], axis=0)
    own_r = jnp.concatenate([first[:, half:], other[:, half:]], axis=0)
    below_l, above_r = upward(own_l), downward(own_r)
    below_r, above_l = upward(own_r), downward(own_l)
    facing = jnp.concatenate([upward(below[:, :quarter]), downward(above[:, quarter:])], axis=1)
    near = jnp.concatenate([second, below, above, facing], axis=0)
    far = across(after(near, other))
    opp_l, opp_r = upward(below_l), downward(above_r)
    return (own_l, own_r, below_l, below_r, above_l, above_r, opp_l, opp_r), near, far


def after(value, *others):
    return lax.optimization_barrier((value, *others))[0]


def scatter_first(first, pieces):
    own_l, own_r, below_l, below_r, above_l, above_r, opp_l, opp_r = pieces
    rows = first.shape[0]
    arrived_l, arrived_r = upward(opp_l), downward(opp_r)
    sum_r, sum_l = upward(above_r), downward(below_l)
    top_l = upward(plus(above_l, arrived_l).astype(jnp.bfloat16))
    low_r = downward(plus(below_r, arrived_r).astype(jnp.bfloat16))
    sums = jnp.concatenate([plus(own_l, sum_l, top_l), plus(own_r, sum_r, low_r)], axis=1)
    sent = relayed(sums[rows:].astype(jnp.bfloat16), None)
    kept = relayed((first.astype(jnp.float32) + sums[:rows]).astype(jnp.bfloat16), 0)
    return plus(kept, sent).astype(jnp.bfloat16)


def scatter_second(second, near, far):
    both = plus(near, across(far)).astype(jnp.bfloat16)
    total = lax.psum_scatter(both, "expert", scatter_dimension=0, axis_index_groups=RINGS)
    return relayed(plus(second, total).astype(jnp.bfloat16), 0)


def accumulate(acc, rows, gate_ref, up_ref, first):
    inner = gate_ref.shape[1]
    for at, ref in ((0, gate_ref), (inner, up_ref)):
        columns = slice(at, at + inner)
        part = jnp.dot(rows, ref[...], preferred_element_type=jnp.float32)
        acc[:, columns] = part if first else acc[:, columns] + part


def mlp_kernel(turns, weight, gate_hbm, up_hbm, down_hbm, *refs):
    pieces, (near, far) = refs[:8], refs[8:10]
    outs, (out_near, out_far) = refs[10:18], refs[18:20]
    gates, ups, downs, acc, hidden, in_sems, out_sems = refs[20:]
    pair, half = pieces[0].shape
    rows = pair // 2
    inner = hidden.shape[1]
    steps = gate_hbm.shape[0] // DEEP
    wides = down_hbm.shape[1] // WIDE

    def fetch(at):
        slot, span = at % SLOTS, pl.ds(at * DEEP, DEEP)
        return (
            pltpu.make_async_copy(gate_hbm.at[span, :], gates.at[slot], in_sems.at[0, slot]),
            pltpu.make_async_copy(up_hbm.at[span, :], ups.at[slot], in_sems.at[1, slot]),
        )

    def fetch_down(at):
        return pltpu.make_async_copy(down_hbm.at[:, pl.ds(at * WIDE, WIDE)], downs.at[at], out_sems.at[at])

    def start(at):
        for copy in fetch(at):
            copy.start()

    def wait(at):
        for copy in fetch(at):
            copy.wait()

    def block(at):
        start = at * DEEP
        if start < 2 * half:
            side, columns = start // half, pl.ds(start % half, DEEP)
            return jnp.concatenate([pieces[2 * dy + side][:, columns] for dy in range(4)], axis=0)
        columns = pl.ds(start - 2 * half, DEEP)
        parts = [ref[dy * rows : (dy + 1) * rows, columns] for dy in range(4) for ref in (near, far)]
        return jnp.concatenate(parts, axis=0)

    for at in range(SLOTS):
        start(at)
    for at in range(steps):
        wait(at)
        accumulate(acc, block(at), gates.at[at % SLOTS], ups.at[at % SLOTS], at == 0)
        if at + SLOTS < steps:
            start(at + SLOTS)
        elif at + SLOTS == steps:
            for wide in range(wides):
                fetch_down(wide).start()
    scale = weight[...]
    value = acc[:, :inner]
    hidden[...] = (value / (1.0 + jnp.exp(-value)) * acc[:, inner:] * scale).astype(jnp.bfloat16)
    for at in range(wides):
        fetch_down(at).wait()
        for part in range(0, WIDE, 512):
            down = downs[at, :, part : part + 512]
            output = jnp.dot(hidden[...], down, preferred_element_type=jnp.float32).astype(jnp.bfloat16)
            start_at = at * WIDE + part
            if start_at < 2 * half:
                side, columns = start_at // half, pl.ds(start_at % half, 512)
                for dy in range(4):
                    outs[2 * dy + side][:, columns] = output[dy * pair : (dy + 1) * pair, :]
            else:
                columns = pl.ds(start_at - 2 * half, 512)
                for dy in range(4):
                    out_near[turns[dy], :, columns] = output[2 * dy * rows : (2 * dy + 1) * rows, :]
                    out_far[turns[dy], :, columns] = output[(2 * dy + 1) * rows : (2 * dy + 2) * rows, :]


def expert(turns, weight, gate_w, up_w, down_w, pieces, near, far):
    width, inner = gate_w.shape
    total = pieces[0].shape[0] * 4
    wides = width // WIDE
    mixed = (4, total // 8, width - 2 * pieces[0].shape[1])
    whole = pl.BlockSpec(memory_space=pltpu.VMEM)
    outs = pl.pallas_call(
        mlp_kernel,
        in_specs=[pl.BlockSpec(memory_space=pltpu.SMEM), whole] + [pl.BlockSpec(memory_space=pltpu.HBM)] * 3 + [whole] * 10,
        out_specs=[whole] * 10,
        out_shape=[jax.ShapeDtypeStruct(p.shape, jnp.bfloat16) for p in pieces]
        + [jax.ShapeDtypeStruct(mixed, jnp.bfloat16)] * 2,
        scratch_shapes=[
            pltpu.VMEM((SLOTS, DEEP, inner), jnp.bfloat16),
            pltpu.VMEM((SLOTS, DEEP, inner), jnp.bfloat16),
            pltpu.VMEM((wides, inner, WIDE), jnp.bfloat16),
            pltpu.VMEM((total, 2 * inner), jnp.float32),
            pltpu.VMEM((total, inner), jnp.bfloat16),
            pltpu.SemaphoreType.DMA((2, SLOTS)),
            pltpu.SemaphoreType.DMA((wides,)),
        ],
        compiler_params=pltpu.CompilerParams(vmem_limit_bytes=LIMIT * 1024 * 1024),
        cost_estimate=pl.CostEstimate(
            flops=6 * total * width * inner,
            bytes_accessed=6 * width * inner,
            transcendentals=total * inner,
        ),
        name="expert_mlp",
    )(turns, weight, gate_w, up_w, down_w, *pieces, near, far)
    return outs[:8], outs[8], outs[9]


def body(acts, norm_gain, w_gate, w_up, w_down, routes, gates):
    gain = norm_gain[0]
    gate_w, up_w, down_w = w_gate[0, 0], w_up[0, 0], w_down[0, 0]
    rows, width = acts.shape[1:]
    me = lax.axis_index("expert")
    turns = jnp.stack([(me // 2 + dy) % 4 for dy in (0, 3, 1, 2)]).astype(jnp.int32)
    ids = jnp.arange(8, dtype=jnp.int32)
    chosen = (routes[:, 0, :, :, None] == ids).astype(jnp.float32)
    weights = jnp.sum(gates[:, 0, :, :, None] * chosen, axis=2)
    weights = jnp.transpose(weights, (1, 0, 2)).reshape(rows, TICKS * 8)
    riders = thirds(weights)
    columns = jnp.arange(TICKS * 8, dtype=jnp.int32)[None, :]
    first, second = acts[0, :, :FIRST], acts[0, :, FIRST:]
    for tick in range(TICKS):
        one, two = normalize(first, second, gain)
        if tick == 0:
            pieces, near, far = gather(one, jnp.concatenate([two, riders], axis=1))
            parts = jnp.stack([near[:, width - FIRST :], far[:, width - FIRST :]]).reshape(2, 4, rows, 128)
            weights = whole_again(jnp.swapaxes(parts, 0, 1).reshape(8 * rows, 128))
        else:
            pieces, near, far = gather(one, two)
        weight = jnp.sum(jnp.where(columns == tick * 8 + me, weights, 0.0), axis=1, keepdims=True)
        pieces, near, far = expert(turns, weight, gate_w, up_w, down_w, pieces, near, far)
        first, second = scatter_first(first, pieces), scatter_second(second, near, far)
    return jnp.concatenate([first, second], axis=1)[None]


def solution(mesh):
    return jax.shard_map(
        body,
        mesh=mesh,
        in_specs=(
            P("section", "expert", None),
            P("section", None),
            P("section", "expert", None, None),
            P("section", "expert", None, None),
            P("section", "expert", None, None),
            P(None, "section", "expert", None),
            P(None, "section", "expert", None),
        ),
        out_specs=P("section", "expert", None),
        check_vma=False,
    )
```

time: 924 us -> 584 us (0.63)
  blocking collectives: 236 us -> 0 us
  local copies, waits for them, and re-layouts: 150 us -> 12.4 us
  starting transfers between devices: 19 us -> 148 us
  matrix products: 115 us -> 0 us
  other arithmetic: 126 us -> 37.9 us
  Pallas kernels: 0 us -> 78 us
  waiting for transfers between devices: 265 us -> 284 us
  between operations: 1.04 us -> 14.7 us
    all_to_all x4 -> x0, blocking collectives: 236 us -> none  [body(): lax.all_to_all(packed, 'expert', split_axis=0, concat_axis=2, tiled=True)]
    all_to_all x4 -> x0, waiting for transfers between devices: 214 us -> none  [body(): lax.all_to_all(output, 'expert', split_axis=2, concat_axis=0, tiled=True)]
    ppermute x4 -> x88, waiting for transfers between devices: 50.9 us -> 258 us  [the longest x32 150 us: upward(): return lax.ppermute(value, 'expert', [(i, (i + 2) % 8) for i in range(8)])]
    ppermute x4 -> x88, starting transfers between devices: 0.3 us -> 148 us  [the longest x32 89.6 us: downward(): return lax.ppermute(value, 'expert', [(i, (i - 2) % 8) for i in range(8)])]
    unnamed x8 -> x0, other arithmetic: 120 us -> none
    dot_general x28 -> x0, matrix products: 115 us -> none  [the longest x4 75.2 us: body(): jnp.einsum('erf,efd->erd', hidden, w_down[0], preferred_element_type=jnp....]
    unnamed x52 -> x62, local copies, waits for them, and re-layouts: 106 us -> 9.68 us
    pallas_call x0 -> x4, Pallas kernels: none -> 78 us  [expert(): pl.pallas_call(mlp_kernel, in_specs=[pl.BlockSpec(memory_space=pltpu.SMEM...]
  transfers between devices with their start and end apart: 8 -> 92, of which waited for: 8 -> 61; matrix products, arithmetic and copies ran while one was open for 1% -> 6% of each run, Pallas kernels for 0% -> 0%
where the time goes in v2:
time: 584 us; the launch traced here: 575 us
  waiting for transfers between devices  284 us (49%)
  starting transfers between devices  148 us (25%)
  Pallas kernels  78 us (13%)
  other arithmetic  37.9 us (6%)
  between operations  14.7 us (3%)
  local copies, waits for them, and re-layouts  12.4 us (2%)
    ppermute x32, waiting for transfers between devices, upward(): return lax.ppermute(value, 'expert', [(i, (i + 2) % 8) for i in range(8)])  150 us
    ppermute x32, starting transfers between devices, downward(): return lax.ppermute(value, 'expert', [(i, (i - 2) % 8) for i in range(8)])  89.6 us
    pallas_call x4, Pallas kernels, expert(): pl.pallas_call(mlp_kernel, in_specs=[pl.BlockSpec(memory_space=pltpu.SMEM...  78 us
    ppermute x32, waiting for transfers between devices, downward(): return lax.ppermute(value, 'expert', [(i, (i - 2) % 8) for i in range(8)])  55.6 us
    ppermute x12, waiting for transfers between devices, relayed(): return lax.ppermute(value, ('section', 'expert'), pairs)  36 us
    ppermute x12, starting transfers between devices, relayed(): return lax.ppermute(value, ('section', 'expert'), pairs)  30 us
    reduce_scatter x4, waiting for transfers between devices, scatter_second(): lax.psum_scatter(both, 'expert', scatter_dimension=0, axis_index_groups=R...  25.9 us
    ppermute x12, starting transfers between devices, across(): return lax.ppermute(value, 'expert', [(i, i ^ 1) for i in range(8)])  17.8 us
  transfers between devices with their start and end apart: 92, of which 61 were waited for; matrix products, arithmetic and copies ran while one was open for 6% of the time, Pallas kernels for 0%

profile of v2, /device:TPU:2, one launch (start us, length us, event | category | flops | bytes accessed | tf_op | source)
XLA Modules:
  0.0 575.1 jit_solution(10385175918919654621)
XLA Ops:
  11.8 3.1 collective-permute-start.1
  17.3 3.5 collective-permute-done.1
  20.9 3.8 collective-permute-start.3
  24.8 6.1 %collective-permute-done.2 = bf16[64,1024]{1,0:T(8,128)(2,1)S(1)} collective-permute-done((bf16[64,1024]{1,0:T(8,128)(2,1)S(1)}, bf16[64,1024]{1,0:T(8,128)(2,1)S(1)}, u32[]{:S(2)}, u32[]{:S(2)}) %collective-permute-start.2) | collective-permute-done | bytes 131104 | tf_op jit(solution)/shard_map/ppermute | solution.py:33
  33.4 3.3 collective-permute-start.9
  36.7 3.2 collective-permute-start.8
  39.9 9.5 %collective-permute-done.6.refs_2_ = bf16[128,2048]{1,0:T(8,128)(2,1)S(1)} collective-permute-done((bf16[128,2048]{1,0:T(8,128)(2,1)S(1)}, bf16[128,2048]{1,0:T(8,128)(2,1)S(1)}, u32[]{:S(2)}, u32[]{:S(2)}) %collective-permute-start.6) | collective-permute-done | bytes 524320 | tf_op jit(solution)/shard_map/ppermute | solution.py:33
  49.4 3.8 collective-permute-start.11
  53.4 3.5 collective-permute-done.5.refs_9_
  60.8 7.7 %collective-permute-done.10.refs_6_ = bf16[128,2048]{1,0:T(8,128)(2,1)} collective-permute-done((bf16[128,2048]{1,0:T(8,128)(2,1)S(1)}, bf16[128,2048]{1,0:T(8,128)(2,1)}, u32[]{:S(2)}, u32[]{:S(2)}) %collective-permute-start.10) | collective-permute-done | bytes 524320 | tf_op jit(solution)/shard_map/ppermute | solution.py:33
  70.6 19.5 %expert_mlp.4 = (bf16[128,2048]{1,0:T(8,128)(2,1)S(1)}, bf16[128,2048]{1,0:T(8,128)(2,1)S(1)}, bf16[128,2048]{1,0:T(8,128)(2,1)}, bf16[128,2048]{1,0:T(8,128)(2,...) custom-call(s32[4]{0:T(128)S(1)} %pad_add_fusion.turns, ...), custom_call_target="tpu_custom_call" | custom-call | flops 12079595520 | bytes 23592960 | tf_op jit(solution)/shard_map/expert_mlp/pallas_call | solution.py:190
  96.7 9.5 %collective-permute-done.13 = bf16[128,2048]{1,0:T(8,128)(2,1)S(1)} collective-permute-done((bf16[128,2048]{1,0:T(8,128)(2,1)S(1)}, bf16[128,2048]{1,0:T(8,128)(2,1)S(1)}, u32[]{:S(2)}, u32[]{:S(2)}) %collective-permute-start.13) | collective-permute-done | bytes 524320 | tf_op jit(solution)/shard_map/ppermute | solution.py:33
  108.2 3.7 collective-permute-start.17
  118.6 5.8 %collective-permute-done.14 = bf16[128,2048]{1,0:T(8,128)(2,1)} collective-permute-done((bf16[128,2048]{1,0:T(8,128)(2,1)S(1)}, bf16[128,2048]{1,0:T(8,128)(2,1)}, u32[]{:S(2)}, u32[]{:S(2)}) %collective-permute-start.14) | collective-permute-done | bytes 524320 | tf_op jit(solution)/shard_map/ppermute | solution.py:33
  129.2 3.1 collective-permute-start.19
  132.4 8.0 %reduce-scatter.5.cloned.1.call-done = bf16[1,64,2048]{2,1,0:T(8,128)(2,1)} async-done(((bf16[4,64,2048]{2,1,0:T(8,128)(2,1)}), bf16[1,64,2048]{2,1,0:T(8,128)(2,1)}) %reduce-scatter.5.cloned.1.call-update) | async-done | bytes 262160 | tf_op jit(solution)/shard_map/reduce_scatter | solution.py:105
  144.0 3.0 collective-permute-done.19
  150.4 2.9 collective-permute-start.30
  157.7 3.3 collective-permute-start.32
  169.8 3.2 collective-permute-start.25
  173.0 9.6 %collective-permute-done.26.refs_5_ = bf16[128,2048]{1,0:T(8,128)(2,1)} collective-permute-done((bf16[128,2048]{1,0:T(8,128)(2,1)S(1)}, bf16[128,2048]{1,0:T(8,128)(2,1)}, u32[]{:S(2)}, u32[]{:S(2)}) %collective-permute-start.26) | collective-permute-done | bytes 524320 | tf_op jit(solution)/shard_map/ppermute | solution.py:37
  185.9 10.9 %collective-permute-done.24.refs_3_ = bf16[128,2048]{1,0:T(8,128)(2,1)} collective-permute-done((bf16[128,2048]{1,0:T(8,128)(2,1)S(1)}, bf16[128,2048]{1,0:T(8,128)(2,1)}, u32[]{:S(2)}, u32[]{:S(2)}) %collective-permute-start.24) | collective-permute-done | bytes 524320 | tf_op jit(solution)/shard_map/ppermute | solution.py:33
  199.7 3.1 collective-permute-done.27.refs_6_
  204.1 19.5 %expert_mlp.5 = (bf16[128,2048]{1,0:T(8,128)(2,1)S(1)}, bf16[128,2048]{1,0:T(8,128)(2,1)S(1)}, bf16[128,2048]{1,0:T(8,128)(2,1)}, bf16[128,2048]{1,0:T(8,128)(2,...) custom-call(s32[4]{0:T(128)S(1)} %pad_add_fusion.turns, ...), custom_call_target="tpu_custom_call" | custom-call | flops 12079595520 | bytes 23592960 | tf_op jit(solution)/shard_map/expert_mlp/pallas_call | solution.py:190
  224.6 3.1 collective-permute-start.38
  229.8 9.9 %collective-permute-done.35 = bf16[128,2048]{1,0:T(8,128)(2,1)S(1)} collective-permute-done((bf16[128,2048]{1,0:T(8,128)(2,1)S(1)}, bf16[128,2048]{1,0:T(8,128)(2,1)S(1)}, u32[]{:S(2)}, u32[]{:S(2)}) %collective-permute-start.35) | collective-permute-done | bytes 524320 | tf_op jit(solution)/shard_map/ppermute | solution.py:33
  241.6 3.6 collective-permute-start.39
  246.7 3.2 collective-permute-done.34
  249.9 6.3 %collective-permute-done.36 = bf16[128,2048]{1,0:T(8,128)(2,1)} collective-permute-done((bf16[128,2048]{1,0:T(8,128)(2,1)}, bf16[128,2048]{1,0:T(8,128)(2,1)}, u32[]{:S(2)}, u32[]{:S(2)}) %collective-permute-start.36) | collective-permute-done | bytes 524320 | tf_op jit(solution)/shard_map/ppermute | solution.py:33
  260.0 7.1 %collective-permute-start.41 = (bf16[64,4096]{1,0:T(8,128)(2,1)}, bf16[64,4096]{1,0:T(8,128)(2,1)S(1)}, u32[]{:S(2)}, u32[]{:S(2)}) collective-permute-start(bf16[64,4096]{1,0:T(8,128)(2,1)} %fusion.22), channel_id=1, source_target_pairs={{0,9},{1,8},{2,11},{3,10},{4,13},{5,12},{6,15},{7,14},{8,17},{9,16... | collective-permute-start | bytes 1572872 | tf_op jit(solution)/shard_map/ppermute | solution.py:25
  267.1 9.9 %reduce-scatter.7.cloned.1.call-done = bf16[1,64,2048]{2,1,0:T(8,128)(2,1)} async-done(((bf16[4,64,2048]{2,1,0:T(8,128)(2,1)}), bf16[1,64,2048]{2,1,0:T(8,128)(2,1)}) %reduce-scatter.7.cloned.1.call-update) | async-done | bytes 262160 | tf_op jit(solution)/shard_map/reduce_scatter | solution.py:105
  279.2 6.8 %collective-permute-done.43 = bf16[64,2048]{1,0:T(8,128)(2,1)S(1)} collective-permute-done((bf16[64,2048]{1,0:T(8,128)(2,1)S(1)}, bf16[64,2048]{1,0:T(8,128)(2,1)S(1)}, u32[]{:S(2)}, u32[]{:S(2)}) %collective-permute-start.43) | collective-permute-done | bytes 262176 | tf_op jit(solution)/shard_map/ppermute | solution.py:25
  286.4 3.2 collective-permute-start.52
  294.2 3.4 collective-permute-start.54
  306.5 3.2 collective-permute-start.47
  309.7 9.5 %collective-permute-done.48.refs_5_ = bf16[128,2048]{1,0:T(8,128)(2,1)} collective-permute-done((bf16[128,2048]{1,0:T(8,128)(2,1)S(1)}, bf16[128,2048]{1,0:T(8,128)(2,1)}, u32[]{:S(2)}, u32[]{:S(2)}) %collective-permute-start.48) | collective-permute-done | bytes 524320 | tf_op jit(solution)/shard_map/ppermute | solution.py:37
  319.2 3.2 collective-permute-start.50
  322.9 9.8 %collective-permute-done.46.refs_3_ = bf16[128,2048]{1,0:T(8,128)(2,1)} collective-permute-done((bf16[128,2048]{1,0:T(8,128)(2,1)S(1)}, bf16[128,2048]{1,0:T(8,128)(2,1)}, u32[]{:S(2)}, u32[]{:S(2)}) %collective-permute-start.46) | collective-permute-done | bytes 524320 | tf_op jit(solution)/shard_map/ppermute | solution.py:33
  339.6 19.5 %expert_mlp.6 = (bf16[128,2048]{1,0:T(8,128)(2,1)S(1)}, bf16[128,2048]{1,0:T(8,128)(2,1)S(1)}, bf16[128,2048]{1,0:T(8,128)(2,1)}, bf16[128,2048]{1,0:T(8,128)(2,...) custom-call(s32[4]{0:T(128)S(1)} %pad_add_fusion.turns, ...), custom_call_target="tpu_custom_call" | custom-call | flops 12079595520 | bytes 23592960 | tf_op jit(solution)/shard_map/expert_mlp/pallas_call | solution.py:190
  360.5 3.1 collective-permute-start.60
  365.7 9.5 %collective-permute-done.57 = bf16[128,2048]{1,0:T(8,128)(2,1)S(1)} collective-permute-done((bf16[128,2048]{1,0:T(8,128)(2,1)S(1)}, bf16[128,2048]{1,0:T(8,128)(2,1)S(1)}, u32[]{:S(2)}, u32[]{:S(2)}) %collective-permute-start.57) | collective-permute-done | bytes 524320 | tf_op jit(solution)/shard_map/ppermute | solution.py:33
  377.1 3.8 collective-permute-start.61
  384.7 5.4 collective-permute-done.58
  394.0 19.2 %collective-permute-start.63 = (bf16[64,4096]{1,0:T(8,128)(2,1)}, bf16[64,4096]{1,0:T(8,128)(2,1)S(1)}, u32[]{:S(2)}, u32[]{:S(2)}) collective-permute-start(bf16[64,4096]{1,0:T(8,128)(2,1)} %fusion.21), channel_id=1, source_target_pairs={{0,9},{1,8},{2,11},{3,10},{4,13},{5,12},{6,15},{7,14},{8,17},{9,16... | collective-permute-start | bytes 1572872 | tf_op jit(solution)/shard_map/ppermute | solution.py:25
  415.5 9.5 %collective-permute-done.63 = bf16[64,4096]{1,0:T(8,128)(2,1)S(1)} collective-permute-done((bf16[64,4096]{1,0:T(8,128)(2,1)}, bf16[64,4096]{1,0:T(8,128)(2,1)S(1)}, u32[]{:S(2)}, u32[]{:S(2)}) %collective-permute-start.63) | collective-permute-done | bytes 524320 | tf_op jit(solution)/shard_map/ppermute | solution.py:25
  425.7 3.8 collective-permute-start.74
  429.7 5.4 collective-permute-done.73
  435.2 3.3 collective-permute-start.76
  441.5 3.7 collective-permute-done.66
  447.6 3.2 collective-permute-start.69
  450.8 9.5 %collective-permute-done.70.refs_5_ = bf16[128,2048]{1,0:T(8,128)(2,1)} collective-permute-done((bf16[128,2048]{1,0:T(8,128)(2,1)S(1)}, bf16[128,2048]{1,0:T(8,128)(2,1)}, u32[]{:S(2)}, u32[]{:S(2)}) %collective-permute-start.70) | collective-permute-done | bytes 524320 | tf_op jit(solution)/shard_map/ppermute | solution.py:37
  460.2 2.8 collective-permute-start.72
  463.6 10.8 %collective-permute-done.68.refs_3_ = bf16[128,2048]{1,0:T(8,128)(2,1)} collective-permute-done((bf16[128,2048]{1,0:T(8,128)(2,1)S(1)}, bf16[128,2048]{1,0:T(8,128)(2,1)}, u32[]{:S(2)}, u32[]{:S(2)}) %collective-permute-start.68) | collective-permute-done | bytes 524320 | tf_op jit(solution)/shard_map/ppermute | solution.py:33
  475.4 6.7 %collective-permute-done.72.refs_7_ = bf16[128,2048]{1,0:T(8,128)(2,1)} collective-permute-done((bf16[128,2048]{1,0:T(8,128)(2,1)}, bf16[128,2048]{1,0:T(8,128)(2,1)}, u32[]{:S(2)}, u32[]{:S(2)}) %collective-permute-start.72) | collective-permute-done | bytes 524320 | tf_op jit(solution)/shard_map/ppermute | solution.py:37
  482.1 3.0 collective-permute-done.71.refs_6_
  486.3 19.5 %expert_mlp.7 = (bf16[128,2048]{1,0:T(8,128)(2,1)S(1)}, bf16[128,2048]{1,0:T(8,128)(2,1)S(1)}, bf16[128,2048]{1,0:T(8,128)(2,1)}, bf16[128,2048]{1,0:T(8,128)(2,...) custom-call(s32[4]{0:T(128)S(1)} %pad_add_fusion.turns, ...), custom_call_target="tpu_custom_call" | custom-call | flops 12079595520 | bytes 23592960 | tf_op jit(solution)/shard_map/expert_mlp/pallas_call | solution.py:190
  507.7 3.1 collective-permute-start.82
  512.8 9.1 %collective-permute-done.79 = bf16[128,2048]{1,0:T(8,128)(2,1)S(1)} collective-permute-done((bf16[128,2048]{1,0:T(8,128)(2,1)S(1)}, bf16[128,2048]{1,0:T(8,128)(2,1)S(1)}, u32[]{:S(2)}, u32[]{:S(2)}) %collective-permute-start.79) | collective-permute-done | bytes 524320 | tf_op jit(solution)/shard_map/ppermute | solution.py:33
  524.1 4.0 collective-permute-start.83
  528.1 4.0 collective-permute-done.86
  534.5 9.3 %collective-permute-done.80 = bf16[128,2048]{1,0:T(8,128)(2,1)S(1)} collective-permute-done((bf16[128,2048]{1,0:T(8,128)(2,1)}, bf16[128,2048]{1,0:T(8,128)(2,1)S(1)}, u32[]{:S(2)}, u32[]{:S(2)}) %collective-permute-start.80) | collective-permute-done | bytes 524320 | tf_op jit(solution)/shard_map/ppermute | solution.py:33
  548.1 6.8 %reduce-scatter.11.cloned.1.call-done = bf16[1,64,2048]{2,1,0:T(8,128)(2,1)} async-done(((bf16[4,64,2048]{2,1,0:T(8,128)(2,1)}), bf16[1,64,2048]{2,1,0:T(8,128)(2,1)}) %reduce-scatter.11.cloned.1.call-update) | async-done | bytes 262160 | tf_op jit(solution)/shard_map/reduce_scatter | solution.py:105
  556.0 3.5 collective-permute-done.84
  559.4 7.1 %collective-permute-done.85 = bf16[64,4096]{1,0:T(8,128)(2,1)S(1)} collective-permute-done((bf16[64,4096]{1,0:T(8,128)(2,1)S(1)}, bf16[64,4096]{1,0:T(8,128)(2,1)S(1)}, u32[]{:S(2)}, u32[]{:S(2)}) %collective-permute-start.85) | collective-permute-done | bytes 524320 | tf_op jit(solution)/shard_map/ppermute | solution.py:25
  (292 shorter events, 136.6 us)
Async XLA Ops:
  6.5 133.8 %reduce-scatter.5.cloned.1.call-start = ((), (), s32[]{:S(2)}) async-start(), calls=%async_computation.4 | async-start | bytes 1310720 | tf_op jit(solution)/shard_map/reduce_scatter | solution.py:105
  15.1 15.8 %collective-permute-start.4 = (bf16[64,4096]{1,0:T(8,128)(2,1)S(1)}, bf16[64,4096]{1,0:T(8,128)(2,1)S(1)}, u32[]{:S(2)}, u32[]{:S(2)}) collective-permute-start(bf16[64,4096]{1,0:T(8,128)(2,1)S(1)} %fusion.14), channel_id=1, source_target_pairs={{0,1},{1,0},{2,3},{3,2},{4,5},{5,4},{6,7},{7,6},{8,9},{9,8},{10,11... | collective-permute-start | bytes 1572872 | tf_op jit(solution)/shard_map/ppermute | solution.py:29
  31.0 25.8 %collective-permute-start.5 = (bf16[256,2176]{1,0:T(8,128)(2,1)S(1)}, bf16[256,2176]{1,0:T(8,128)(2,1)}, u32[]{:S(2)}, u32[]{:S(2)}) collective-permute-start(bf16[256,2176]{1,0:T(8,128)(2,1)S(1)} %maximum_maximum_fusion.refs_8_), channel_id=1, source_target_pairs={{0,1},{1,0},{2,3},{3,2},{4,5},{5,4},{6,7},{7,6},{8,9},{9,8},{10,11... | collective-permute-start | bytes 3342344 | tf_op jit(solution)/shard_map/ppermute | solution.py:29
  33.3 16.1 %collective-permute-start.6 = (bf16[128,2048]{1,0:T(8,128)(2,1)S(1)}, bf16[128,2048]{1,0:T(8,128)(2,1)S(1)}, u32[]{:S(2)}, u32[]{:S(2)}) collective-permute-start(bf16[128,2048]{1,0:T(8,128)(2,1)S(1)} %pad_maximum_fusion.4.refs_0_), channel_id=1, source_target_pairs={{0,2},{1,3},{2,4},{3,5},{4,6},{5,7},{6,0},{7,1},{8,10},{9,11},{10,... | collective-permute-start | bytes 1572872 | tf_op jit(solution)/shard_map/ppermute | solution.py:33
  33.4 16.0 %collective-permute-start.9 = (bf16[128,2048]{1,0:T(8,128)(2,1)S(1)}, bf16[128,2048]{1,0:T(8,128)(2,1)S(1)}, u32[]{:S(2)}, u32[]{:S(2)}) collective-permute-start(bf16[128,2048]{1,0:T(8,128)(2,1)S(1)} %pad_maximum_fusion.5.refs_1_), channel_id=1, source_target_pairs={{0,6},{1,7},{2,0},{3,1},{4,2},{5,3},{6,4},{7,5},{8,14},{9,15},{10,... | collective-permute-start | bytes 1572872 | tf_op jit(solution)/shard_map/ppermute | solution.py:37
  36.7 24.1 %collective-permute-start.7 = (bf16[128,2048]{1,0:T(8,128)(2,1)S(1)}, bf16[128,2048]{1,0:T(8,128)(2,1)}, u32[]{:S(2)}, u32[]{:S(2)}) collective-permute-start(bf16[128,2048]{1,0:T(8,128)(2,1)S(1)} %pad_maximum_fusion.5.refs_1_), channel_id=1, source_target_pairs={{0,2},{1,3},{2,4},{3,5},{4,6},{5,7},{6,0},{7,1},{8,10},{9,11},{10,... | collective-permute-start | bytes 1572872 | tf_op jit(solution)/shard_map/ppermute | solution.py:33
  36.7 24.1 %collective-permute-start.8 = (bf16[128,2048]{1,0:T(8,128)(2,1)S(1)}, bf16[128,2048]{1,0:T(8,128)(2,1)}, u32[]{:S(2)}, u32[]{:S(2)}) collective-permute-start(bf16[128,2048]{1,0:T(8,128)(2,1)S(1)} %pad_maximum_fusion.4.refs_0_), channel_id=1, source_target_pairs={{0,6},{1,7},{2,0},{3,1},{4,2},{5,3},{6,4},{7,5},{8,14},{9,15},{10,... | collective-permute-start | bytes 1572872 | tf_op jit(solution)/shard_map/ppermute | solution.py:37
  49.4 19.1 %collective-permute-start.10 = (bf16[128,2048]{1,0:T(8,128)(2,1)S(1)}, bf16[128,2048]{1,0:T(8,128)(2,1)}, u32[]{:S(2)}, u32[]{:S(2)}) collective-permute-start(bf16[128,2048]{1,0:T(8,128)(2,1)S(1)} %collective-permute-done.6.refs_2_), channel_id=1, source_target_pairs={{0,2},{1,3},{2,4},{3,5},{4,6},{5,7},{6,0},{7,1},{8,10},{9,11},{10,... | collective-permute-start | bytes 1572872 | tf_op jit(solution)/shard_map/ppermute | solution.py:33
  49.4 19.1 %collective-permute-start.11 = (bf16[128,2048]{1,0:T(8,128)(2,1)S(1)}, bf16[128,2048]{1,0:T(8,128)(2,1)}, u32[]{:S(2)}, u32[]{:S(2)}) collective-permute-start(bf16[128,2048]{1,0:T(8,128)(2,1)S(1)} %collective-permute-done.9.refs_5_), channel_id=1, source_target_pairs={{0,6},{1,7},{2,0},{3,1},{4,2},{5,3},{6,4},{7,5},{8,14},{9,15},{10,... | collective-permute-start | bytes 1572872 | tf_op jit(solution)/shard_map/ppermute | solution.py:37
  90.2 16.1 %collective-permute-start.13 = (bf16[128,2048]{1,0:T(8,128)(2,1)S(1)}, bf16[128,2048]{1,0:T(8,128)(2,1)S(1)}, u32[]{:S(2)}, u32[]{:S(2)}) collective-permute-start(bf16[128,2048]{1,0:T(8,128)(2,1)S(1)} %get-tuple-element.53), channel_id=1, source_target_pairs={{0,2},{1,3},{2,4},{3,5},{4,6},{5,7},{6,0},{7,1},{8,10},{9,11},{10,... | collective-permute-start | bytes 1572872 | tf_op jit(solution)/shard_map/ppermute | solution.py:33
  91.0 23.4 %collective-permute-start.20 = (bf16[4,64,2048]{2,1,0:T(8,128)(2,1)S(1)}, bf16[4,64,2048]{2,1,0:T(8,128)(2,1)S(1)}, u32[]{:S(2)}, u32[]{:S(2)}) collective-permute-start(bf16[4,64,2048]{2,1,0:T(8,128)(2,1)S(1)} %get-tuple-element.59), channel_id=1, source_target_pairs={{0,1},{1,0},{2,3},{3,2},{4,5},{5,4},{6,7},{7,6},{8,9},{9,8},{10,11... | collective-permute-start | bytes 3145736 | tf_op jit(solution)/shard_map/ppermute | solution.py:29
  94.7 23.9 %collective-permute-start.12 = (bf16[128,2048]{1,0:T(8,128)(2,1)}, bf16[128,2048]{1,0:T(8,128)(2,1)}, u32[]{:S(2)}, u32[]{:S(2)}) collective-permute-start(bf16[128,2048]{1,0:T(8,128)(2,1)} %get-tuple-element.51), channel_id=1, source_target_pairs={{0,6},{1,7},{2,0},{3,1},{4,2},{5,3},{6,4},{7,5},{8,14},{9,15},{10,... | collective-permute-start | bytes 1572872 | tf_op jit(solution)/shard_map/ppermute | solution.py:37
  96.6 29.5 %collective-permute-start.15 = (bf16[128,2048]{1,0:T(8,128)(2,1)}, bf16[128,2048]{1,0:T(8,128)(2,1)}, u32[]{:S(2)}, u32[]{:S(2)}) collective-permute-start(bf16[128,2048]{1,0:T(8,128)(2,1)} %get-tuple-element.55), channel_id=1, source_target_pairs={{0,2},{1,3},{2,4},{3,5},{4,6},{5,7},{6,0},{7,1},{8,10},{9,11},{10,... | collective-permute-start | bytes 1572872 | tf_op jit(solution)/shard_map/ppermute | solution.py:33
  106.4 18.0 %collective-permute-start.14 = (bf16[128,2048]{1,0:T(8,128)(2,1)S(1)}, bf16[128,2048]{1,0:T(8,128)(2,1)}, u32[]{:S(2)}, u32[]{:S(2)}) collective-permute-start(bf16[128,2048]{1,0:T(8,128)(2,1)S(1)} %add_convert_fusion.15), channel_id=1, source_target_pairs={{0,2},{1,3},{2,4},{3,5},{4,6},{5,7},{6,0},{7,1},{8,10},{9,11},{10,... | collective-permute-start | bytes 1572872 | tf_op jit(solution)/shard_map/ppermute | solution.py:33
  108.2 17.8 %collective-permute-start.17 = (bf16[128,2048]{1,0:T(8,128)(2,1)}, bf16[128,2048]{1,0:T(8,128)(2,1)}, u32[]{:S(2)}, u32[]{:S(2)}) collective-permute-start(bf16[128,2048]{1,0:T(8,128)(2,1)} %add_convert_fusion.14), channel_id=1, source_target_pairs={{0,6},{1,7},{2,0},{3,1},{4,2},{5,3},{6,4},{7,5},{8,14},{9,15},{10,... | collective-permute-start | bytes 1572872 | tf_op jit(solution)/shard_map/ppermute | solution.py:37
  115.8 161.2 %reduce-scatter.7.cloned.1.call-start = ((), (), s32[]{:S(2)}) async-start(), calls=%async_computation.5 | async-start | bytes 1310720 | tf_op jit(solution)/shard_map/reduce_scatter | solution.py:105
  128.4 15.7 %collective-permute-start.18 = (bf16[64,4096]{1,0:T(8,128)(2,1)}, bf16[64,4096]{1,0:T(8,128)(2,1)S(1)}, u32[]{:S(2)}, u32[]{:S(2)}) collective-permute-start(bf16[64,4096]{1,0:T(8,128)(2,1)} %fusion.15), channel_id=1, source_target_pairs={{0,8},{1,9},{2,10},{3,11},{4,12},{5,13},{6,14},{7,15},{8,16},{9,17... | collective-permute-start | bytes 1572872 | tf_op jit(solution)/shard_map/ppermute | solution.py:25
  129.2 17.8 %collective-permute-start.19 = (bf16[64,4096]{1,0:T(8,128)(2,1)}, bf16[64,4096]{1,0:T(8,128)(2,1)S(1)}, u32[]{:S(2)}, u32[]{:S(2)}) collective-permute-start(bf16[64,4096]{1,0:T(8,128)(2,1)} %fusion.23), channel_id=1, source_target_pairs={{0,9},{1,8},{2,11},{3,10},{4,13},{5,12},{6,15},{7,14},{8,17},{9,16... | collective-permute-start | bytes 1572872 | tf_op jit(solution)/shard_map/ppermute | solution.py:25
  165.7 31.1 %collective-permute-start.33 = (bf16[256,2048]{1,0:T(8,128)(2,1)S(1)}, bf16[256,2048]{1,0:T(8,128)(2,1)S(1)}, u32[]{:S(2)}, u32[]{:S(2)}) collective-permute-start(bf16[256,2048]{1,0:T(8,128)(2,1)S(1)} %maximum_maximum_fusion.1.refs_8_), channel_id=1, source_target_pairs={{0,1},{1,0},{2,3},{3,2},{4,5},{5,4},{6,7},{7,6},{8,9},{9,8},{10,11... | collective-permute-start | bytes 3145736 | tf_op jit(solution)/shard_map/ppermute | solution.py:29
  169.3 16.2 %collective-permute-start.23 = (bf16[128,2048]{1,0:T(8,128)(2,1)S(1)}, bf16[128,2048]{1,0:T(8,128)(2,1)}, u32[]{:S(2)}, u32[]{:S(2)}) collective-permute-start(bf16[128,2048]{1,0:T(8,128)(2,1)S(1)} %pad_maximum_fusion.6.refs_0_), channel_id=1, source_target_pairs={{0,2},{1,3},{2,4},{3,5},{4,6},{5,7},{6,0},{7,1},{8,10},{9,11},{10,... | collective-permute-start | bytes 1572872 | tf_op jit(solution)/shard_map/ppermute | solution.py:33
  169.8 27.0 %collective-permute-start.24 = (bf16[128,2048]{1,0:T(8,128)(2,1)S(1)}, bf16[128,2048]{1,0:T(8,128)(2,1)}, u32[]{:S(2)}, u32[]{:S(2)}) collective-permute-start(bf16[128,2048]{1,0:T(8,128)(2,1)S(1)} %pad_maximum_fusion.7.refs_1_), channel_id=1, source_target_pairs={{0,2},{1,3},{2,4},{3,5},{4,6},{5,7},{6,0},{7,1},{8,10},{9,11},{10,... | collective-permute-start | bytes 1572872 | tf_op jit(solution)/shard_map/ppermute | solution.py:33
  169.8 26.9 %collective-permute-start.25 = (bf16[128,2048]{1,0:T(8,128)(2,1)S(1)}, bf16[128,2048]{1,0:T(8,128)(2,1)}, u32[]{:S(2)}, u32[]{:S(2)}) collective-permute-start(bf16[128,2048]{1,0:T(8,128)(2,1)S(1)} %pad_maximum_fusion.6.refs_0_), channel_id=1, source_target_pairs={{0,6},{1,7},{2,0},{3,1},{4,2},{5,3},{6,4},{7,5},{8,14},{9,15},{10,... | collective-permute-start | bytes 1572872 | tf_op jit(solution)/shard_map/ppermute | solution.py:37
  182.6 17.1 %collective-permute-start.28 = (bf16[128,2048]{1,0:T(8,128)(2,1)}, bf16[128,2048]{1,0:T(8,128)(2,1)}, u32[]{:S(2)}, u32[]{:S(2)}) collective-permute-start(bf16[128,2048]{1,0:T(8,128)(2,1)} %collective-permute-done.26.refs_5_), channel_id=1, source_target_pairs={{0,6},{1,7},{2,0},{3,1},{4,2},{5,3},{6,4},{7,5},{8,14},{9,15},{10,... | collective-permute-start | bytes 1572872 | tf_op jit(solution)/shard_map/ppermute | solution.py:37
  185.5 17.3 %collective-permute-start.27 = (bf16[128,2048]{1,0:T(8,128)(2,1)}, bf16[128,2048]{1,0:T(8,128)(2,1)}, u32[]{:S(2)}, u32[]{:S(2)}) collective-permute-start(bf16[128,2048]{1,0:T(8,128)(2,1)} %collective-permute-done.23.refs_2_), channel_id=1, source_target_pairs={{0,2},{1,3},{2,4},{3,5},{4,6},{5,7},{6,0},{7,1},{8,10},{9,11},{10,... | collective-permute-start | bytes 1572872 | tf_op jit(solution)/shard_map/ppermute | solution.py:33
  223.6 16.1 %collective-permute-start.35 = (bf16[128,2048]{1,0:T(8,128)(2,1)S(1)}, bf16[128,2048]{1,0:T(8,128)(2,1)S(1)}, u32[]{:S(2)}, u32[]{:S(2)}) collective-permute-start(bf16[128,2048]{1,0:T(8,128)(2,1)S(1)} %get-tuple-element.64), channel_id=1, source_target_pairs={{0,2},{1,3},{2,4},{3,5},{4,6},{5,7},{6,0},{7,1},{8,10},{9,11},{10,... | collective-permute-start | bytes 1572872 | tf_op jit(solution)/shard_map/ppermute | solution.py:33
  223.6 21.6 %collective-permute-start.42 = (bf16[4,64,2048]{2,1,0:T(8,128)(2,1)S(1)}, bf16[4,64,2048]{2,1,0:T(8,128)(2,1)S(1)}, u32[]{:S(2)}, u32[]{:S(2)}) collective-permute-start(bf16[4,64,2048]{2,1,0:T(8,128)(2,1)S(1)} %get-tuple-element.70), channel_id=1, source_target_pairs={{0,1},{1,0},{2,3},{3,2},{4,5},{5,4},{6,7},{7,6},{8,9},{9,8},{10,11... | collective-permute-start | bytes 3145736 | tf_op jit(solution)/shard_map/ppermute | solution.py:29
  224.6 16.0 %collective-permute-start.38 = (bf16[128,2048]{1,0:T(8,128)(2,1)S(1)}, bf16[128,2048]{1,0:T(8,128)(2,1)S(1)}, u32[]{:S(2)}, u32[]{:S(2)}) collective-permute-start(bf16[128,2048]{1,0:T(8,128)(2,1)S(1)} %get-tuple-element.68), channel_id=1, source_target_pairs={{0,6},{1,7},{2,0},{3,1},{4,2},{5,3},{6,4},{7,5},{8,14},{9,15},{10,... | collective-permute-start | bytes 1572872 | tf_op jit(solution)/shard_map/ppermute | solution.py:37
  227.8 22.1 %collective-permute-start.34 = (bf16[128,2048]{1,0:T(8,128)(2,1)}, bf16[128,2048]{1,0:T(8,128)(2,1)S(1)}, u32[]{:S(2)}, u32[]{:S(2)}) collective-permute-start(bf16[128,2048]{1,0:T(8,128)(2,1)} %get-tuple-element.62), channel_id=1, source_target_pairs={{0,6},{1,7},{2,0},{3,1},{4,2},{5,3},{6,4},{7,5},{8,14},{9,15},{10,... | collective-permute-start | bytes 1572872 | tf_op jit(solution)/shard_map/ppermute | solution.py:37
  227.8 29.8 %collective-permute-start.37 = (bf16[128,2048]{1,0:T(8,128)(2,1)}, bf16[128,2048]{1,0:T(8,128)(2,1)S(1)}, u32[]{:S(2)}, u32[]{:S(2)}) collective-permute-start(bf16[128,2048]{1,0:T(8,128)(2,1)} %get-tuple-element.66), channel_id=1, source_target_pairs={{0,2},{1,3},{2,4},{3,5},{4,6},{5,7},{6,0},{7,1},{8,10},{9,11},{10,... | collective-permute-start | bytes 1572872 | tf_op jit(solution)/shard_map/ppermute | solution.py:33
  240.6 15.6 %collective-permute-start.36 = (bf16[128,2048]{1,0:T(8,128)(2,1)}, bf16[128,2048]{1,0:T(8,128)(2,1)}, u32[]{:S(2)}, u32[]{:S(2)}) collective-permute-start(bf16[128,2048]{1,0:T(8,128)(2,1)} %add_convert_fusion.12), channel_id=1, source_target_pairs={{0,2},{1,3},{2,4},{3,5},{4,6},{5,7},{6,0},{7,1},{8,10},{9,11},{10,... | collective-permute-start | bytes 1572872 | tf_op jit(solution)/shard_map/ppermute | solution.py:33
  241.6 16.0 %collective-permute-start.39 = (bf16[128,2048]{1,0:T(8,128)(2,1)}, bf16[128,2048]{1,0:T(8,128)(2,1)}, u32[]{:S(2)}, u32[]{:S(2)}) collective-permute-start(bf16[128,2048]{1,0:T(8,128)(2,1)} %add_convert_fusion.11), channel_id=1, source_target_pairs={{0,6},{1,7},{2,0},{3,1},{4,2},{5,3},{6,4},{7,5},{8,14},{9,15},{10,... | collective-permute-start | bytes 1572872 | tf_op jit(solution)/shard_map/ppermute | solution.py:37
  246.6 167.7 %reduce-scatter.9.cloned.1.call-start = ((), (), s32[]{:S(2)}) async-start(), calls=%async_computation.6 | async-start | bytes 1310720 | tf_op jit(solution)/shard_map/reduce_scatter | solution.py:105
  259.1 19.1 %collective-permute-start.40 = (bf16[64,4096]{1,0:T(8,128)(2,1)S(1)}, bf16[64,4096]{1,0:T(8,128)(2,1)S(1)}, u32[]{:S(2)}, u32[]{:S(2)}) collective-permute-start(bf16[64,4096]{1,0:T(8,128)(2,1)S(1)} %fusion.3), channel_id=1, source_target_pairs={{0,8},{1,9},{2,10},{3,11},{4,12},{5,13},{6,14},{7,15},{8,16},{9,17... | collective-permute-start | bytes 1572872 | tf_op jit(solution)/shard_map/ppermute | solution.py:25
  260.0 18.9 %collective-permute-start.41 = (bf16[64,4096]{1,0:T(8,128)(2,1)}, bf16[64,4096]{1,0:T(8,128)(2,1)S(1)}, u32[]{:S(2)}, u32[]{:S(2)}) collective-permute-start(bf16[64,4096]{1,0:T(8,128)(2,1)} %fusion.22), channel_id=1, source_target_pairs={{0,9},{1,8},{2,11},{3,10},{4,13},{5,12},{6,15},{7,14},{8,17},{9,16... | collective-permute-start | bytes 1572872 | tf_op jit(solution)/shard_map/ppermute | solution.py:25
  302.0 30.7 %collective-permute-start.55 = (bf16[256,2048]{1,0:T(8,128)(2,1)S(1)}, bf16[256,2048]{1,0:T(8,128)(2,1)S(1)}, u32[]{:S(2)}, u32[]{:S(2)}) collective-permute-start(bf16[256,2048]{1,0:T(8,128)(2,1)S(1)} %maximum_maximum_fusion.2.refs_8_), channel_id=1, source_target_pairs={{0,1},{1,0},{2,3},{3,2},{4,5},{5,4},{6,7},{7,6},{8,9},{9,8},{10,11... | collective-permute-start | bytes 3145736 | tf_op jit(solution)/shard_map/ppermute | solution.py:29
  304.2 15.0 %collective-permute-start.48 = (bf16[128,2048]{1,0:T(8,128)(2,1)S(1)}, bf16[128,2048]{1,0:T(8,128)(2,1)}, u32[]{:S(2)}, u32[]{:S(2)}) collective-permute-start(bf16[128,2048]{1,0:T(8,128)(2,1)S(1)} %pad_maximum_fusion.9.refs_1_), channel_id=1, source_target_pairs={{0,6},{1,7},{2,0},{3,1},{4,2},{5,3},{6,4},{7,5},{8,14},{9,15},{10,... | collective-permute-start | bytes 1572872 | tf_op jit(solution)/shard_map/ppermute | solution.py:37
  306.3 16.2 %collective-permute-start.45 = (bf16[128,2048]{1,0:T(8,128)(2,1)S(1)}, bf16[128,2048]{1,0:T(8,128)(2,1)}, u32[]{:S(2)}, u32[]{:S(2)}) collective-permute-start(bf16[128,2048]{1,0:T(8,128)(2,1)S(1)} %pad_maximum_fusion.8.refs_0_), channel_id=1, source_target_pairs={{0,2},{1,3},{2,4},{3,5},{4,6},{5,7},{6,0},{7,1},{8,10},{9,11},{10,... | collective-permute-start | bytes 1572872 | tf_op jit(solution)/shard_map/ppermute | solution.py:33
  306.4 26.3 %collective-permute-start.46 = (bf16[128,2048]{1,0:T(8,128)(2,1)S(1)}, bf16[128,2048]{1,0:T(8,128)(2,1)}, u32[]{:S(2)}, u32[]{:S(2)}) collective-permute-start(bf16[128,2048]{1,0:T(8,128)(2,1)S(1)} %pad_maximum_fusion.9.refs_1_), channel_id=1, source_target_pairs={{0,2},{1,3},{2,4},{3,5},{4,6},{5,7},{6,0},{7,1},{8,10},{9,11},{10,... | collective-permute-start | bytes 1572872 | tf_op jit(solution)/shard_map/ppermute | solution.py:33
  306.5 26.3 %collective-permute-start.47 = (bf16[128,2048]{1,0:T(8,128)(2,1)S(1)}, bf16[128,2048]{1,0:T(8,128)(2,1)}, u32[]{:S(2)}, u32[]{:S(2)}) collective-permute-start(bf16[128,2048]{1,0:T(8,128)(2,1)S(1)} %pad_maximum_fusion.8.refs_0_), channel_id=1, source_target_pairs={{0,6},{1,7},{2,0},{3,1},{4,2},{5,3},{6,4},{7,5},{8,14},{9,15},{10,... | collective-permute-start | bytes 1572872 | tf_op jit(solution)/shard_map/ppermute | solution.py:37
  319.2 16.4 %collective-permute-start.50 = (bf16[128,2048]{1,0:T(8,128)(2,1)}, bf16[128,2048]{1,0:T(8,128)(2,1)}, u32[]{:S(2)}, u32[]{:S(2)}) collective-permute-start(bf16[128,2048]{1,0:T(8,128)(2,1)} %collective-permute-done.48.refs_5_), channel_id=1, source_target_pairs={{0,6},{1,7},{2,0},{3,1},{4,2},{5,3},{6,4},{7,5},{8,14},{9,15},{10,... | collective-permute-start | bytes 1572872 | tf_op jit(solution)/shard_map/ppermute | solution.py:37
  322.6 15.8 %collective-permute-start.49 = (bf16[128,2048]{1,0:T(8,128)(2,1)}, bf16[128,2048]{1,0:T(8,128)(2,1)}, u32[]{:S(2)}, u32[]{:S(2)}) collective-permute-start(bf16[128,2048]{1,0:T(8,128)(2,1)} %collective-permute-done.45.refs_2_), channel_id=1, source_target_pairs={{0,2},{1,3},{2,4},{3,5},{4,6},{5,7},{6,0},{7,1},{8,10},{9,11},{10,... | collective-permute-start | bytes 1572872 | tf_op jit(solution)/shard_map/ppermute | solution.py:33
  359.1 16.1 %collective-permute-start.57 = (bf16[128,2048]{1,0:T(8,128)(2,1)S(1)}, bf16[128,2048]{1,0:T(8,128)(2,1)S(1)}, u32[]{:S(2)}, u32[]{:S(2)}) collective-permute-start(bf16[128,2048]{1,0:T(8,128)(2,1)S(1)} %get-tuple-element.75), channel_id=1, source_target_pairs={{0,2},{1,3},{2,4},{3,5},{4,6},{5,7},{6,0},{7,1},{8,10},{9,11},{10,... | collective-permute-start | bytes 1572872 | tf_op jit(solution)/shard_map/ppermute | solution.py:33
  359.2 21.7 %collective-permute-start.64 = (bf16[4,64,2048]{2,1,0:T(8,128)(2,1)S(1)}, bf16[4,64,2048]{2,1,0:T(8,128)(2,1)S(1)}, u32[]{:S(2)}, u32[]{:S(2)}) collective-permute-start(bf16[4,64,2048]{2,1,0:T(8,128)(2,1)S(1)} %get-tuple-element.81), channel_id=1, source_target_pairs={{0,1},{1,0},{2,3},{3,2},{4,5},{5,4},{6,7},{7,6},{8,9},{9,8},{10,11... | collective-permute-start | bytes 3145736 | tf_op jit(solution)/shard_map/ppermute | solution.py:29
  360.5 15.6 %collective-permute-start.60 = (bf16[128,2048]{1,0:T(8,128)(2,1)S(1)}, bf16[128,2048]{1,0:T(8,128)(2,1)S(1)}, u32[]{:S(2)}, u32[]{:S(2)}) collective-permute-start(bf16[128,2048]{1,0:T(8,128)(2,1)S(1)} %get-tuple-element.79), channel_id=1, source_target_pairs={{0,6},{1,7},{2,0},{3,1},{4,2},{5,3},{6,4},{7,5},{8,14},{9,15},{10,... | collective-permute-start | bytes 1572872 | tf_op jit(solution)/shard_map/ppermute | solution.py:37
  363.7 21.1 %collective-permute-start.56 = (bf16[128,2048]{1,0:T(8,128)(2,1)}, bf16[128,2048]{1,0:T(8,128)(2,1)S(1)}, u32[]{:S(2)}, u32[]{:S(2)}) collective-permute-start(bf16[128,2048]{1,0:T(8,128)(2,1)} %get-tuple-element.73), channel_id=1, source_target_pairs={{0,6},{1,7},{2,0},{3,1},{4,2},{5,3},{6,4},{7,5},{8,14},{9,15},{10,... | collective-permute-start | bytes 1572872 | tf_op jit(solution)/shard_map/ppermute | solution.py:37
  363.7 27.9 %collective-permute-start.59 = (bf16[128,2048]{1,0:T(8,128)(2,1)}, bf16[128,2048]{1,0:T(8,128)(2,1)S(1)}, u32[]{:S(2)}, u32[]{:S(2)}) collective-permute-start(bf16[128,2048]{1,0:T(8,128)(2,1)} %get-tuple-element.77), channel_id=1, source_target_pairs={{0,2},{1,3},{2,4},{3,5},{4,6},{5,7},{6,0},{7,1},{8,10},{9,11},{10,... | collective-permute-start | bytes 1572872 | tf_op jit(solution)/shard_map/ppermute | solution.py:33
  382.2 172.6 %reduce-scatter.11.cloned.1.call-start = ((), (), s32[]{:S(2)}) async-start(), calls=%async_computation.7 | async-start | bytes 1310720 | tf_op jit(solution)/shard_map/reduce_scatter | solution.py:105
  393.0 22.4 %collective-permute-start.62 = (bf16[64,4096]{1,0:T(8,128)(2,1)S(1)}, bf16[64,4096]{1,0:T(8,128)(2,1)S(1)}, u32[]{:S(2)}, u32[]{:S(2)}) collective-permute-start(bf16[64,4096]{1,0:T(8,128)(2,1)S(1)} %fusion.7), channel_id=1, source_target_pairs={{0,8},{1,9},{2,10},{3,11},{4,12},{5,13},{6,14},{7,15},{8,16},{9,17... | collective-permute-start | bytes 1572872 | tf_op jit(solution)/shard_map/ppermute | solution.py:25
  394.0 31.0 %collective-permute-start.63 = (bf16[64,4096]{1,0:T(8,128)(2,1)}, bf16[64,4096]{1,0:T(8,128)(2,1)S(1)}, u32[]{:S(2)}, u32[]{:S(2)}) collective-permute-start(bf16[64,4096]{1,0:T(8,128)(2,1)} %fusion.21), channel_id=1, source_target_pairs={{0,9},{1,8},{2,11},{3,10},{4,13},{5,12},{6,15},{7,14},{8,17},{9,16... | collective-permute-start | bytes 1572872 | tf_op jit(solution)/shard_map/ppermute | solution.py:25
  429.6 15.6 %collective-permute-start.66 = (bf16[64,4096]{1,0:T(8,128)(2,1)S(1)}, bf16[64,4096]{1,0:T(8,128)(2,1)S(1)}, u32[]{:S(2)}, u32[]{:S(2)}) collective-permute-start(bf16[64,4096]{1,0:T(8,128)(2,1)S(1)} %fusion.10), channel_id=1, source_target_pairs={{0,1},{1,0},{2,3},{3,2},{4,5},{5,4},{6,7},{7,6},{8,9},{9,8},{10,11... | collective-permute-start | bytes 1572872 | tf_op jit(solution)/shard_map/ppermute | solution.py:29
  445.2 29.2 %collective-permute-start.77 = (bf16[256,2048]{1,0:T(8,128)(2,1)S(1)}, bf16[256,2048]{1,0:T(8,128)(2,1)S(1)}, u32[]{:S(2)}, u32[]{:S(2)}) collective-permute-start(bf16[256,2048]{1,0:T(8,128)(2,1)S(1)} %maximum_maximum_fusion.3.refs_8_), channel_id=1, source_target_pairs={{0,1},{1,0},{2,3},{3,2},{4,5},{5,4},{6,7},{7,6},{8,9},{9,8},{10,11... | collective-permute-start | bytes 3145736 | tf_op jit(solution)/shard_map/ppermute | solution.py:29
  447.1 16.1 %collective-permute-start.67 = (bf16[128,2048]{1,0:T(8,128)(2,1)S(1)}, bf16[128,2048]{1,0:T(8,128)(2,1)}, u32[]{:S(2)}, u32[]{:S(2)}) collective-permute-start(bf16[128,2048]{1,0:T(8,128)(2,1)S(1)} %pad_maximum_fusion.10.refs_0_), channel_id=1, source_target_pairs={{0,2},{1,3},{2,4},{3,5},{4,6},{5,7},{6,0},{7,1},{8,10},{9,11},{10,... | collective-permute-start | bytes 1572872 | tf_op jit(solution)/shard_map/ppermute | solution.py:33
  447.5 26.9 %collective-permute-start.68 = (bf16[128,2048]{1,0:T(8,128)(2,1)S(1)}, bf16[128,2048]{1,0:T(8,128)(2,1)}, u32[]{:S(2)}, u32[]{:S(2)}) collective-permute-start(bf16[128,2048]{1,0:T(8,128)(2,1)S(1)} %pad_maximum_fusion.11.refs_1_), channel_id=1, source_target_pairs={{0,2},{1,3},{2,4},{3,5},{4,6},{5,7},{6,0},{7,1},{8,10},{9,11},{10,... | collective-permute-start | bytes 1572872 | tf_op jit(solution)/shard_map/ppermute | solution.py:33
  447.6 26.8 %collective-permute-start.69 = (bf16[128,2048]{1,0:T(8,128)(2,1)S(1)}, bf16[128,2048]{1,0:T(8,128)(2,1)}, u32[]{:S(2)}, u32[]{:S(2)}) collective-permute-start(bf16[128,2048]{1,0:T(8,128)(2,1)S(1)} %pad_maximum_fusion.10.refs_0_), channel_id=1, source_target_pairs={{0,6},{1,7},{2,0},{3,1},{4,2},{5,3},{6,4},{7,5},{8,14},{9,15},{10,... | collective-permute-start | bytes 1572872 | tf_op jit(solution)/shard_map/ppermute | solution.py:37
  460.2 21.9 %collective-permute-start.72 = (bf16[128,2048]{1,0:T(8,128)(2,1)}, bf16[128,2048]{1,0:T(8,128)(2,1)}, u32[]{:S(2)}, u32[]{:S(2)}) collective-permute-start(bf16[128,2048]{1,0:T(8,128)(2,1)} %collective-permute-done.70.refs_5_), channel_id=1, source_target_pairs={{0,6},{1,7},{2,0},{3,1},{4,2},{5,3},{6,4},{7,5},{8,14},{9,15},{10,... | collective-permute-start | bytes 1572872 | tf_op jit(solution)/shard_map/ppermute | solution.py:37
  463.2 21.9 %collective-permute-start.71 = (bf16[128,2048]{1,0:T(8,128)(2,1)}, bf16[128,2048]{1,0:T(8,128)(2,1)}, u32[]{:S(2)}, u32[]{:S(2)}) collective-permute-start(bf16[128,2048]{1,0:T(8,128)(2,1)} %collective-permute-done.67.refs_2_), channel_id=1, source_target_pairs={{0,2},{1,3},{2,4},{3,5},{4,6},{5,7},{6,0},{7,1},{8,10},{9,11},{10,... | collective-permute-start | bytes 1572872 | tf_op jit(solution)/shard_map/ppermute | solution.py:33
  505.8 16.1 %collective-permute-start.79 = (bf16[128,2048]{1,0:T(8,128)(2,1)S(1)}, bf16[128,2048]{1,0:T(8,128)(2,1)S(1)}, u32[]{:S(2)}, u32[]{:S(2)}) collective-permute-start(bf16[128,2048]{1,0:T(8,128)(2,1)S(1)} %get-tuple-element.86), channel_id=1, source_target_pairs={{0,2},{1,3},{2,4},{3,5},{4,6},{5,7},{6,0},{7,1},{8,10},{9,11},{10,... | collective-permute-start | bytes 1572872 | tf_op jit(solution)/shard_map/ppermute | solution.py:33
  505.9 26.2 %collective-permute-start.86 = (bf16[4,64,2048]{2,1,0:T(8,128)(2,1)S(1)}, bf16[4,64,2048]{2,1,0:T(8,128)(2,1)S(1)}, u32[]{:S(2)}, u32[]{:S(2)}) collective-permute-start(bf16[4,64,2048]{2,1,0:T(8,128)(2,1)S(1)} %get-tuple-element.92), channel_id=1, source_target_pairs={{0,1},{1,0},{2,3},{3,2},{4,5},{5,4},{6,7},{7,6},{8,9},{9,8},{10,11... | collective-permute-start | bytes 3145736 | tf_op jit(solution)/shard_map/ppermute | solution.py:29
  507.7 15.5 %collective-permute-start.82 = (bf16[128,2048]{1,0:T(8,128)(2,1)S(1)}, bf16[128,2048]{1,0:T(8,128)(2,1)S(1)}, u32[]{:S(2)}, u32[]{:S(2)}) collective-permute-start(bf16[128,2048]{1,0:T(8,128)(2,1)S(1)} %get-tuple-element.90), channel_id=1, source_target_pairs={{0,6},{1,7},{2,0},{3,1},{4,2},{5,3},{6,4},{7,5},{8,14},{9,15},{10,... | collective-permute-start | bytes 1572872 | tf_op jit(solution)/shard_map/ppermute | solution.py:37
  510.8 23.7 %collective-permute-start.78 = (bf16[128,2048]{1,0:T(8,128)(2,1)}, bf16[128,2048]{1,0:T(8,128)(2,1)S(1)}, u32[]{:S(2)}, u32[]{:S(2)}) collective-permute-start(bf16[128,2048]{1,0:T(8,128)(2,1)} %get-tuple-element.84), channel_id=1, source_target_pairs={{0,6},{1,7},{2,0},{3,1},{4,2},{5,3},{6,4},{7,5},{8,14},{9,15},{10,... | collective-permute-start | bytes 1572872 | tf_op jit(solution)/shard_map/ppermute | solution.py:37
  510.8 33.3 %collective-permute-start.81 = (bf16[128,2048]{1,0:T(8,128)(2,1)}, bf16[128,2048]{1,0:T(8,128)(2,1)S(1)}, u32[]{:S(2)}, u32[]{:S(2)}) collective-permute-start(bf16[128,2048]{1,0:T(8,128)(2,1)} %get-tuple-element.88), channel_id=1, source_target_pairs={{0,2},{1,3},{2,4},{3,5},{4,6},{5,7},{6,0},{7,1},{8,10},{9,11},{10,... | collective-permute-start | bytes 1572872 | tf_op jit(solution)/shard_map/ppermute | solution.py:33
  522.9 21.0 %collective-permute-start.80 = (bf16[128,2048]{1,0:T(8,128)(2,1)}, bf16[128,2048]{1,0:T(8,128)(2,1)S(1)}, u32[]{:S(2)}, u32[]{:S(2)}) collective-permute-start(bf16[128,2048]{1,0:T(8,128)(2,1)} %add_convert_fusion.6), channel_id=1, source_target_pairs={{0,2},{1,3},{2,4},{3,5},{4,6},{5,7},{6,0},{7,1},{8,10},{9,11},{10,... | collective-permute-start | bytes 1572872 | tf_op jit(solution)/shard_map/ppermute | solution.py:33
  524.1 22.4 %collective-permute-start.83 = (bf16[128,2048]{1,0:T(8,128)(2,1)}, bf16[128,2048]{1,0:T(8,128)(2,1)S(1)}, u32[]{:S(2)}, u32[]{:S(2)}) collective-permute-start(bf16[128,2048]{1,0:T(8,128)(2,1)} %add_convert_fusion.5), channel_id=1, source_target_pairs={{0,6},{1,7},{2,0},{3,1},{4,2},{5,3},{6,4},{7,5},{8,14},{9,15},{10,... | collective-permute-start | bytes 1572872 | tf_op jit(solution)/shard_map/ppermute | solution.py:37
  548.0 18.6 %collective-permute-start.85 = (bf16[64,4096]{1,0:T(8,128)(2,1)S(1)}, bf16[64,4096]{1,0:T(8,128)(2,1)S(1)}, u32[]{:S(2)}, u32[]{:S(2)}) collective-permute-start(bf16[64,4096]{1,0:T(8,128)(2,1)S(1)} %fusion.20), channel_id=1, source_target_pairs={{0,9},{1,8},{2,11},{3,10},{4,13},{5,12},{6,15},{7,14},{8,17},{9,16... | collective-permute-start | bytes 1572872 | tf_op jit(solution)/shard_map/ppermute | solution.py:25
  (59 other events, 545.0 us)
Sparse Core Ops, SparseCore 0:
  116.0 24.3 reduce-scatter.4
  246.8 30.2 reduce-scatter.6
  382.4 31.9 reduce-scatter.8
  533.6 21.2 reduce-scatter.10

commit v3 on v2

--- a/solution.py
+++ b/solution.py
@@ -8,12 +8,11 @@
 from jax.sharding import PartitionSpec as P
 
 TICKS = 4
-FIRST = 4096
+FIRST = 3584
 DEEP = 1024
-WIDE = 2048
+WIDE = 1024
 SLOTS = 4
-RINGS = [[0, 2, 4, 6], [1, 3, 5, 7]]
-LIMIT = 38
+LIMIT = 40
 
 
 def relayed(value, turn):
@@ -101,28 +100,23 @@
 
 
 def scatter_second(second, near, far):
-    both = plus(near, across(far)).astype(jnp.bfloat16)
-    total = lax.psum_scatter(both, "expert", scatter_dimension=0, axis_index_groups=RINGS)
-    return relayed(plus(second, total).astype(jnp.bfloat16), 0)
-
-
-def accumulate(acc, rows, gate_ref, up_ref, first):
-    inner = gate_ref.shape[1]
-    for at, ref in ((0, gate_ref), (inner, up_ref)):
-        columns = slice(at, at + inner)
-        part = jnp.dot(rows, ref[...], preferred_element_type=jnp.float32)
-        acc[:, columns] = part if first else acc[:, columns] + part
-
-
-def mlp_kernel(turns, weight, gate_hbm, up_hbm, down_hbm, *refs):
+    rows = second.shape[0]
+    both = plus(near, across(far))
+    kept = relayed((second.astype(jnp.float32) + both[:rows]).astype(jnp.bfloat16), 0)
+    parts = [both[i * rows : (i + 1) * rows].astype(jnp.bfloat16) for i in (1, 2, 3)]
+    sent = [relayed(part, turn) for part, turn in zip(parts, (-2, 2, 4))]
+    return plus(kept, *sent).astype(jnp.bfloat16)
+
+
+def mlp_kernel(weight, gate_hbm, up_hbm, down_hbm, *refs):
     pieces, (near, far) = refs[:8], refs[8:10]
     outs, (out_near, out_far) = refs[10:18], refs[18:20]
-    gates, ups, downs, acc, hidden, in_sems, out_sems = refs[20:]
+    block, gates, ups, downs, acc, hidden, in_sems, out_sems, row_sems, put_sems = refs[20:]
     pair, half = pieces[0].shape
     rows = pair // 2
-    inner = hidden.shape[1]
-    steps = gate_hbm.shape[0] // DEEP
-    wides = down_hbm.shape[1] // WIDE
+    width, inner = gate_hbm.shape
+    split = 2 * half
+    steps, wides = width // DEEP, width // WIDE
 
     def fetch(at):
         slot, span = at % SLOTS, pl.ds(at * DEEP, DEEP)
@@ -134,66 +128,91 @@
     def fetch_down(at):
         return pltpu.make_async_copy(down_hbm.at[:, pl.ds(at * WIDE, WIDE)], downs.at[at], out_sems.at[at])
 
-    def start(at):
+    def spots(firsts, seconds):
+        for side in range(2):
+            for dy in range(4):
+                at = block.at[pl.ds(dy * pair, pair), pl.ds(side * half, half)]
+                yield firsts[2 * dy + side], at, (side + 1) * half
+        for dx, ref in enumerate(seconds):
+            for dy in range(4):
+                at = block.at[pl.ds((2 * dy + dx) * rows, rows), pl.ds(split, width - split)]
+                yield ref.at[pl.ds(dy * rows, rows), pl.ds(0, width - split)], at, width
+
+    arrivals = [
+        (pltpu.make_async_copy(ref, at, row_sems.at[i]), end)
+        for i, (ref, at, end) in enumerate(spots(pieces, (near, far)))
+    ]
+    departures = [
+        (pltpu.make_async_copy(at, ref, put_sems.at[i]), end)
+        for i, (ref, at, end) in enumerate(spots(outs, (out_near, out_far)))
+    ]
+    ends = (half, split, width)
+
+    def within(start, stop):
+        return [end for begin, end in zip((0, *ends), ends) if begin < stop and end > start]
+
+    for copy, end in arrivals:
+        if end == half:
+            copy.start()
+    for copy in fetch(0):
+        copy.start()
+    for copy, end in arrivals:
+        if end > half:
+            copy.start()
+    for at in range(1, SLOTS):
         for copy in fetch(at):
             copy.start()
-
-    def wait(at):
+    here = set()
+    for at in range(steps):
+        for end in within(at * DEEP, (at + 1) * DEEP):
+            if end not in here:
+                here.add(end)
+                for copy, of in arrivals:
+                    if of == end:
+                        copy.wait()
         for copy in fetch(at):
             copy.wait()
-
-    def block(at):
-        start = at * DEEP
-        if start < 2 * half:
-            side, columns = start // half, pl.ds(start % half, DEEP)
-            return jnp.concatenate([pieces[2 * dy + side][:, columns] for dy in range(4)], axis=0)
-        columns = pl.ds(start - 2 * half, DEEP)
-        parts = [ref[dy * rows : (dy + 1) * rows, columns] for dy in range(4) for ref in (near, far)]
-        return jnp.concatenate(parts, axis=0)
-
-    for at in range(SLOTS):
-        start(at)
-    for at in range(steps):
-        wait(at)
-        accumulate(acc, block(at), gates.at[at % SLOTS], ups.at[at % SLOTS], at == 0)
+        lines = block[:, at * DEEP : (at + 1) * DEEP]
+        for column, ref in ((0, gates), (inner, ups)):
+            columns = slice(column, column + inner)
+            part = jnp.dot(lines, ref[at % SLOTS], preferred_element_type=jnp.float32)
+            acc[:, columns] = part if at == 0 else acc[:, columns] + part
         if at + SLOTS < steps:
-            start(at + SLOTS)
+            for copy in fetch(at + SLOTS):
+                copy.start()
         elif at + SLOTS == steps:
             for wide in range(wides):
                 fetch_down(wide).start()
-    scale = weight[...]
     value = acc[:, :inner]
-    hidden[...] = (value / (1.0 + jnp.exp(-value)) * acc[:, inner:] * scale).astype(jnp.bfloat16)
+    hidden[...] = (value / (1.0 + jnp.exp(-value)) * acc[:, inner:] * weight[...]).astype(jnp.bfloat16)
+    done = 0
     for at in range(wides):
         fetch_down(at).wait()
-        for part in range(0, WIDE, 512):
-            down = downs[at, :, part : part + 512]
-            output = jnp.dot(hidden[...], down, preferred_element_type=jnp.float32).astype(jnp.bfloat16)
-            start_at = at * WIDE + part
-            if start_at < 2 * half:
-                side, columns = start_at // half, pl.ds(start_at % half, 512)
-                for dy in range(4):
-                    outs[2 * dy + side][:, columns] = output[dy * pair : (dy + 1) * pair, :]
-            else:
-                columns = pl.ds(start_at - 2 * half, 512)
-                for dy in range(4):
-                    out_near[turns[dy], :, columns] = output[2 * dy * rows : (2 * dy + 1) * rows, :]
-                    out_far[turns[dy], :, columns] = output[(2 * dy + 1) * rows : (2 * dy + 2) * rows, :]
-
-
-def expert(turns, weight, gate_w, up_w, down_w, pieces, near, far):
+        output = jnp.dot(hidden[...], downs[at], preferred_element_type=jnp.float32)
+        block[:, at * WIDE : (at + 1) * WIDE] = output.astype(jnp.bfloat16)
+        for copy, end in departures:
+            if done < end <= (at + 1) * WIDE:
+                copy.start()
+        done = (at + 1) * WIDE
+    for copy, _ in departures:
+        copy.wait()
+
+
+def expert(weight, gate_w, up_w, down_w, pieces, near, far):
     width, inner = gate_w.shape
-    total = pieces[0].shape[0] * 4
+    pair, half = pieces[0].shape
+    total = pair * 4
     wides = width // WIDE
-    mixed = (4, total // 8, width - 2 * pieces[0].shape[1])
-    whole = pl.BlockSpec(memory_space=pltpu.VMEM)
+    mixed = (2 * pair, width - 2 * half)
+    anywhere = pl.BlockSpec(memory_space=pl.ANY)
     outs = pl.pallas_call(
         mlp_kernel,
-        in_specs=[pl.BlockSpec(memory_space=pltpu.SMEM), whole] + [pl.BlockSpec(memory_space=pltpu.HBM)] * 3 + [whole] * 10,
-        out_specs=[whole] * 10,
-        out_shape=[jax.ShapeDtypeStruct(p.shape, jnp.bfloat16) for p in pieces]
+        in_specs=[pl.BlockSpec(memory_space=pltpu.VMEM)] + [anywhere] * 13,
+        out_specs=[anywhere] * 10,
+        out_shape=[jax.ShapeDtypeStruct((pair, half), jnp.bfloat16)] * 8
         + [jax.ShapeDtypeStruct(mixed, jnp.bfloat16)] * 2,
         scratch_shapes=[
+            pltpu.VMEM((total, width), jnp.bfloat16),
             pltpu.VMEM((SLOTS, DEEP, inner), jnp.bfloat16),
             pltpu.VMEM((SLOTS, DEEP, inner), jnp.bfloat16),
             pltpu.VMEM((wides, inner, WIDE), jnp.bfloat16),
@@ -201,6 +220,8 @@
             pltpu.VMEM((total, inner), jnp.bfloat16),
             pltpu.SemaphoreType.DMA((2, SLOTS)),
             pltpu.SemaphoreType.DMA((wides,)),
+            pltpu.SemaphoreType.DMA((16,)),
+            pltpu.SemaphoreType.DMA((16,)),
         ],
         compiler_params=pltpu.CompilerParams(vmem_limit_bytes=LIMIT * 1024 * 1024),
         cost_estimate=pl.CostEstimate(
@@ -209,7 +230,7 @@
             transcendentals=total * inner,
         ),
         name="expert_mlp",
-    )(turns, weight, gate_w, up_w, down_w, *pieces, near, far)
+    )(weight, gate_w, up_w, down_w, *pieces, near, far)
     return outs[:8], outs[8], outs[9]
 
 
@@ -218,7 +239,6 @@
     gate_w, up_w, down_w = w_gate[0, 0], w_up[0, 0], w_down[0, 0]
     rows, width = acts.shape[1:]
     me = lax.axis_index("expert")
-    turns = jnp.stack([(me // 2 + dy) % 4 for dy in (0, 3, 1, 2)]).astype(jnp.int32)
     ids = jnp.arange(8, dtype=jnp.int32)
     chosen = (routes[:, 0, :, :, None] == ids).astype(jnp.float32)
     weights = jnp.sum(gates[:, 0, :, :, None] * chosen, axis=2)
@@ -235,7 +255,7 @@
         else:
             pieces, near, far = gather(one, two)
         weight = jnp.sum(jnp.where(columns == tick * 8 + me, weights, 0.0), axis=1, keepdims=True)
-        pieces, near, far = expert(turns, weight, gate_w, up_w, down_w, pieces, near, far)
+        pieces, near, far = expert(weight, gate_w, up_w, down_w, pieces, near, far)
         first, second = scatter_first(first, pieces), scatter_second(second, near, far)
     return jnp.concatenate([first, second], axis=1)[None]
 

time: 584 us -> 563 us (0.964)
  starting transfers between devices: 148 us -> 192 us
  other arithmetic: 37.9 us -> 14.5 us
  waiting for transfers between devices: 284 us -> 268 us
  between operations: 14.7 us -> 1.24 us
  local copies, waits for them, and re-layouts: 12.4 us -> 4.55 us
    ppermute x32, waiting for transfers between devices: 150 us -> 96 us  [upward(): return lax.ppermute(value, 'expert', [(i, (i + 2) % 8) for i in range(8)])]
    ppermute x12 -> x24, waiting for transfers between devices: 36 us -> 79.2 us  [relayed(): return lax.ppermute(value, ('section', 'expert'), pairs)]
    ppermute x12 -> x24, starting transfers between devices: 30 us -> 63.2 us  [relayed(): return lax.ppermute(value, ('section', 'expert'), pairs)]
    reduce_scatter x4 -> x0, waiting for transfers between devices: 25.9 us -> none  [scatter_second(): lax.psum_scatter(both, 'expert', scatter_dimension=0, axis_index_groups=R...]
    ppermute x32, waiting for transfers between devices: 55.6 us -> 74.5 us  [downward(): return lax.ppermute(value, 'expert', [(i, (i - 2) % 8) for i in range(8)])]
    convert_element_type x8 -> x5, other arithmetic: 9.53 us -> 0.45 us  [the longest x4 0.29 us: scatter_second(): (second.astype(jnp.float32) + both[:rows]).astype(jnp.bfloat16)]
    unnamed x62 -> x42, local copies, waits for them, and re-layouts: 9.68 us -> 1.55 us
  transfers between devices with their start and end apart: 92 -> 100, of which waited for: 61 -> 62; matrix products, arithmetic and copies ran while one was open for 6% -> 2% of each run, Pallas kernels for 0% -> 0%
where the time goes in v3:
time: 563 us; the launch traced here: 558 us
  waiting for transfers between devices  268 us (48%)
  starting transfers between devices  192 us (34%)
  Pallas kernels  77.8 us (14%)
  other arithmetic  14.5 us (3%)
    ppermute x32, waiting for transfers between devices, upward(): return lax.ppermute(value, 'expert', [(i, (i + 2) % 8) for i in range(8)])  96 us
    ppermute x32, starting transfers between devices, downward(): return lax.ppermute(value, 'expert', [(i, (i - 2) % 8) for i in range(8)])  92.5 us
    ppermute x24, waiting for transfers between devices, relayed(): return lax.ppermute(value, ('section', 'expert'), pairs)  79.2 us
    pallas_call x4, Pallas kernels, expert(): pl.pallas_call(mlp_kernel, in_specs=[pl.BlockSpec(memory_space=pltpu.VMEM...  77.8 us
    ppermute x32, waiting for transfers between devices, downward(): return lax.ppermute(value, 'expert', [(i, (i - 2) % 8) for i in range(8)])  74.5 us
    ppermute x24, starting transfers between devices, relayed(): return lax.ppermute(value, ('section', 'expert'), pairs)  63.2 us
    ppermute x12, starting transfers between devices, across(): return lax.ppermute(value, 'expert', [(i, i ^ 1) for i in range(8)])  22.4 us
    ppermute x12, waiting for transfers between devices, across(): return lax.ppermute(value, 'expert', [(i, i ^ 1) for i in range(8)])  18.6 us
  transfers between devices with their start and end apart: 100, of which 62 were waited for; matrix products, arithmetic and copies ran while one was open for 2% of the time, Pallas kernels for 0%

profile of v3, /device:TPU:2, one launch (start us, length us, event | category | flops | bytes accessed | tf_op | source)
XLA Modules:
  0.0 558.4 jit_solution(340233250890064519)
XLA Ops:
  10.9 4.9 collective-permute-done.1
  15.8 3.8 collective-permute-start.3
  19.7 6.5 %collective-permute-done.2 = bf16[64,1280]{1,0:T(8,128)(2,1)S(1)} collective-permute-done((bf16[64,1280]{1,0:T(8,128)(2,1)S(1)}, bf16[64,1280]{1,0:T(8,128)(2,1)S(1)}, u32[]{:S(2)}, u32[]{:S(2)}) %collective-permute-start.2) | collective-permute-done | bytes 163872 | tf_op jit(solution)/shard_map/ppermute | solution.py:32
  28.7 3.3 collective-permute-start.9
  32.0 3.2 collective-permute-start.8
  35.2 8.1 %collective-permute-done.6.refs_2_ = bf16[128,1792]{1,0:T(8,128)(2,1)S(1)} collective-permute-done((bf16[128,1792]{1,0:T(8,128)(2,1)S(1)}, bf16[128,1792]{1,0:T(8,128)(2,1)S(1)}, u32[]{:S(2)}, u32[]{:S(2)}) %collective-permute-start.6) | collective-permute-done | bytes 458784 | tf_op jit(solution)/shard_map/ppermute | solution.py:32
  43.3 3.8 collective-permute-start.11
  47.2 10.4 %collective-permute-done.5.refs_9_ = bf16[256,2688]{1,0:T(8,128)(2,1)} collective-permute-done((bf16[256,2688]{1,0:T(8,128)(2,1)S(1)}, bf16[256,2688]{1,0:T(8,128)(2,1)}, u32[]{:S(2)}, u32[]{:S(2)}) %collective-permute-start.5) | collective-permute-done | bytes 1376288 | tf_op jit(solution)/shard_map/ppermute | solution.py:28
  59.3 19.5 %expert_mlp.4 = (bf16[128,1792]{1,0:T(8,128)(2,1)S(1)}, bf16[128,1792]{1,0:T(8,128)(2,1)S(1)}, bf16[128,1792]{1,0:T(8,128)(2,1)S(1)}, bf16[128,1792]{1,0:T(8,128...) custom-call(f32[512,1]{1,0:T(8,128)S(1)} %copy.33.weight, ...), custom_call_target="tpu_custom_call" | custom-call | flops 12079595520 | bytes 23592960 | tf_op jit(solution)/shard_map/expert_mlp/pallas_call | solution.py:208
  86.2 7.3 %collective-permute-done.13 = bf16[128,1792]{1,0:T(8,128)(2,1)S(1)} collective-permute-done((bf16[128,1792]{1,0:T(8,128)(2,1)S(1)}, bf16[128,1792]{1,0:T(8,128)(2,1)S(1)}, u32[]{:S(2)}, u32[]{:S(2)}) %collective-permute-start.13) | collective-permute-done | bytes 458784 | tf_op jit(solution)/shard_map/ppermute | solution.py:32
  93.7 7.4 %collective-permute-done.16 = bf16[128,1792]{1,0:T(8,128)(2,1)S(1)} collective-permute-done((bf16[128,1792]{1,0:T(8,128)(2,1)S(1)}, bf16[128,1792]{1,0:T(8,128)(2,1)S(1)}, u32[]{:S(2)}, u32[]{:S(2)}) %collective-permute-start.16) | collective-permute-done | bytes 458784 | tf_op jit(solution)/shard_map/ppermute | solution.py:36
  101.2 3.3 collective-permute-start.17
  104.6 4.0 collective-permute-done.14
  110.9 3.3 collective-permute-start.19
  121.2 4.3 collective-permute-done.18
  125.6 5.6 %collective-permute-start.21 = (bf16[64,2560]{1,0:T(8,128)(2,1)S(1)}, bf16[64,2560]{1,0:T(8,128)(2,1)S(1)}, u32[]{:S(2)}, u32[]{:S(2)}) collective-permute-start(bf16[64,2560]{1,0:T(8,128)(2,1)S(1)} %fusion.39), channel_id=1, source_target_pairs={{0,8},{1,9},{2,10},{3,11},{4,12},{5,13},{6,14},{7,15},{8,16},{9,17... | collective-permute-start | bytes 983048 | tf_op jit(solution)/shard_map/ppermute | solution.py:24
  131.5 6.1 %collective-permute-done.23 = bf16[64,2560]{1,0:T(8,128)(2,1)S(1)} collective-permute-done((bf16[64,2560]{1,0:T(8,128)(2,1)S(1)}, bf16[64,2560]{1,0:T(8,128)(2,1)S(1)}, u32[]{:S(2)}, u32[]{:S(2)}) %collective-permute-start.23) | collective-permute-done | bytes 327712 | tf_op jit(solution)/shard_map/ppermute | solution.py:24
  137.6 3.9 collective-permute-done.24
  161.0 3.4 collective-permute-start.29
  164.6 3.2 collective-permute-start.28
  167.8 7.6 %collective-permute-done.29.refs_5_ = bf16[128,1792]{1,0:T(8,128)(2,1)S(1)} collective-permute-done((bf16[128,1792]{1,0:T(8,128)(2,1)S(1)}, bf16[128,1792]{1,0:T(8,128)(2,1)S(1)}, u32[]{:S(2)}, u32[]{:S(2)}) %collective-permute-start.29) | collective-permute-done | bytes 458784 | tf_op jit(solution)/shard_map/ppermute | solution.py:36
  175.4 3.7 collective-permute-start.31
  179.5 8.4 %collective-permute-done.27.refs_3_ = bf16[128,1792]{1,0:T(8,128)(2,1)} collective-permute-done((bf16[128,1792]{1,0:T(8,128)(2,1)S(1)}, bf16[128,1792]{1,0:T(8,128)(2,1)}, u32[]{:S(2)}, u32[]{:S(2)}) %collective-permute-start.27) | collective-permute-done | bytes 458784 | tf_op jit(solution)/shard_map/ppermute | solution.py:32
  189.2 3.6 collective-permute-done.30.refs_6_
  192.8 19.5 %expert_mlp.5 = (bf16[128,1792]{1,0:T(8,128)(2,1)S(1)}, bf16[128,1792]{1,0:T(8,128)(2,1)S(1)}, bf16[128,1792]{1,0:T(8,128)(2,1)S(1)}, bf16[128,1792]{1,0:T(8,128...) custom-call(f32[512,1]{1,0:T(8,128)S(1)} %copy.34.weight, ...), custom_call_target="tpu_custom_call" | custom-call | flops 12079595520 | bytes 23592960 | tf_op jit(solution)/shard_map/expert_mlp/pallas_call | solution.py:208
  219.3 7.8 %collective-permute-done.38 = bf16[128,1792]{1,0:T(8,128)(2,1)S(1)} collective-permute-done((bf16[128,1792]{1,0:T(8,128)(2,1)S(1)}, bf16[128,1792]{1,0:T(8,128)(2,1)S(1)}, u32[]{:S(2)}, u32[]{:S(2)}) %collective-permute-start.38) | collective-permute-done | bytes 458784 | tf_op jit(solution)/shard_map/ppermute | solution.py:32
  227.6 6.7 %collective-permute-done.41 = bf16[128,1792]{1,0:T(8,128)(2,1)S(1)} collective-permute-done((bf16[128,1792]{1,0:T(8,128)(2,1)S(1)}, bf16[128,1792]{1,0:T(8,128)(2,1)S(1)}, u32[]{:S(2)}, u32[]{:S(2)}) %collective-permute-start.41) | collective-permute-done | bytes 458784 | tf_op jit(solution)/shard_map/ppermute | solution.py:36
  234.4 3.3 collective-permute-start.42
  239.8 3.9 collective-permute-done.42
  244.2 5.7 %collective-permute-start.44 = (bf16[64,3584]{1,0:T(8,128)(2,1)S(1)}, bf16[64,3584]{1,0:T(8,128)(2,1)S(1)}, u32[]{:S(2)}, u32[]{:S(2)}) collective-permute-start(bf16[64,3584]{1,0:T(8,128)(2,1)S(1)} %fusion.22), channel_id=1, source_target_pairs={{0,9},{1,8},{2,11},{3,10},{4,13},{5,12},{6,15},{7,14},{8,17},{9,16... | collective-permute-start | bytes 1376264 | tf_op jit(solution)/shard_map/ppermute | solution.py:24
  251.1 4.7 collective-permute-start.47
  258.5 8.8 %collective-permute-start.49 = (bf16[64,2560]{1,0:T(8,128)(2,1)S(1)}, bf16[64,2560]{1,0:T(8,128)(2,1)S(1)}, u32[]{:S(2)}, u32[]{:S(2)}) collective-permute-start(bf16[64,2560]{1,0:T(8,128)(2,1)S(1)} %get-tuple-element.118), channel_id=1, source_target_pairs={{0,12},{1,13},{2,14},{3,15},{4,8},{5,9},{6,10},{7,11},{8,20},{9,21... | collective-permute-start | bytes 983048 | tf_op jit(solution)/shard_map/ppermute | solution.py:24
  267.6 9.0 %collective-permute-done.48 = bf16[64,2560]{1,0:T(8,128)(2,1)S(1)} collective-permute-done((bf16[64,2560]{1,0:T(8,128)(2,1)S(1)}, bf16[64,2560]{1,0:T(8,128)(2,1)S(1)}, u32[]{:S(2)}, u32[]{:S(2)}) %collective-permute-start.48) | collective-permute-done | bytes 327712 | tf_op jit(solution)/shard_map/ppermute | solution.py:24
  283.9 3.8 collective-permute-done.57
  296.3 3.4 collective-permute-start.54
  303.1 7.6 %collective-permute-done.54.refs_5_ = bf16[128,1792]{1,0:T(8,128)(2,1)S(1)} collective-permute-done((bf16[128,1792]{1,0:T(8,128)(2,1)S(1)}, bf16[128,1792]{1,0:T(8,128)(2,1)S(1)}, u32[]{:S(2)}, u32[]{:S(2)}) %collective-permute-start.54) | collective-permute-done | bytes 458784 | tf_op jit(solution)/shard_map/ppermute | solution.py:36
  310.7 3.7 collective-permute-start.56
  314.8 9.6 %collective-permute-done.52.refs_3_ = bf16[128,1792]{1,0:T(8,128)(2,1)} collective-permute-done((bf16[128,1792]{1,0:T(8,128)(2,1)S(1)}, bf16[128,1792]{1,0:T(8,128)(2,1)}, u32[]{:S(2)}, u32[]{:S(2)}) %collective-permute-start.52) | collective-permute-done | bytes 458784 | tf_op jit(solution)/shard_map/ppermute | solution.py:32
  326.4 3.6 collective-permute-done.55.refs_6_
  330.0 19.5 %expert_mlp.6 = (bf16[128,1792]{1,0:T(8,128)(2,1)S(1)}, bf16[128,1792]{1,0:T(8,128)(2,1)S(1)}, bf16[128,1792]{1,0:T(8,128)(2,1)S(1)}, bf16[128,1792]{1,0:T(8,128...) custom-call(f32[512,1]{1,0:T(8,128)S(1)} %copy.35.weight, ...), custom_call_target="tpu_custom_call" | custom-call | flops 12079595520 | bytes 23592960 | tf_op jit(solution)/shard_map/expert_mlp/pallas_call | solution.py:208
  356.7 7.5 %collective-permute-done.63 = bf16[128,1792]{1,0:T(8,128)(2,1)S(1)} collective-permute-done((bf16[128,1792]{1,0:T(8,128)(2,1)S(1)}, bf16[128,1792]{1,0:T(8,128)(2,1)S(1)}, u32[]{:S(2)}, u32[]{:S(2)}) %collective-permute-start.63) | collective-permute-done | bytes 458784 | tf_op jit(solution)/shard_map/ppermute | solution.py:32
  364.6 6.7 %collective-permute-done.66 = bf16[128,1792]{1,0:T(8,128)(2,1)S(1)} collective-permute-done((bf16[128,1792]{1,0:T(8,128)(2,1)S(1)}, bf16[128,1792]{1,0:T(8,128)(2,1)S(1)}, u32[]{:S(2)}, u32[]{:S(2)}) %collective-permute-start.66) | collective-permute-done | bytes 458784 | tf_op jit(solution)/shard_map/ppermute | solution.py:36
  371.4 3.8 collective-permute-start.67
  375.2 3.4 collective-permute-done.64
  388.2 9.3 %collective-permute-done.68 = bf16[64,3584]{1,0:T(8,128)(2,1)S(1)} collective-permute-done((bf16[64,3584]{1,0:T(8,128)(2,1)S(1)}, bf16[64,3584]{1,0:T(8,128)(2,1)S(1)}, u32[]{:S(2)}, u32[]{:S(2)}) %collective-permute-start.68) | collective-permute-done | bytes 458784 | tf_op jit(solution)/shard_map/ppermute | solution.py:24
  397.4 3.5 collective-permute-start.74
  406.4 8.0 %collective-permute-done.73 = bf16[64,2560]{1,0:T(8,128)(2,1)S(1)} collective-permute-done((bf16[64,2560]{1,0:T(8,128)(2,1)S(1)}, bf16[64,2560]{1,0:T(8,128)(2,1)S(1)}, u32[]{:S(2)}, u32[]{:S(2)}) %collective-permute-start.73) | collective-permute-done | bytes 327712 | tf_op jit(solution)/shard_map/ppermute | solution.py:24
  423.1 4.0 collective-permute-done.82
  427.3 3.3 collective-permute-start.85
  437.1 3.8 collective-permute-start.79
  444.2 6.4 %collective-permute-done.79.refs_5_ = bf16[128,1792]{1,0:T(8,128)(2,1)S(1)} collective-permute-done((bf16[128,1792]{1,0:T(8,128)(2,1)S(1)}, bf16[128,1792]{1,0:T(8,128)(2,1)S(1)}, u32[]{:S(2)}, u32[]{:S(2)}) %collective-permute-start.79) | collective-permute-done | bytes 458784 | tf_op jit(solution)/shard_map/ppermute | solution.py:36
  450.7 3.7 collective-permute-start.81
  454.9 3.6 collective-permute-done.77.refs_3_
  460.5 4.0 collective-permute-done.80.refs_6_
  464.5 19.5 %expert_mlp.7 = (bf16[128,1792]{1,0:T(8,128)(2,1)S(1)}, bf16[128,1792]{1,0:T(8,128)(2,1)S(1)}, bf16[128,1792]{1,0:T(8,128)(2,1)S(1)}, bf16[128,1792]{1,0:T(8,128...) custom-call(f32[512,1]{1,0:T(8,128)S(1)} %copy.36.weight, ...), custom_call_target="tpu_custom_call" | custom-call | flops 12079595520 | bytes 23592960 | tf_op jit(solution)/shard_map/expert_mlp/pallas_call | solution.py:208
  484.1 3.2 collective-permute-start.87
  494.8 7.6 %collective-permute-done.91 = bf16[128,1792]{1,0:T(8,128)(2,1)S(1)} collective-permute-done((bf16[128,1792]{1,0:T(8,128)(2,1)S(1)}, bf16[128,1792]{1,0:T(8,128)(2,1)S(1)}, u32[]{:S(2)}, u32[]{:S(2)}) %collective-permute-start.91) | collective-permute-done | bytes 458784 | tf_op jit(solution)/shard_map/ppermute | solution.py:36
  502.5 3.8 collective-permute-start.92
  506.5 5.8 %collective-permute-done.92 = bf16[128,1792]{1,0:T(8,128)(2,1)S(1)} collective-permute-done((bf16[128,1792]{1,0:T(8,128)(2,1)S(1)}, bf16[128,1792]{1,0:T(8,128)(2,1)S(1)}, u32[]{:S(2)}, u32[]{:S(2)}) %collective-permute-start.92) | collective-permute-done | bytes 458784 | tf_op jit(solution)/shard_map/ppermute | solution.py:36
  512.7 11.3 %collective-permute-start.94 = (bf16[64,3584]{1,0:T(8,128)(2,1)S(1)}, bf16[64,3584]{1,0:T(8,128)(2,1)S(1)}, u32[]{:S(2)}, u32[]{:S(2)}) collective-permute-start(bf16[64,3584]{1,0:T(8,128)(2,1)S(1)} %fusion.20), channel_id=1, source_target_pairs={{0,9},{1,8},{2,11},{3,10},{4,13},{5,12},{6,15},{7,14},{8,17},{9,16... | collective-permute-start | bytes 1376264 | tf_op jit(solution)/shard_map/ppermute | solution.py:24
  525.2 8.0 %collective-permute-start.97 = (bf16[64,2560]{1,0:T(8,128)(2,1)S(1)}, bf16[64,2560]{1,0:T(8,128)(2,1)S(1)}, u32[]{:S(2)}, u32[]{:S(2)}) collective-permute-start(bf16[64,2560]{1,0:T(8,128)(2,1)S(1)} %get-tuple-element.111), channel_id=1, source_target_pairs={{0,14},{1,15},{2,8},{3,9},{4,10},{5,11},{6,12},{7,13},{8,22},{9,23... | collective-permute-start | bytes 983048 | tf_op jit(solution)/shard_map/ppermute | solution.py:24
  537.5 5.7 %collective-permute-done.96 = bf16[64,2560]{1,0:T(8,128)(2,1)S(1)} collective-permute-done((bf16[64,2560]{1,0:T(8,128)(2,1)S(1)}, bf16[64,2560]{1,0:T(8,128)(2,1)S(1)}, u32[]{:S(2)}, u32[]{:S(2)}) %collective-permute-start.96) | collective-permute-done | bytes 327712 | tf_op jit(solution)/shard_map/ppermute | solution.py:24
  543.1 4.3 collective-permute-done.97
  547.4 6.5 %collective-permute-done.98 = bf16[64,2560]{1,0:T(8,128)(2,1)S(1)} collective-permute-done((bf16[64,2560]{1,0:T(8,128)(2,1)S(1)}, bf16[64,2560]{1,0:T(8,128)(2,1)S(1)}, u32[]{:S(2)}, u32[]{:S(2)}) %collective-permute-start.98) | collective-permute-done | bytes 327712 | tf_op jit(solution)/shard_map/ppermute | solution.py:24
  (288 shorter events, 151.3 us)
Async XLA Ops:
  8.7 17.6 %collective-permute-start.4 = (bf16[64,3584]{1,0:T(8,128)(2,1)S(1)}, bf16[64,3584]{1,0:T(8,128)(2,1)S(1)}, u32[]{:S(2)}, u32[]{:S(2)}) collective-permute-start(bf16[64,3584]{1,0:T(8,128)(2,1)S(1)} %fusion.14), channel_id=1, source_target_pairs={{0,1},{1,0},{2,3},{3,2},{4,5},{5,4},{6,7},{7,6},{8,9},{9,8},{10,11... | collective-permute-start | bytes 1376264 | tf_op jit(solution)/shard_map/ppermute | solution.py:28
  26.3 31.3 %collective-permute-start.5 = (bf16[256,2688]{1,0:T(8,128)(2,1)S(1)}, bf16[256,2688]{1,0:T(8,128)(2,1)}, u32[]{:S(2)}, u32[]{:S(2)}) collective-permute-start(bf16[256,2688]{1,0:T(8,128)(2,1)S(1)} %maximum_maximum_fusion.refs_8_), channel_id=1, source_target_pairs={{0,1},{1,0},{2,3},{3,2},{4,5},{5,4},{6,7},{7,6},{8,9},{9,8},{10,11... | collective-permute-start | bytes 4128776 | tf_op jit(solution)/shard_map/ppermute | solution.py:28
  28.6 14.7 %collective-permute-start.6 = (bf16[128,1792]{1,0:T(8,128)(2,1)S(1)}, bf16[128,1792]{1,0:T(8,128)(2,1)S(1)}, u32[]{:S(2)}, u32[]{:S(2)}) collective-permute-start(bf16[128,1792]{1,0:T(8,128)(2,1)S(1)} %pad_maximum_fusion.4.refs_0_), channel_id=1, source_target_pairs={{0,2},{1,3},{2,4},{3,5},{4,6},{5,7},{6,0},{7,1},{8,10},{9,11},{10,... | collective-permute-start | bytes 1376264 | tf_op jit(solution)/shard_map/ppermute | solution.py:32
  28.7 14.6 %collective-permute-start.9 = (bf16[128,1792]{1,0:T(8,128)(2,1)S(1)}, bf16[128,1792]{1,0:T(8,128)(2,1)S(1)}, u32[]{:S(2)}, u32[]{:S(2)}) collective-permute-start(bf16[128,1792]{1,0:T(8,128)(2,1)S(1)} %pad_maximum_fusion.5.refs_1_), channel_id=1, source_target_pairs={{0,6},{1,7},{2,0},{3,1},{4,2},{5,3},{6,4},{7,5},{8,14},{9,15},{10,... | collective-permute-start | bytes 1376264 | tf_op jit(solution)/shard_map/ppermute | solution.py:36
  32.0 27.1 %collective-permute-start.7 = (bf16[128,1792]{1,0:T(8,128)(2,1)S(1)}, bf16[128,1792]{1,0:T(8,128)(2,1)}, u32[]{:S(2)}, u32[]{:S(2)}) collective-permute-start(bf16[128,1792]{1,0:T(8,128)(2,1)S(1)} %pad_maximum_fusion.5.refs_1_), channel_id=1, source_target_pairs={{0,2},{1,3},{2,4},{3,5},{4,6},{5,7},{6,0},{7,1},{8,10},{9,11},{10,... | collective-permute-start | bytes 1376264 | tf_op jit(solution)/shard_map/ppermute | solution.py:32
  32.0 27.1 %collective-permute-start.8 = (bf16[128,1792]{1,0:T(8,128)(2,1)S(1)}, bf16[128,1792]{1,0:T(8,128)(2,1)}, u32[]{:S(2)}, u32[]{:S(2)}) collective-permute-start(bf16[128,1792]{1,0:T(8,128)(2,1)S(1)} %pad_maximum_fusion.4.refs_0_), channel_id=1, source_target_pairs={{0,6},{1,7},{2,0},{3,1},{4,2},{5,3},{6,4},{7,5},{8,14},{9,15},{10,... | collective-permute-start | bytes 1376264 | tf_op jit(solution)/shard_map/ppermute | solution.py:36
  43.3 16.0 %collective-permute-start.10 = (bf16[128,1792]{1,0:T(8,128)(2,1)S(1)}, bf16[128,1792]{1,0:T(8,128)(2,1)}, u32[]{:S(2)}, u32[]{:S(2)}) collective-permute-start(bf16[128,1792]{1,0:T(8,128)(2,1)S(1)} %collective-permute-done.6.refs_2_), channel_id=1, source_target_pairs={{0,2},{1,3},{2,4},{3,5},{4,6},{5,7},{6,0},{7,1},{8,10},{9,11},{10,... | collective-permute-start | bytes 1376264 | tf_op jit(solution)/shard_map/ppermute | solution.py:32
  43.3 16.0 %collective-permute-start.11 = (bf16[128,1792]{1,0:T(8,128)(2,1)S(1)}, bf16[128,1792]{1,0:T(8,128)(2,1)}, u32[]{:S(2)}, u32[]{:S(2)}) collective-permute-start(bf16[128,1792]{1,0:T(8,128)(2,1)S(1)} %collective-permute-done.9.refs_5_), channel_id=1, source_target_pairs={{0,6},{1,7},{2,0},{3,1},{4,2},{5,3},{6,4},{7,5},{8,14},{9,15},{10,... | collective-permute-start | bytes 1376264 | tf_op jit(solution)/shard_map/ppermute | solution.py:36
  78.8 14.7 %collective-permute-start.13 = (bf16[128,1792]{1,0:T(8,128)(2,1)S(1)}, bf16[128,1792]{1,0:T(8,128)(2,1)S(1)}, u32[]{:S(2)}, u32[]{:S(2)}) collective-permute-start(bf16[128,1792]{1,0:T(8,128)(2,1)S(1)} %get-tuple-element.53), channel_id=1, source_target_pairs={{0,2},{1,3},{2,4},{3,5},{4,6},{5,7},{6,0},{7,1},{8,10},{9,11},{10,... | collective-permute-start | bytes 1376264 | tf_op jit(solution)/shard_map/ppermute | solution.py:32
  78.9 35.3 %collective-permute-start.20 = (bf16[256,2560]{1,0:T(8,128)(2,1)S(1)}, bf16[256,2560]{1,0:T(8,128)(2,1)S(1)}, u32[]{:S(2)}, u32[]{:S(2)}) collective-permute-start(bf16[256,2560]{1,0:T(8,128)(2,1)S(1)} %get-tuple-element.59), channel_id=1, source_target_pairs={{0,1},{1,0},{2,3},{3,2},{4,5},{5,4},{6,7},{7,6},{8,9},{9,8},{10,11... | collective-permute-start | bytes 3932168 | tf_op jit(solution)/shard_map/ppermute | solution.py:28
  80.9 23.7 %collective-permute-start.12 = (bf16[128,1792]{1,0:T(8,128)(2,1)S(1)}, bf16[128,1792]{1,0:T(8,128)(2,1)S(1)}, u32[]{:S(2)}, u32[]{:S(2)}) collective-permute-start(bf16[128,1792]{1,0:T(8,128)(2,1)S(1)} %get-tuple-element.51), channel_id=1, source_target_pairs={{0,6},{1,7},{2,0},{3,1},{4,2},{5,3},{6,4},{7,5},{8,14},{9,15},{10,... | collective-permute-start | bytes 1376264 | tf_op jit(solution)/shard_map/ppermute | solution.py:36
  84.0 17.1 %collective-permute-start.16 = (bf16[128,1792]{1,0:T(8,128)(2,1)S(1)}, bf16[128,1792]{1,0:T(8,128)(2,1)S(1)}, u32[]{:S(2)}, u32[]{:S(2)}) collective-permute-start(bf16[128,1792]{1,0:T(8,128)(2,1)S(1)} %get-tuple-element.57), channel_id=1, source_target_pairs={{0,6},{1,7},{2,0},{3,1},{4,2},{5,3},{6,4},{7,5},{8,14},{9,15},{10,... | collective-permute-start | bytes 1376264 | tf_op jit(solution)/shard_map/ppermute | solution.py:36
  85.3 23.4 %collective-permute-start.15 = (bf16[128,1792]{1,0:T(8,128)(2,1)S(1)}, bf16[128,1792]{1,0:T(8,128)(2,1)S(1)}, u32[]{:S(2)}, u32[]{:S(2)}) collective-permute-start(bf16[128,1792]{1,0:T(8,128)(2,1)S(1)} %get-tuple-element.55), channel_id=1, source_target_pairs={{0,2},{1,3},{2,4},{3,5},{4,6},{5,7},{6,0},{7,1},{8,10},{9,11},{10,... | collective-permute-start | bytes 1376264 | tf_op jit(solution)/shard_map/ppermute | solution.py:32
  93.6 15.0 %collective-permute-start.14 = (bf16[128,1792]{1,0:T(8,128)(2,1)S(1)}, bf16[128,1792]{1,0:T(8,128)(2,1)S(1)}, u32[]{:S(2)}, u32[]{:S(2)}) collective-permute-start(bf16[128,1792]{1,0:T(8,128)(2,1)S(1)} %add_convert_fusion.11), channel_id=1, source_target_pairs={{0,2},{1,3},{2,4},{3,5},{4,6},{5,7},{6,0},{7,1},{8,10},{9,11},{10,... | collective-permute-start | bytes 1376264 | tf_op jit(solution)/shard_map/ppermute | solution.py:32
  110.8 14.8 %collective-permute-start.18 = (bf16[64,3584]{1,0:T(8,128)(2,1)S(1)}, bf16[64,3584]{1,0:T(8,128)(2,1)S(1)}, u32[]{:S(2)}, u32[]{:S(2)}) collective-permute-start(bf16[64,3584]{1,0:T(8,128)(2,1)S(1)} %fusion.15), channel_id=1, source_target_pairs={{0,8},{1,9},{2,10},{3,11},{4,12},{5,13},{6,14},{7,15},{8,16},{9,17... | collective-permute-start | bytes 1376264 | tf_op jit(solution)/shard_map/ppermute | solution.py:24
  110.9 20.2 %collective-permute-start.19 = (bf16[64,3584]{1,0:T(8,128)(2,1)S(1)}, bf16[64,3584]{1,0:T(8,128)(2,1)S(1)}, u32[]{:S(2)}, u32[]{:S(2)}) collective-permute-start(bf16[64,3584]{1,0:T(8,128)(2,1)S(1)} %fusion.23), channel_id=1, source_target_pairs={{0,9},{1,8},{2,11},{3,10},{4,13},{5,12},{6,15},{7,14},{8,17},{9,16... | collective-permute-start | bytes 1376264 | tf_op jit(solution)/shard_map/ppermute | solution.py:24
  114.8 16.7 %collective-permute-start.22 = (bf16[64,2560]{1,0:T(8,128)(2,1)S(1)}, bf16[64,2560]{1,0:T(8,128)(2,1)S(1)}, u32[]{:S(2)}, u32[]{:S(2)}) collective-permute-start(bf16[64,2560]{1,0:T(8,128)(2,1)S(1)} %get-tuple-element.120), channel_id=1, source_target_pairs={{0,14},{1,15},{2,8},{3,9},{4,10},{5,11},{6,12},{7,13},{8,22},{9,23... | collective-permute-start | bytes 983048 | tf_op jit(solution)/shard_map/ppermute | solution.py:24
  118.0 19.6 %collective-permute-start.23 = (bf16[64,2560]{1,0:T(8,128)(2,1)S(1)}, bf16[64,2560]{1,0:T(8,128)(2,1)S(1)}, u32[]{:S(2)}, u32[]{:S(2)}) collective-permute-start(bf16[64,2560]{1,0:T(8,128)(2,1)S(1)} %get-tuple-element.122), channel_id=1, source_target_pairs={{0,10},{1,11},{2,12},{3,13},{4,14},{5,15},{6,8},{7,9},{8,18},{9,19... | collective-permute-start | bytes 983048 | tf_op jit(solution)/shard_map/ppermute | solution.py:24
  118.0 23.5 %collective-permute-start.24 = (bf16[64,2560]{1,0:T(8,128)(2,1)S(1)}, bf16[64,2560]{1,0:T(8,128)(2,1)S(1)}, u32[]{:S(2)}, u32[]{:S(2)}) collective-permute-start(bf16[64,2560]{1,0:T(8,128)(2,1)S(1)} %get-tuple-element.121), channel_id=1, source_target_pairs={{0,12},{1,13},{2,14},{3,15},{4,8},{5,9},{6,10},{7,11},{8,20},{9,21... | collective-permute-start | bytes 983048 | tf_op jit(solution)/shard_map/ppermute | solution.py:24
  125.6 18.2 %collective-permute-start.21 = (bf16[64,2560]{1,0:T(8,128)(2,1)S(1)}, bf16[64,2560]{1,0:T(8,128)(2,1)S(1)}, u32[]{:S(2)}, u32[]{:S(2)}) collective-permute-start(bf16[64,2560]{1,0:T(8,128)(2,1)S(1)} %fusion.39), channel_id=1, source_target_pairs={{0,8},{1,9},{2,10},{3,11},{4,12},{5,13},{6,14},{7,15},{8,16},{9,17... | collective-permute-start | bytes 983048 | tf_op jit(solution)/shard_map/ppermute | solution.py:24
  159.3 33.5 %collective-permute-start.36 = (bf16[256,2560]{1,0:T(8,128)(2,1)S(1)}, bf16[256,2560]{1,0:T(8,128)(2,1)}, u32[]{:S(2)}, u32[]{:S(2)}) collective-permute-start(bf16[256,2560]{1,0:T(8,128)(2,1)S(1)} %maximum_maximum_fusion.1.refs_8_), channel_id=1, source_target_pairs={{0,1},{1,0},{2,3},{3,2},{4,5},{5,4},{6,7},{7,6},{8,9},{9,8},{10,11... | collective-permute-start | bytes 3932168 | tf_op jit(solution)/shard_map/ppermute | solution.py:28
  164.4 14.7 %collective-permute-start.26 = (bf16[128,1792]{1,0:T(8,128)(2,1)S(1)}, bf16[128,1792]{1,0:T(8,128)(2,1)S(1)}, u32[]{:S(2)}, u32[]{:S(2)}) collective-permute-start(bf16[128,1792]{1,0:T(8,128)(2,1)S(1)} %pad_maximum_fusion.6.refs_0_), channel_id=1, source_target_pairs={{0,2},{1,3},{2,4},{3,5},{4,6},{5,7},{6,0},{7,1},{8,10},{9,11},{10,... | collective-permute-start | bytes 1376264 | tf_op jit(solution)/shard_map/ppermute | solution.py:32
  164.5 23.4 %collective-permute-start.27 = (bf16[128,1792]{1,0:T(8,128)(2,1)S(1)}, bf16[128,1792]{1,0:T(8,128)(2,1)}, u32[]{:S(2)}, u32[]{:S(2)}) collective-permute-start(bf16[128,1792]{1,0:T(8,128)(2,1)S(1)} %pad_maximum_fusion.7.refs_1_), channel_id=1, source_target_pairs={{0,2},{1,3},{2,4},{3,5},{4,6},{5,7},{6,0},{7,1},{8,10},{9,11},{10,... | collective-permute-start | bytes 1376264 | tf_op jit(solution)/shard_map/ppermute | solution.py:32
  164.6 23.3 %collective-permute-start.28 = (bf16[128,1792]{1,0:T(8,128)(2,1)S(1)}, bf16[128,1792]{1,0:T(8,128)(2,1)}, u32[]{:S(2)}, u32[]{:S(2)}) collective-permute-start(bf16[128,1792]{1,0:T(8,128)(2,1)S(1)} %pad_maximum_fusion.6.refs_0_), channel_id=1, source_target_pairs={{0,6},{1,7},{2,0},{3,1},{4,2},{5,3},{6,4},{7,5},{8,14},{9,15},{10,... | collective-permute-start | bytes 1376264 | tf_op jit(solution)/shard_map/ppermute | solution.py:36
  212.3 14.7 %collective-permute-start.38 = (bf16[128,1792]{1,0:T(8,128)(2,1)S(1)}, bf16[128,1792]{1,0:T(8,128)(2,1)S(1)}, u32[]{:S(2)}, u32[]{:S(2)}) collective-permute-start(bf16[128,1792]{1,0:T(8,128)(2,1)S(1)} %get-tuple-element.64), channel_id=1, source_target_pairs={{0,2},{1,3},{2,4},{3,5},{4,6},{5,7},{6,0},{7,1},{8,10},{9,11},{10,... | collective-permute-start | bytes 1376264 | tf_op jit(solution)/shard_map/ppermute | solution.py:32
  212.4 37.6 %collective-permute-start.45 = (bf16[256,2560]{1,0:T(8,128)(2,1)S(1)}, bf16[256,2560]{1,0:T(8,128)(2,1)S(1)}, u32[]{:S(2)}, u32[]{:S(2)}) collective-permute-start(bf16[256,2560]{1,0:T(8,128)(2,1)S(1)} %get-tuple-element.70), channel_id=1, source_target_pairs={{0,1},{1,0},{2,3},{3,2},{4,5},{5,4},{6,7},{7,6},{8,9},{9,8},{10,11... | collective-permute-start | bytes 3932168 | tf_op jit(solution)/shard_map/ppermute | solution.py:28
  214.1 23.7 %collective-permute-start.37 = (bf16[128,1792]{1,0:T(8,128)(2,1)S(1)}, bf16[128,1792]{1,0:T(8,128)(2,1)S(1)}, u32[]{:S(2)}, u32[]{:S(2)}) collective-permute-start(bf16[128,1792]{1,0:T(8,128)(2,1)S(1)} %get-tuple-element.62), channel_id=1, source_target_pairs={{0,6},{1,7},{2,0},{3,1},{4,2},{5,3},{6,4},{7,5},{8,14},{9,15},{10,... | collective-permute-start | bytes 1376264 | tf_op jit(solution)/shard_map/ppermute | solution.py:36
  217.2 17.1 %collective-permute-start.41 = (bf16[128,1792]{1,0:T(8,128)(2,1)S(1)}, bf16[128,1792]{1,0:T(8,128)(2,1)S(1)}, u32[]{:S(2)}, u32[]{:S(2)}) collective-permute-start(bf16[128,1792]{1,0:T(8,128)(2,1)S(1)} %get-tuple-element.68), channel_id=1, source_target_pairs={{0,6},{1,7},{2,0},{3,1},{4,2},{5,3},{6,4},{7,5},{8,14},{9,15},{10,... | collective-permute-start | bytes 1376264 | tf_op jit(solution)/shard_map/ppermute | solution.py:36
  217.3 22.5 %collective-permute-start.40 = (bf16[128,1792]{1,0:T(8,128)(2,1)S(1)}, bf16[128,1792]{1,0:T(8,128)(2,1)S(1)}, u32[]{:S(2)}, u32[]{:S(2)}) collective-permute-start(bf16[128,1792]{1,0:T(8,128)(2,1)S(1)} %get-tuple-element.66), channel_id=1, source_target_pairs={{0,2},{1,3},{2,4},{3,5},{4,6},{5,7},{6,0},{7,1},{8,10},{9,11},{10,... | collective-permute-start | bytes 1376264 | tf_op jit(solution)/shard_map/ppermute | solution.py:32
  244.2 23.1 %collective-permute-start.44 = (bf16[64,3584]{1,0:T(8,128)(2,1)S(1)}, bf16[64,3584]{1,0:T(8,128)(2,1)S(1)}, u32[]{:S(2)}, u32[]{:S(2)}) collective-permute-start(bf16[64,3584]{1,0:T(8,128)(2,1)S(1)} %fusion.22), channel_id=1, source_target_pairs={{0,9},{1,8},{2,11},{3,10},{4,13},{5,12},{6,15},{7,14},{8,17},{9,16... | collective-permute-start | bytes 1376264 | tf_op jit(solution)/shard_map/ppermute | solution.py:24
  251.0 16.6 %collective-permute-start.46 = (bf16[64,2560]{1,0:T(8,128)(2,1)S(1)}, bf16[64,2560]{1,0:T(8,128)(2,1)S(1)}, u32[]{:S(2)}, u32[]{:S(2)}) collective-permute-start(bf16[64,2560]{1,0:T(8,128)(2,1)S(1)} %fusion.27), channel_id=1, source_target_pairs={{0,8},{1,9},{2,10},{3,11},{4,12},{5,13},{6,14},{7,15},{8,16},{9,17... | collective-permute-start | bytes 983048 | tf_op jit(solution)/shard_map/ppermute | solution.py:24
  251.1 16.5 %collective-permute-start.47 = (bf16[64,2560]{1,0:T(8,128)(2,1)S(1)}, bf16[64,2560]{1,0:T(8,128)(2,1)S(1)}, u32[]{:S(2)}, u32[]{:S(2)}) collective-permute-start(bf16[64,2560]{1,0:T(8,128)(2,1)S(1)} %get-tuple-element.117), channel_id=1, source_target_pairs={{0,14},{1,15},{2,8},{3,9},{4,10},{5,11},{6,12},{7,13},{8,22},{9,23... | collective-permute-start | bytes 983048 | tf_op jit(solution)/shard_map/ppermute | solution.py:24
  255.9 20.8 %collective-permute-start.48 = (bf16[64,2560]{1,0:T(8,128)(2,1)S(1)}, bf16[64,2560]{1,0:T(8,128)(2,1)S(1)}, u32[]{:S(2)}, u32[]{:S(2)}) collective-permute-start(bf16[64,2560]{1,0:T(8,128)(2,1)S(1)} %get-tuple-element.119), channel_id=1, source_target_pairs={{0,10},{1,11},{2,12},{3,13},{4,14},{5,15},{6,8},{7,9},{8,18},{9,19... | collective-permute-start | bytes 983048 | tf_op jit(solution)/shard_map/ppermute | solution.py:24
  258.5 20.0 %collective-permute-start.49 = (bf16[64,2560]{1,0:T(8,128)(2,1)S(1)}, bf16[64,2560]{1,0:T(8,128)(2,1)S(1)}, u32[]{:S(2)}, u32[]{:S(2)}) collective-permute-start(bf16[64,2560]{1,0:T(8,128)(2,1)S(1)} %get-tuple-element.118), channel_id=1, source_target_pairs={{0,12},{1,13},{2,14},{3,15},{4,8},{5,9},{6,10},{7,11},{8,20},{9,21... | collective-permute-start | bytes 983048 | tf_op jit(solution)/shard_map/ppermute | solution.py:24
  294.5 35.5 %collective-permute-start.61 = (bf16[256,2560]{1,0:T(8,128)(2,1)S(1)}, bf16[256,2560]{1,0:T(8,128)(2,1)}, u32[]{:S(2)}, u32[]{:S(2)}) collective-permute-start(bf16[256,2560]{1,0:T(8,128)(2,1)S(1)} %maximum_maximum_fusion.2.refs_8_), channel_id=1, source_target_pairs={{0,1},{1,0},{2,3},{3,2},{4,5},{5,4},{6,7},{7,6},{8,9},{9,8},{10,11... | collective-permute-start | bytes 3932168 | tf_op jit(solution)/shard_map/ppermute | solution.py:28
  299.7 14.7 %collective-permute-start.51 = (bf16[128,1792]{1,0:T(8,128)(2,1)S(1)}, bf16[128,1792]{1,0:T(8,128)(2,1)S(1)}, u32[]{:S(2)}, u32[]{:S(2)}) collective-permute-start(bf16[128,1792]{1,0:T(8,128)(2,1)S(1)} %pad_maximum_fusion.8.refs_0_), channel_id=1, source_target_pairs={{0,2},{1,3},{2,4},{3,5},{4,6},{5,7},{6,0},{7,1},{8,10},{9,11},{10,... | collective-permute-start | bytes 1376264 | tf_op jit(solution)/shard_map/ppermute | solution.py:32
  299.8 24.6 %collective-permute-start.52 = (bf16[128,1792]{1,0:T(8,128)(2,1)S(1)}, bf16[128,1792]{1,0:T(8,128)(2,1)}, u32[]{:S(2)}, u32[]{:S(2)}) collective-permute-start(bf16[128,1792]{1,0:T(8,128)(2,1)S(1)} %pad_maximum_fusion.9.refs_1_), channel_id=1, source_target_pairs={{0,2},{1,3},{2,4},{3,5},{4,6},{5,7},{6,0},{7,1},{8,10},{9,11},{10,... | collective-permute-start | bytes 1376264 | tf_op jit(solution)/shard_map/ppermute | solution.py:32
  299.9 24.5 %collective-permute-start.53 = (bf16[128,1792]{1,0:T(8,128)(2,1)S(1)}, bf16[128,1792]{1,0:T(8,128)(2,1)}, u32[]{:S(2)}, u32[]{:S(2)}) collective-permute-start(bf16[128,1792]{1,0:T(8,128)(2,1)S(1)} %pad_maximum_fusion.8.refs_0_), channel_id=1, source_target_pairs={{0,6},{1,7},{2,0},{3,1},{4,2},{5,3},{6,4},{7,5},{8,14},{9,15},{10,... | collective-permute-start | bytes 1376264 | tf_op jit(solution)/shard_map/ppermute | solution.py:36
  310.7 15.7 %collective-permute-start.56 = (bf16[128,1792]{1,0:T(8,128)(2,1)S(1)}, bf16[128,1792]{1,0:T(8,128)(2,1)}, u32[]{:S(2)}, u32[]{:S(2)}) collective-permute-start(bf16[128,1792]{1,0:T(8,128)(2,1)S(1)} %collective-permute-done.54.refs_5_), channel_id=1, source_target_pairs={{0,6},{1,7},{2,0},{3,1},{4,2},{5,3},{6,4},{7,5},{8,14},{9,15},{10,... | collective-permute-start | bytes 1376264 | tf_op jit(solution)/shard_map/ppermute | solution.py:36
  314.5 15.5 %collective-permute-start.55 = (bf16[128,1792]{1,0:T(8,128)(2,1)S(1)}, bf16[128,1792]{1,0:T(8,128)(2,1)}, u32[]{:S(2)}, u32[]{:S(2)}) collective-permute-start(bf16[128,1792]{1,0:T(8,128)(2,1)S(1)} %collective-permute-done.51.refs_2_), channel_id=1, source_target_pairs={{0,2},{1,3},{2,4},{3,5},{4,6},{5,7},{6,0},{7,1},{8,10},{9,11},{10,... | collective-permute-start | bytes 1376264 | tf_op jit(solution)/shard_map/ppermute | solution.py:32
  349.4 14.7 %collective-permute-start.63 = (bf16[128,1792]{1,0:T(8,128)(2,1)S(1)}, bf16[128,1792]{1,0:T(8,128)(2,1)S(1)}, u32[]{:S(2)}, u32[]{:S(2)}) collective-permute-start(bf16[128,1792]{1,0:T(8,128)(2,1)S(1)} %get-tuple-element.75), channel_id=1, source_target_pairs={{0,2},{1,3},{2,4},{3,5},{4,6},{5,7},{6,0},{7,1},{8,10},{9,11},{10,... | collective-permute-start | bytes 1376264 | tf_op jit(solution)/shard_map/ppermute | solution.py:32
  349.5 34.2 %collective-permute-start.70 = (bf16[256,2560]{1,0:T(8,128)(2,1)S(1)}, bf16[256,2560]{1,0:T(8,128)(2,1)S(1)}, u32[]{:S(2)}, u32[]{:S(2)}) collective-permute-start(bf16[256,2560]{1,0:T(8,128)(2,1)S(1)} %get-tuple-element.81), channel_id=1, source_target_pairs={{0,1},{1,0},{2,3},{3,2},{4,5},{5,4},{6,7},{7,6},{8,9},{9,8},{10,11... | collective-permute-start | bytes 3932168 | tf_op jit(solution)/shard_map/ppermute | solution.py:28
  351.5 23.7 %collective-permute-start.62 = (bf16[128,1792]{1,0:T(8,128)(2,1)S(1)}, bf16[128,1792]{1,0:T(8,128)(2,1)S(1)}, u32[]{:S(2)}, u32[]{:S(2)}) collective-permute-start(bf16[128,1792]{1,0:T(8,128)(2,1)S(1)} %get-tuple-element.73), channel_id=1, source_target_pairs={{0,6},{1,7},{2,0},{3,1},{4,2},{5,3},{6,4},{7,5},{8,14},{9,15},{10,... | collective-permute-start | bytes 1376264 | tf_op jit(solution)/shard_map/ppermute | solution.py:36
  354.7 16.6 %collective-permute-start.66 = (bf16[128,1792]{1,0:T(8,128)(2,1)S(1)}, bf16[128,1792]{1,0:T(8,128)(2,1)S(1)}, u32[]{:S(2)}, u32[]{:S(2)}) collective-permute-start(bf16[128,1792]{1,0:T(8,128)(2,1)S(1)} %get-tuple-element.79), channel_id=1, source_target_pairs={{0,6},{1,7},{2,0},{3,1},{4,2},{5,3},{6,4},{7,5},{8,14},{9,15},{10,... | collective-permute-start | bytes 1376264 | tf_op jit(solution)/shard_map/ppermute | solution.py:36
  354.7 24.1 %collective-permute-start.65 = (bf16[128,1792]{1,0:T(8,128)(2,1)S(1)}, bf16[128,1792]{1,0:T(8,128)(2,1)S(1)}, u32[]{:S(2)}, u32[]{:S(2)}) collective-permute-start(bf16[128,1792]{1,0:T(8,128)(2,1)S(1)} %get-tuple-element.77), channel_id=1, source_target_pairs={{0,2},{1,3},{2,4},{3,5},{4,6},{5,7},{6,0},{7,1},{8,10},{9,11},{10,... | collective-permute-start | bytes 1376264 | tf_op jit(solution)/shard_map/ppermute | solution.py:32
  381.5 15.9 %collective-permute-start.68 = (bf16[64,3584]{1,0:T(8,128)(2,1)S(1)}, bf16[64,3584]{1,0:T(8,128)(2,1)S(1)}, u32[]{:S(2)}, u32[]{:S(2)}) collective-permute-start(bf16[64,3584]{1,0:T(8,128)(2,1)S(1)} %fusion.7), channel_id=1, source_target_pairs={{0,8},{1,9},{2,10},{3,11},{4,12},{5,13},{6,14},{7,15},{8,16},{9,17... | collective-permute-start | bytes 1376264 | tf_op jit(solution)/shard_map/ppermute | solution.py:24
  381.7 19.3 %collective-permute-start.69 = (bf16[64,3584]{1,0:T(8,128)(2,1)S(1)}, bf16[64,3584]{1,0:T(8,128)(2,1)S(1)}, u32[]{:S(2)}, u32[]{:S(2)}) collective-permute-start(bf16[64,3584]{1,0:T(8,128)(2,1)S(1)} %fusion.21), channel_id=1, source_target_pairs={{0,9},{1,8},{2,11},{3,10},{4,13},{5,12},{6,15},{7,14},{8,17},{9,16... | collective-permute-start | bytes 1376264 | tf_op jit(solution)/shard_map/ppermute | solution.py:24
  384.8 18.9 %collective-permute-start.71 = (bf16[64,2560]{1,0:T(8,128)(2,1)S(1)}, bf16[64,2560]{1,0:T(8,128)(2,1)S(1)}, u32[]{:S(2)}, u32[]{:S(2)}) collective-permute-start(bf16[64,2560]{1,0:T(8,128)(2,1)S(1)} %fusion.31), channel_id=1, source_target_pairs={{0,8},{1,9},{2,10},{3,11},{4,12},{5,13},{6,14},{7,15},{8,16},{9,17... | collective-permute-start | bytes 983048 | tf_op jit(solution)/shard_map/ppermute | solution.py:24
  385.0 21.5 %collective-permute-start.72 = (bf16[64,2560]{1,0:T(8,128)(2,1)S(1)}, bf16[64,2560]{1,0:T(8,128)(2,1)S(1)}, u32[]{:S(2)}, u32[]{:S(2)}) collective-permute-start(bf16[64,2560]{1,0:T(8,128)(2,1)S(1)} %get-tuple-element.114), channel_id=1, source_target_pairs={{0,14},{1,15},{2,8},{3,9},{4,10},{5,11},{6,12},{7,13},{8,22},{9,23... | collective-permute-start | bytes 983048 | tf_op jit(solution)/shard_map/ppermute | solution.py:24
  388.2 26.3 %collective-permute-start.73 = (bf16[64,2560]{1,0:T(8,128)(2,1)S(1)}, bf16[64,2560]{1,0:T(8,128)(2,1)S(1)}, u32[]{:S(2)}, u32[]{:S(2)}) collective-permute-start(bf16[64,2560]{1,0:T(8,128)(2,1)S(1)} %get-tuple-element.116), channel_id=1, source_target_pairs={{0,10},{1,11},{2,12},{3,13},{4,14},{5,15},{6,8},{7,9},{8,18},{9,19... | collective-permute-start | bytes 983048 | tf_op jit(solution)/shard_map/ppermute | solution.py:24
  397.4 19.9 %collective-permute-start.74 = (bf16[64,2560]{1,0:T(8,128)(2,1)S(1)}, bf16[64,2560]{1,0:T(8,128)(2,1)S(1)}, u32[]{:S(2)}, u32[]{:S(2)}) collective-permute-start(bf16[64,2560]{1,0:T(8,128)(2,1)S(1)} %get-tuple-element.115), channel_id=1, source_target_pairs={{0,12},{1,13},{2,14},{3,15},{4,8},{5,9},{6,10},{7,11},{8,20},{9,21... | collective-permute-start | bytes 983048 | tf_op jit(solution)/shard_map/ppermute | solution.py:24
  435.3 29.2 %collective-permute-start.86 = (bf16[256,2560]{1,0:T(8,128)(2,1)S(1)}, bf16[256,2560]{1,0:T(8,128)(2,1)}, u32[]{:S(2)}, u32[]{:S(2)}) collective-permute-start(bf16[256,2560]{1,0:T(8,128)(2,1)S(1)} %maximum_maximum_fusion.3.refs_8_), channel_id=1, source_target_pairs={{0,1},{1,0},{2,3},{3,2},{4,5},{5,4},{6,7},{7,6},{8,9},{9,8},{10,11... | collective-permute-start | bytes 3932168 | tf_op jit(solution)/shard_map/ppermute | solution.py:28
  440.9 17.5 %collective-permute-start.77 = (bf16[128,1792]{1,0:T(8,128)(2,1)S(1)}, bf16[128,1792]{1,0:T(8,128)(2,1)}, u32[]{:S(2)}, u32[]{:S(2)}) collective-permute-start(bf16[128,1792]{1,0:T(8,128)(2,1)S(1)} %pad_maximum_fusion.11.refs_1_), channel_id=1, source_target_pairs={{0,2},{1,3},{2,4},{3,5},{4,6},{5,7},{6,0},{7,1},{8,10},{9,11},{10,... | collective-permute-start | bytes 1376264 | tf_op jit(solution)/shard_map/ppermute | solution.py:32
  441.0 17.4 %collective-permute-start.78 = (bf16[128,1792]{1,0:T(8,128)(2,1)S(1)}, bf16[128,1792]{1,0:T(8,128)(2,1)}, u32[]{:S(2)}, u32[]{:S(2)}) collective-permute-start(bf16[128,1792]{1,0:T(8,128)(2,1)S(1)} %pad_maximum_fusion.10.refs_0_), channel_id=1, source_target_pairs={{0,6},{1,7},{2,0},{3,1},{4,2},{5,3},{6,4},{7,5},{8,14},{9,15},{10,... | collective-permute-start | bytes 1376264 | tf_op jit(solution)/shard_map/ppermute | solution.py:36
  484.1 22.2 %collective-permute-start.87 = (bf16[128,1792]{1,0:T(8,128)(2,1)S(1)}, bf16[128,1792]{1,0:T(8,128)(2,1)S(1)}, u32[]{:S(2)}, u32[]{:S(2)}) collective-permute-start(bf16[128,1792]{1,0:T(8,128)(2,1)S(1)} %get-tuple-element.84), channel_id=1, source_target_pairs={{0,6},{1,7},{2,0},{3,1},{4,2},{5,3},{6,4},{7,5},{8,14},{9,15},{10,... | collective-permute-start | bytes 1376264 | tf_op jit(solution)/shard_map/ppermute | solution.py:36
  487.3 15.1 %collective-permute-start.91 = (bf16[128,1792]{1,0:T(8,128)(2,1)S(1)}, bf16[128,1792]{1,0:T(8,128)(2,1)S(1)}, u32[]{:S(2)}, u32[]{:S(2)}) collective-permute-start(bf16[128,1792]{1,0:T(8,128)(2,1)S(1)} %get-tuple-element.90), channel_id=1, source_target_pairs={{0,6},{1,7},{2,0},{3,1},{4,2},{5,3},{6,4},{7,5},{8,14},{9,15},{10,... | collective-permute-start | bytes 1376264 | tf_op jit(solution)/shard_map/ppermute | solution.py:36
  487.3 19.1 %collective-permute-start.90 = (bf16[128,1792]{1,0:T(8,128)(2,1)S(1)}, bf16[128,1792]{1,0:T(8,128)(2,1)S(1)}, u32[]{:S(2)}, u32[]{:S(2)}) collective-permute-start(bf16[128,1792]{1,0:T(8,128)(2,1)S(1)} %get-tuple-element.88), channel_id=1, source_target_pairs={{0,2},{1,3},{2,4},{3,5},{4,6},{5,7},{6,0},{7,1},{8,10},{9,11},{10,... | collective-permute-start | bytes 1376264 | tf_op jit(solution)/shard_map/ppermute | solution.py:32
  489.3 34.6 %collective-permute-start.95 = (bf16[256,2560]{1,0:T(8,128)(2,1)S(1)}, bf16[256,2560]{1,0:T(8,128)(2,1)S(1)}, u32[]{:S(2)}, u32[]{:S(2)}) collective-permute-start(bf16[256,2560]{1,0:T(8,128)(2,1)S(1)} %get-tuple-element.92), channel_id=1, source_target_pairs={{0,1},{1,0},{2,3},{3,2},{4,5},{5,4},{6,7},{7,6},{8,9},{9,8},{10,11... | collective-permute-start | bytes 3932168 | tf_op jit(solution)/shard_map/ppermute | solution.py:28
  512.6 23.5 %collective-permute-start.93 = (bf16[64,3584]{1,0:T(8,128)(2,1)S(1)}, bf16[64,3584]{1,0:T(8,128)(2,1)S(1)}, u32[]{:S(2)}, u32[]{:S(2)}) collective-permute-start(bf16[64,3584]{1,0:T(8,128)(2,1)S(1)} %fusion.11), channel_id=1, source_target_pairs={{0,8},{1,9},{2,10},{3,11},{4,12},{5,13},{6,14},{7,15},{8,16},{9,17... | collective-permute-start | bytes 1376264 | tf_op jit(solution)/shard_map/ppermute | solution.py:24
  512.7 24.6 %collective-permute-start.94 = (bf16[64,3584]{1,0:T(8,128)(2,1)S(1)}, bf16[64,3584]{1,0:T(8,128)(2,1)S(1)}, u32[]{:S(2)}, u32[]{:S(2)}) collective-permute-start(bf16[64,3584]{1,0:T(8,128)(2,1)S(1)} %fusion.20), channel_id=1, source_target_pairs={{0,9},{1,8},{2,11},{3,10},{4,13},{5,12},{6,15},{7,14},{8,17},{9,16... | collective-permute-start | bytes 1376264 | tf_op jit(solution)/shard_map/ppermute | solution.py:24
  525.0 18.1 %collective-permute-start.96 = (bf16[64,2560]{1,0:T(8,128)(2,1)S(1)}, bf16[64,2560]{1,0:T(8,128)(2,1)S(1)}, u32[]{:S(2)}, u32[]{:S(2)}) collective-permute-start(bf16[64,2560]{1,0:T(8,128)(2,1)S(1)} %fusion.35), channel_id=1, source_target_pairs={{0,8},{1,9},{2,10},{3,11},{4,12},{5,13},{6,14},{7,15},{8,16},{9,17... | collective-permute-start | bytes 983048 | tf_op jit(solution)/shard_map/ppermute | solution.py:24
  525.2 22.3 %collective-permute-start.97 = (bf16[64,2560]{1,0:T(8,128)(2,1)S(1)}, bf16[64,2560]{1,0:T(8,128)(2,1)S(1)}, u32[]{:S(2)}, u32[]{:S(2)}) collective-permute-start(bf16[64,2560]{1,0:T(8,128)(2,1)S(1)} %get-tuple-element.111), channel_id=1, source_target_pairs={{0,14},{1,15},{2,8},{3,9},{4,10},{5,11},{6,12},{7,13},{8,22},{9,23... | collective-permute-start | bytes 983048 | tf_op jit(solution)/shard_map/ppermute | solution.py:24
  533.2 20.8 %collective-permute-start.98 = (bf16[64,2560]{1,0:T(8,128)(2,1)S(1)}, bf16[64,2560]{1,0:T(8,128)(2,1)S(1)}, u32[]{:S(2)}, u32[]{:S(2)}) collective-permute-start(bf16[64,2560]{1,0:T(8,128)(2,1)S(1)} %get-tuple-element.113), channel_id=1, source_target_pairs={{0,10},{1,11},{2,12},{3,13},{4,14},{5,15},{6,8},{7,9},{8,18},{9,19... | collective-permute-start | bytes 983048 | tf_op jit(solution)/shard_map/ppermute | solution.py:24
  536.1 21.0 %collective-permute-start.99 = (bf16[64,2560]{1,0:T(8,128)(2,1)S(1)}, bf16[64,2560]{1,0:T(8,128)(2,1)S(1)}, u32[]{:S(2)}, u32[]{:S(2)}) collective-permute-start(bf16[64,2560]{1,0:T(8,128)(2,1)S(1)} %get-tuple-element.112), channel_id=1, source_target_pairs={{0,12},{1,13},{2,14},{3,15},{4,8},{5,9},{6,10},{7,11},{8,20},{9,21... | collective-permute-start | bytes 983048 | tf_op jit(solution)/shard_map/ppermute | solution.py:24
  (57 other events, 585.5 us)

commit v4 on v3

--- a/solution.py
+++ b/solution.py
@@ -86,26 +86,23 @@
     return lax.optimization_barrier((value, *others))[0]
 
 
-def scatter_first(first, pieces):
+def scatter_sum(first, second, pieces, near, far):
     own_l, own_r, below_l, below_r, above_l, above_r, opp_l, opp_r = pieces
-    rows = first.shape[0]
+    rows, split = first.shape
+    other = across(far)
     arrived_l, arrived_r = upward(opp_l), downward(opp_r)
     sum_r, sum_l = upward(above_r), downward(below_l)
     top_l = upward(plus(above_l, arrived_l).astype(jnp.bfloat16))
     low_r = downward(plus(below_r, arrived_r).astype(jnp.bfloat16))
+    both = plus(near, other)
+    parts = [both[i * rows : (i + 1) * rows].astype(jnp.bfloat16) for i in (1, 2, 3)]
+    more = [relayed(part, turn) for part, turn in zip(parts, (-2, 2, 4))]
     sums = jnp.concatenate([plus(own_l, sum_l, top_l), plus(own_r, sum_r, low_r)], axis=1)
     sent = relayed(sums[rows:].astype(jnp.bfloat16), None)
-    kept = relayed((first.astype(jnp.float32) + sums[:rows]).astype(jnp.bfloat16), 0)
-    return plus(kept, sent).astype(jnp.bfloat16)
-
-
-def scatter_second(second, near, far):
-    rows = second.shape[0]
-    both = plus(near, across(far))
-    kept = relayed((second.astype(jnp.float32) + both[:rows]).astype(jnp.bfloat16), 0)
-    parts = [both[i * rows : (i + 1) * rows].astype(jnp.bfloat16) for i in (1, 2, 3)]
-    sent = [relayed(part, turn) for part, turn in zip(parts, (-2, 2, 4))]
-    return plus(kept, *sent).astype(jnp.bfloat16)
+    home = jnp.concatenate([first.astype(jnp.float32) + sums[:rows], second.astype(jnp.float32) + both[:rows]], axis=1)
+    kept = relayed(home.astype(jnp.bfloat16), 0)
+    first = plus(kept[:, :split], sent).astype(jnp.bfloat16)
+    return first, plus(kept[:, split:], *more).astype(jnp.bfloat16)
 
 
 def mlp_kernel(weight, gate_hbm, up_hbm, down_hbm, *refs):
@@ -256,7 +253,7 @@
             pieces, near, far = gather(one, two)
         weight = jnp.sum(jnp.where(columns == tick * 8 + me, weights, 0.0), axis=1, keepdims=True)
         pieces, near, far = expert(weight, gate_w, up_w, down_w, pieces, near, far)
-        first, second = scatter_first(first, pieces), scatter_second(second, near, far)
+        first, second = scatter_sum(first, second, pieces, near, far)
     return jnp.concatenate([first, second], axis=1)[None]
 
 

time: 563 us -> 550 us (0.977)
  starting transfers between devices: 192 us -> 162 us
  waiting for transfers between devices: 268 us -> 280 us
    ppermute x24 -> x20, starting transfers between devices: 63.2 us -> 32.3 us  [relayed(): return lax.ppermute(value, ('section', 'expert'), pairs)]
    ppermute x24 -> x20, waiting for transfers between devices: 79.2 us -> 94.8 us  [relayed(): return lax.ppermute(value, ('section', 'expert'), pairs)]
    ppermute x12, waiting for transfers between devices: 18.6 us -> 12.5 us  [across(): return lax.ppermute(value, 'expert', [(i, i ^ 1) for i in range(8)])]
    ppermute x32, starting transfers between devices: 92.5 us -> 98.4 us  [downward(): return lax.ppermute(value, 'expert', [(i, (i - 2) % 8) for i in range(8)])]
  transfers between devices with their start and end apart: 100 -> 96, of which waited for: 62 -> 63; matrix products, arithmetic and copies ran while one was open for 2% -> 2% of each run, Pallas kernels for 0% -> 0%
where the time goes in v4:
time: 550 us; the launch traced here: 543 us
  waiting for transfers between devices  280 us (51%)
  starting transfers between devices  162 us (29%)
  Pallas kernels  77.8 us (14%)
  other arithmetic  14.7 us (3%)
  local copies, waits for them, and re-layouts  7.72 us (1%)
    ppermute x32, waiting for transfers between devices, upward(): return lax.ppermute(value, 'expert', [(i, (i + 2) % 8) for i in range(8)])  101 us
    ppermute x32, starting transfers between devices, downward(): return lax.ppermute(value, 'expert', [(i, (i - 2) % 8) for i in range(8)])  98.4 us
    ppermute x20, waiting for transfers between devices, relayed(): return lax.ppermute(value, ('section', 'expert'), pairs)  94.8 us
    pallas_call x4, Pallas kernels, expert(): pl.pallas_call(mlp_kernel, in_specs=[pl.BlockSpec(memory_space=pltpu.VMEM...  77.8 us
    ppermute x32, waiting for transfers between devices, downward(): return lax.ppermute(value, 'expert', [(i, (i - 2) % 8) for i in range(8)])  71.5 us
    ppermute x20, starting transfers between devices, relayed(): return lax.ppermute(value, ('section', 'expert'), pairs)  32.3 us
    ppermute x12, starting transfers between devices, across(): return lax.ppermute(value, 'expert', [(i, i ^ 1) for i in range(8)])  22.3 us
    ppermute x12, waiting for transfers between devices, across(): return lax.ppermute(value, 'expert', [(i, i ^ 1) for i in range(8)])  12.5 us
  transfers between devices with their start and end apart: 96, of which 63 were waited for; matrix products, arithmetic and copies ran while one was open for 2% of the time, Pallas kernels for 0%

profile of v4, /device:TPU:2, one launch (start us, length us, event | category | flops | bytes accessed | tf_op | source)
XLA Modules:
  0.0 543.5 jit_solution(2469880662679407069)
XLA Ops:
  10.9 4.9 collective-permute-done.1
  15.8 3.8 collective-permute-start.3
  19.7 6.5 %collective-permute-done.2 = bf16[64,1280]{1,0:T(8,128)(2,1)S(1)} collective-permute-done((bf16[64,1280]{1,0:T(8,128)(2,1)S(1)}, bf16[64,1280]{1,0:T(8,128)(2,1)S(1)}, u32[]{:S(2)}, u32[]{:S(2)}) %collective-permute-start.2) | collective-permute-done | bytes 163872 | tf_op jit(solution)/shard_map/ppermute | solution.py:32
  28.7 3.3 collective-permute-start.9
  32.0 3.2 collective-permute-start.8
  35.2 8.1 %collective-permute-done.6.refs_2_ = bf16[128,1792]{1,0:T(8,128)(2,1)S(1)} collective-permute-done((bf16[128,1792]{1,0:T(8,128)(2,1)S(1)}, bf16[128,1792]{1,0:T(8,128)(2,1)S(1)}, u32[]{:S(2)}, u32[]{:S(2)}) %collective-permute-start.6) | collective-permute-done | bytes 458784 | tf_op jit(solution)/shard_map/ppermute | solution.py:32
  43.3 3.8 collective-permute-start.11
  47.2 10.4 %collective-permute-done.5.refs_9_ = bf16[256,2688]{1,0:T(8,128)(2,1)} collective-permute-done((bf16[256,2688]{1,0:T(8,128)(2,1)S(1)}, bf16[256,2688]{1,0:T(8,128)(2,1)}, u32[]{:S(2)}, u32[]{:S(2)}) %collective-permute-start.5) | collective-permute-done | bytes 1376288 | tf_op jit(solution)/shard_map/ppermute | solution.py:28
  59.3 19.5 %expert_mlp.4 = (bf16[128,1792]{1,0:T(8,128)(2,1)S(1)}, bf16[128,1792]{1,0:T(8,128)(2,1)S(1)}, bf16[128,1792]{1,0:T(8,128)(2,1)S(1)}, bf16[128,1792]{1,0:T(8,128...) custom-call(f32[512,1]{1,0:T(8,128)S(1)} %copy.33.weight, ...), custom_call_target="tpu_custom_call" | custom-call | flops 12079595520 | bytes 23592960 | tf_op jit(solution)/shard_map/expert_mlp/pallas_call | solution.py:205
  78.9 3.2 collective-permute-start.12
  86.2 7.3 %collective-permute-done.13 = bf16[128,1792]{1,0:T(8,128)(2,1)S(1)} collective-permute-done((bf16[128,1792]{1,0:T(8,128)(2,1)S(1)}, bf16[128,1792]{1,0:T(8,128)(2,1)S(1)}, u32[]{:S(2)}, u32[]{:S(2)}) %collective-permute-start.13) | collective-permute-done | bytes 458784 | tf_op jit(solution)/shard_map/ppermute | solution.py:32
  93.7 5.4 %collective-permute-done.16 = bf16[128,1792]{1,0:T(8,128)(2,1)S(1)} collective-permute-done((bf16[128,1792]{1,0:T(8,128)(2,1)S(1)}, bf16[128,1792]{1,0:T(8,128)(2,1)S(1)}, u32[]{:S(2)}, u32[]{:S(2)}) %collective-permute-start.16) | collective-permute-done | bytes 458784 | tf_op jit(solution)/shard_map/ppermute | solution.py:36
  99.3 3.3 collective-permute-start.17
  102.6 6.0 %collective-permute-done.14 = bf16[128,1792]{1,0:T(8,128)(2,1)S(1)} collective-permute-done((bf16[128,1792]{1,0:T(8,128)(2,1)S(1)}, bf16[128,1792]{1,0:T(8,128)(2,1)S(1)}, u32[]{:S(2)}, u32[]{:S(2)}) %collective-permute-start.14) | collective-permute-done | bytes 458784 | tf_op jit(solution)/shard_map/ppermute | solution.py:32
  113.5 3.4 collective-permute-start.21
  119.5 7.2 %collective-permute-done.20 = bf16[64,3584]{1,0:T(8,128)(2,1)S(1)} collective-permute-done((bf16[64,3584]{1,0:T(8,128)(2,1)S(1)}, bf16[64,3584]{1,0:T(8,128)(2,1)S(1)}, u32[]{:S(2)}, u32[]{:S(2)}) %collective-permute-start.20) | collective-permute-done | bytes 458784 | tf_op jit(solution)/shard_map/ppermute | solution.py:24
  126.7 4.2 collective-permute-done.19
  133.9 5.0 collective-permute-done.22
  138.9 4.1 collective-permute-done.23
  153.2 3.4 collective-permute-start.34
  159.8 4.8 collective-permute-start.35
  164.6 3.8 collective-permute-start.28
  171.8 7.3 %collective-permute-done.28.refs_5_ = bf16[128,1792]{1,0:T(8,128)(2,1)S(1)} collective-permute-done((bf16[128,1792]{1,0:T(8,128)(2,1)S(1)}, bf16[128,1792]{1,0:T(8,128)(2,1)S(1)}, u32[]{:S(2)}, u32[]{:S(2)}) %collective-permute-start.28) | collective-permute-done | bytes 458784 | tf_op jit(solution)/shard_map/ppermute | solution.py:36
  179.1 3.7 collective-permute-start.30
  183.1 4.2 collective-permute-done.26.refs_3_
  188.9 3.9 collective-permute-done.29.refs_6_
  192.7 19.5 %expert_mlp.5 = (bf16[128,1792]{1,0:T(8,128)(2,1)S(1)}, bf16[128,1792]{1,0:T(8,128)(2,1)S(1)}, bf16[128,1792]{1,0:T(8,128)(2,1)S(1)}, bf16[128,1792]{1,0:T(8,128...) custom-call(f32[512,1]{1,0:T(8,128)S(1)} %copy.34.weight, ...), custom_call_target="tpu_custom_call" | custom-call | flops 12079595520 | bytes 23592960 | tf_op jit(solution)/shard_map/expert_mlp/pallas_call | solution.py:205
  218.3 6.4 %collective-permute-done.37 = bf16[128,1792]{1,0:T(8,128)(2,1)S(1)} collective-permute-done((bf16[128,1792]{1,0:T(8,128)(2,1)S(1)}, bf16[128,1792]{1,0:T(8,128)(2,1)S(1)}, u32[]{:S(2)}, u32[]{:S(2)}) %collective-permute-start.37) | collective-permute-done | bytes 458784 | tf_op jit(solution)/shard_map/ppermute | solution.py:32
  225.2 6.1 %collective-permute-done.40 = bf16[128,1792]{1,0:T(8,128)(2,1)S(1)} collective-permute-done((bf16[128,1792]{1,0:T(8,128)(2,1)S(1)}, bf16[128,1792]{1,0:T(8,128)(2,1)S(1)}, u32[]{:S(2)}, u32[]{:S(2)}) %collective-permute-start.40) | collective-permute-done | bytes 458784 | tf_op jit(solution)/shard_map/ppermute | solution.py:36
  231.5 3.8 collective-permute-start.41
  235.4 5.8 %collective-permute-done.41 = bf16[128,1792]{1,0:T(8,128)(2,1)S(1)} collective-permute-done((bf16[128,1792]{1,0:T(8,128)(2,1)S(1)}, bf16[128,1792]{1,0:T(8,128)(2,1)S(1)}, u32[]{:S(2)}, u32[]{:S(2)}) %collective-permute-start.41) | collective-permute-done | bytes 458784 | tf_op jit(solution)/shard_map/ppermute | solution.py:36
  246.9 3.4 collective-permute-start.45
  252.7 6.5 %collective-permute-done.44 = bf16[64,3584]{1,0:T(8,128)(2,1)S(1)} collective-permute-done((bf16[64,3584]{1,0:T(8,128)(2,1)S(1)}, bf16[64,3584]{1,0:T(8,128)(2,1)S(1)}, u32[]{:S(2)}, u32[]{:S(2)}) %collective-permute-start.44) | collective-permute-done | bytes 458784 | tf_op jit(solution)/shard_map/ppermute | solution.py:24
  259.2 4.5 collective-permute-done.43
  266.2 7.9 %collective-permute-done.46 = bf16[64,2560]{1,0:T(8,128)(2,1)S(1)} collective-permute-done((bf16[64,2560]{1,0:T(8,128)(2,1)S(1)}, bf16[64,2560]{1,0:T(8,128)(2,1)S(1)}, u32[]{:S(2)}, u32[]{:S(2)}) %collective-permute-start.46) | collective-permute-done | bytes 327712 | tf_op jit(solution)/shard_map/ppermute | solution.py:24
  281.6 5.9 %collective-permute-done.55 = bf16[64,2560]{1,0:T(8,128)(2,1)S(1)} collective-permute-done((bf16[64,2560]{1,0:T(8,128)(2,1)S(1)}, bf16[64,2560]{1,0:T(8,128)(2,1)S(1)}, u32[]{:S(2)}, u32[]{:S(2)}) %collective-permute-start.55) | collective-permute-done | bytes 327712 | tf_op jit(solution)/shard_map/ppermute | solution.py:32
  287.7 3.3 collective-permute-start.58
  295.7 3.8 collective-permute-start.52
  302.9 7.6 %collective-permute-done.52.refs_5_ = bf16[128,1792]{1,0:T(8,128)(2,1)S(1)} collective-permute-done((bf16[128,1792]{1,0:T(8,128)(2,1)S(1)}, bf16[128,1792]{1,0:T(8,128)(2,1)S(1)}, u32[]{:S(2)}, u32[]{:S(2)}) %collective-permute-start.52) | collective-permute-done | bytes 458784 | tf_op jit(solution)/shard_map/ppermute | solution.py:36
  310.5 3.7 collective-permute-start.54
  314.6 5.2 collective-permute-done.50.refs_3_
  324.7 19.5 %expert_mlp.6 = (bf16[128,1792]{1,0:T(8,128)(2,1)S(1)}, bf16[128,1792]{1,0:T(8,128)(2,1)S(1)}, bf16[128,1792]{1,0:T(8,128)(2,1)S(1)}, bf16[128,1792]{1,0:T(8,128...) custom-call(f32[512,1]{1,0:T(8,128)S(1)} %copy.35.weight, ...), custom_call_target="tpu_custom_call" | custom-call | flops 12079595520 | bytes 23592960 | tf_op jit(solution)/shard_map/expert_mlp/pallas_call | solution.py:205
  352.3 6.6 %collective-permute-done.61 = bf16[128,1792]{1,0:T(8,128)(2,1)S(1)} collective-permute-done((bf16[128,1792]{1,0:T(8,128)(2,1)S(1)}, bf16[128,1792]{1,0:T(8,128)(2,1)S(1)}, u32[]{:S(2)}, u32[]{:S(2)}) %collective-permute-start.61) | collective-permute-done | bytes 458784 | tf_op jit(solution)/shard_map/ppermute | solution.py:32
  359.3 4.5 collective-permute-done.64
  363.9 3.8 collective-permute-start.65
  369.6 4.1 collective-permute-done.65
  379.4 3.4 collective-permute-start.69
  383.7 8.9 %collective-permute-done.68 = bf16[64,3584]{1,0:T(8,128)(2,1)S(1)} collective-permute-done((bf16[64,3584]{1,0:T(8,128)(2,1)S(1)}, bf16[64,3584]{1,0:T(8,128)(2,1)S(1)}, u32[]{:S(2)}, u32[]{:S(2)}) %collective-permute-start.68) | collective-permute-done | bytes 458784 | tf_op jit(solution)/shard_map/ppermute | solution.py:24
  399.2 7.4 %collective-permute-done.70 = bf16[64,2560]{1,0:T(8,128)(2,1)S(1)} collective-permute-done((bf16[64,2560]{1,0:T(8,128)(2,1)S(1)}, bf16[64,2560]{1,0:T(8,128)(2,1)S(1)}, u32[]{:S(2)}, u32[]{:S(2)}) %collective-permute-start.70) | collective-permute-done | bytes 327712 | tf_op jit(solution)/shard_map/ppermute | solution.py:24
  414.8 5.4 collective-permute-done.79
  420.3 3.3 collective-permute-start.82
  428.4 3.8 collective-permute-start.76
  435.5 7.6 %collective-permute-done.76.refs_5_ = bf16[128,1792]{1,0:T(8,128)(2,1)S(1)} collective-permute-done((bf16[128,1792]{1,0:T(8,128)(2,1)S(1)}, bf16[128,1792]{1,0:T(8,128)(2,1)S(1)}, u32[]{:S(2)}, u32[]{:S(2)}) %collective-permute-start.76) | collective-permute-done | bytes 458784 | tf_op jit(solution)/shard_map/ppermute | solution.py:36
  443.1 3.7 collective-permute-start.78
  447.4 5.5 %collective-permute-done.74.refs_3_ = bf16[128,1792]{1,0:T(8,128)(2,1)} collective-permute-done((bf16[128,1792]{1,0:T(8,128)(2,1)S(1)}, bf16[128,1792]{1,0:T(8,128)(2,1)}, u32[]{:S(2)}, u32[]{:S(2)}) %collective-permute-start.74) | collective-permute-done | bytes 458784 | tf_op jit(solution)/shard_map/ppermute | solution.py:32
  457.9 19.5 %expert_mlp.7 = (bf16[128,1792]{1,0:T(8,128)(2,1)S(1)}, bf16[128,1792]{1,0:T(8,128)(2,1)S(1)}, bf16[128,1792]{1,0:T(8,128)(2,1)S(1)}, bf16[128,1792]{1,0:T(8,128...) custom-call(f32[512,1]{1,0:T(8,128)S(1)} %copy.36.weight, ...), custom_call_target="tpu_custom_call" | custom-call | flops 12079595520 | bytes 23592960 | tf_op jit(solution)/shard_map/expert_mlp/pallas_call | solution.py:205
  485.2 5.7 %collective-permute-done.88 = bf16[128,1792]{1,0:T(8,128)(2,1)S(1)} collective-permute-done((bf16[128,1792]{1,0:T(8,128)(2,1)S(1)}, bf16[128,1792]{1,0:T(8,128)(2,1)S(1)}, u32[]{:S(2)}, u32[]{:S(2)}) %collective-permute-start.88) | collective-permute-done | bytes 458784 | tf_op jit(solution)/shard_map/ppermute | solution.py:36
  491.0 3.3 collective-permute-start.89
  494.3 5.3 collective-permute-done.85
  502.4 7.1 %collective-permute-done.86 = bf16[128,1792]{1,0:T(8,128)(2,1)S(1)} collective-permute-done((bf16[128,1792]{1,0:T(8,128)(2,1)S(1)}, bf16[128,1792]{1,0:T(8,128)(2,1)S(1)}, u32[]{:S(2)}, u32[]{:S(2)}) %collective-permute-start.86) | collective-permute-done | bytes 458784 | tf_op jit(solution)/shard_map/ppermute | solution.py:32
  511.3 8.7 %collective-permute-start.94 = (bf16[64,2560]{1,0:T(8,128)(2,1)S(1)}, bf16[64,2560]{1,0:T(8,128)(2,1)S(1)}, u32[]{:S(2)}, u32[]{:S(2)}) collective-permute-start(bf16[64,2560]{1,0:T(8,128)(2,1)S(1)} %get-tuple-element.113), channel_id=1, source_target_pairs={{0,10},{1,11},{2,12},{3,13},{4,14},{5,15},{6,8},{7,9},{8,18},{9,19... | collective-permute-start | bytes 983048 | tf_op jit(solution)/shard_map/ppermute | solution.py:24
  520.1 5.9 %collective-permute-done.92 = bf16[64,3584]{1,0:T(8,128)(2,1)S(1)} collective-permute-done((bf16[64,3584]{1,0:T(8,128)(2,1)S(1)}, bf16[64,3584]{1,0:T(8,128)(2,1)S(1)}, u32[]{:S(2)}, u32[]{:S(2)}) %collective-permute-start.92) | collective-permute-done | bytes 458784 | tf_op jit(solution)/shard_map/ppermute | solution.py:24
  526.0 5.1 collective-permute-done.91
  536.5 5.7 %collective-permute-done.95 = bf16[64,2560]{1,0:T(8,128)(2,1)S(1)} collective-permute-done((bf16[64,2560]{1,0:T(8,128)(2,1)S(1)}, bf16[64,2560]{1,0:T(8,128)(2,1)S(1)}, u32[]{:S(2)}, u32[]{:S(2)}) %collective-permute-start.95) | collective-permute-done | bytes 327712 | tf_op jit(solution)/shard_map/ppermute | solution.py:24
  (284 shorter events, 151.8 us)
Async XLA Ops:
  8.7 17.6 %collective-permute-start.4 = (bf16[64,3584]{1,0:T(8,128)(2,1)S(1)}, bf16[64,3584]{1,0:T(8,128)(2,1)S(1)}, u32[]{:S(2)}, u32[]{:S(2)}) collective-permute-start(bf16[64,3584]{1,0:T(8,128)(2,1)S(1)} %fusion.14), channel_id=1, source_target_pairs={{0,1},{1,0},{2,3},{3,2},{4,5},{5,4},{6,7},{7,6},{8,9},{9,8},{10,11... | collective-permute-start | bytes 1376264 | tf_op jit(solution)/shard_map/ppermute | solution.py:28
  26.3 31.3 %collective-permute-start.5 = (bf16[256,2688]{1,0:T(8,128)(2,1)S(1)}, bf16[256,2688]{1,0:T(8,128)(2,1)}, u32[]{:S(2)}, u32[]{:S(2)}) collective-permute-start(bf16[256,2688]{1,0:T(8,128)(2,1)S(1)} %maximum_maximum_fusion.refs_8_), channel_id=1, source_target_pairs={{0,1},{1,0},{2,3},{3,2},{4,5},{5,4},{6,7},{7,6},{8,9},{9,8},{10,11... | collective-permute-start | bytes 4128776 | tf_op jit(solution)/shard_map/ppermute | solution.py:28
  28.6 14.7 %collective-permute-start.6 = (bf16[128,1792]{1,0:T(8,128)(2,1)S(1)}, bf16[128,1792]{1,0:T(8,128)(2,1)S(1)}, u32[]{:S(2)}, u32[]{:S(2)}) collective-permute-start(bf16[128,1792]{1,0:T(8,128)(2,1)S(1)} %pad_maximum_fusion.8.refs_0_), channel_id=1, source_target_pairs={{0,2},{1,3},{2,4},{3,5},{4,6},{5,7},{6,0},{7,1},{8,10},{9,11},{10,... | collective-permute-start | bytes 1376264 | tf_op jit(solution)/shard_map/ppermute | solution.py:32
  28.7 14.6 %collective-permute-start.9 = (bf16[128,1792]{1,0:T(8,128)(2,1)S(1)}, bf16[128,1792]{1,0:T(8,128)(2,1)S(1)}, u32[]{:S(2)}, u32[]{:S(2)}) collective-permute-start(bf16[128,1792]{1,0:T(8,128)(2,1)S(1)} %pad_maximum_fusion.9.refs_1_), channel_id=1, source_target_pairs={{0,6},{1,7},{2,0},{3,1},{4,2},{5,3},{6,4},{7,5},{8,14},{9,15},{10,... | collective-permute-start | bytes 1376264 | tf_op jit(solution)/shard_map/ppermute | solution.py:36
  32.0 27.1 %collective-permute-start.7 = (bf16[128,1792]{1,0:T(8,128)(2,1)S(1)}, bf16[128,1792]{1,0:T(8,128)(2,1)}, u32[]{:S(2)}, u32[]{:S(2)}) collective-permute-start(bf16[128,1792]{1,0:T(8,128)(2,1)S(1)} %pad_maximum_fusion.9.refs_1_), channel_id=1, source_target_pairs={{0,2},{1,3},{2,4},{3,5},{4,6},{5,7},{6,0},{7,1},{8,10},{9,11},{10,... | collective-permute-start | bytes 1376264 | tf_op jit(solution)/shard_map/ppermute | solution.py:32
  32.0 27.1 %collective-permute-start.8 = (bf16[128,1792]{1,0:T(8,128)(2,1)S(1)}, bf16[128,1792]{1,0:T(8,128)(2,1)}, u32[]{:S(2)}, u32[]{:S(2)}) collective-permute-start(bf16[128,1792]{1,0:T(8,128)(2,1)S(1)} %pad_maximum_fusion.8.refs_0_), channel_id=1, source_target_pairs={{0,6},{1,7},{2,0},{3,1},{4,2},{5,3},{6,4},{7,5},{8,14},{9,15},{10,... | collective-permute-start | bytes 1376264 | tf_op jit(solution)/shard_map/ppermute | solution.py:36
  43.3 16.0 %collective-permute-start.10 = (bf16[128,1792]{1,0:T(8,128)(2,1)S(1)}, bf16[128,1792]{1,0:T(8,128)(2,1)}, u32[]{:S(2)}, u32[]{:S(2)}) collective-permute-start(bf16[128,1792]{1,0:T(8,128)(2,1)S(1)} %collective-permute-done.6.refs_2_), channel_id=1, source_target_pairs={{0,2},{1,3},{2,4},{3,5},{4,6},{5,7},{6,0},{7,1},{8,10},{9,11},{10,... | collective-permute-start | bytes 1376264 | tf_op jit(solution)/shard_map/ppermute | solution.py:32
  43.3 16.0 %collective-permute-start.11 = (bf16[128,1792]{1,0:T(8,128)(2,1)S(1)}, bf16[128,1792]{1,0:T(8,128)(2,1)}, u32[]{:S(2)}, u32[]{:S(2)}) collective-permute-start(bf16[128,1792]{1,0:T(8,128)(2,1)S(1)} %collective-permute-done.9.refs_5_), channel_id=1, source_target_pairs={{0,6},{1,7},{2,0},{3,1},{4,2},{5,3},{6,4},{7,5},{8,14},{9,15},{10,... | collective-permute-start | bytes 1376264 | tf_op jit(solution)/shard_map/ppermute | solution.py:36
  78.8 14.7 %collective-permute-start.13 = (bf16[128,1792]{1,0:T(8,128)(2,1)S(1)}, bf16[128,1792]{1,0:T(8,128)(2,1)S(1)}, u32[]{:S(2)}, u32[]{:S(2)}) collective-permute-start(bf16[128,1792]{1,0:T(8,128)(2,1)S(1)} %get-tuple-element.53), channel_id=1, source_target_pairs={{0,2},{1,3},{2,4},{3,5},{4,6},{5,7},{6,0},{7,1},{8,10},{9,11},{10,... | collective-permute-start | bytes 1376264 | tf_op jit(solution)/shard_map/ppermute | solution.py:32
  78.9 23.7 %collective-permute-start.12 = (bf16[128,1792]{1,0:T(8,128)(2,1)S(1)}, bf16[128,1792]{1,0:T(8,128)(2,1)S(1)}, u32[]{:S(2)}, u32[]{:S(2)}) collective-permute-start(bf16[128,1792]{1,0:T(8,128)(2,1)S(1)} %get-tuple-element.51), channel_id=1, source_target_pairs={{0,6},{1,7},{2,0},{3,1},{4,2},{5,3},{6,4},{7,5},{8,14},{9,15},{10,... | collective-permute-start | bytes 1376264 | tf_op jit(solution)/shard_map/ppermute | solution.py:36
  82.1 17.1 %collective-permute-start.16 = (bf16[128,1792]{1,0:T(8,128)(2,1)S(1)}, bf16[128,1792]{1,0:T(8,128)(2,1)S(1)}, u32[]{:S(2)}, u32[]{:S(2)}) collective-permute-start(bf16[128,1792]{1,0:T(8,128)(2,1)S(1)} %get-tuple-element.57), channel_id=1, source_target_pairs={{0,6},{1,7},{2,0},{3,1},{4,2},{5,3},{6,4},{7,5},{8,14},{9,15},{10,... | collective-permute-start | bytes 1376264 | tf_op jit(solution)/shard_map/ppermute | solution.py:36
  83.9 24.8 %collective-permute-start.15 = (bf16[128,1792]{1,0:T(8,128)(2,1)S(1)}, bf16[128,1792]{1,0:T(8,128)(2,1)S(1)}, u32[]{:S(2)}, u32[]{:S(2)}) collective-permute-start(bf16[128,1792]{1,0:T(8,128)(2,1)S(1)} %get-tuple-element.55), channel_id=1, source_target_pairs={{0,2},{1,3},{2,4},{3,5},{4,6},{5,7},{6,0},{7,1},{8,10},{9,11},{10,... | collective-permute-start | bytes 1376264 | tf_op jit(solution)/shard_map/ppermute | solution.py:32
  84.1 27.7 %collective-permute-start.18 = (bf16[256,2560]{1,0:T(8,128)(2,1)S(1)}, bf16[256,2560]{1,0:T(8,128)(2,1)S(1)}, u32[]{:S(2)}, u32[]{:S(2)}) collective-permute-start(bf16[256,2560]{1,0:T(8,128)(2,1)S(1)} %get-tuple-element.59), channel_id=1, source_target_pairs={{0,1},{1,0},{2,3},{3,2},{4,5},{5,4},{6,7},{7,6},{8,9},{9,8},{10,11... | collective-permute-start | bytes 3932168 | tf_op jit(solution)/shard_map/ppermute | solution.py:28
  93.6 15.0 %collective-permute-start.14 = (bf16[128,1792]{1,0:T(8,128)(2,1)S(1)}, bf16[128,1792]{1,0:T(8,128)(2,1)S(1)}, u32[]{:S(2)}, u32[]{:S(2)}) collective-permute-start(bf16[128,1792]{1,0:T(8,128)(2,1)S(1)} %add_convert_fusion.11), channel_id=1, source_target_pairs={{0,2},{1,3},{2,4},{3,5},{4,6},{5,7},{6,0},{7,1},{8,10},{9,11},{10,... | collective-permute-start | bytes 1376264 | tf_op jit(solution)/shard_map/ppermute | solution.py:32
  109.0 17.7 %collective-permute-start.20 = (bf16[64,3584]{1,0:T(8,128)(2,1)S(1)}, bf16[64,3584]{1,0:T(8,128)(2,1)S(1)}, u32[]{:S(2)}, u32[]{:S(2)}) collective-permute-start(bf16[64,3584]{1,0:T(8,128)(2,1)S(1)} %fusion.23), channel_id=1, source_target_pairs={{0,9},{1,8},{2,11},{3,10},{4,13},{5,12},{6,15},{7,14},{8,17},{9,16... | collective-permute-start | bytes 1376264 | tf_op jit(solution)/shard_map/ppermute | solution.py:24
  112.4 18.6 %collective-permute-start.19 = (bf16[64,6144]{1,0:T(8,128)(2,1)S(1)}, bf16[64,6144]{1,0:T(8,128)(2,1)S(1)}, u32[]{:S(2)}, u32[]{:S(2)}) collective-permute-start(bf16[64,6144]{1,0:T(8,128)(2,1)S(1)} %pad_maximum_fusion.4), channel_id=1, source_target_pairs={{0,8},{1,9},{2,10},{3,11},{4,12},{5,13},{6,14},{7,15},{8,16},{9,17... | collective-permute-start | bytes 2359304 | tf_op jit(solution)/shard_map/ppermute | solution.py:24
  113.5 20.4 %collective-permute-start.21 = (bf16[64,2560]{1,0:T(8,128)(2,1)S(1)}, bf16[64,2560]{1,0:T(8,128)(2,1)S(1)}, u32[]{:S(2)}, u32[]{:S(2)}) collective-permute-start(bf16[64,2560]{1,0:T(8,128)(2,1)S(1)} %get-tuple-element.120), channel_id=1, source_target_pairs={{0,14},{1,15},{2,8},{3,9},{4,10},{5,11},{6,12},{7,13},{8,22},{9,23... | collective-permute-start | bytes 983048 | tf_op jit(solution)/shard_map/ppermute | solution.py:24
  116.9 22.0 %collective-permute-start.22 = (bf16[64,2560]{1,0:T(8,128)(2,1)S(1)}, bf16[64,2560]{1,0:T(8,128)(2,1)S(1)}, u32[]{:S(2)}, u32[]{:S(2)}) collective-permute-start(bf16[64,2560]{1,0:T(8,128)(2,1)S(1)} %get-tuple-element.122), channel_id=1, source_target_pairs={{0,10},{1,11},{2,12},{3,13},{4,14},{5,15},{6,8},{7,9},{8,18},{9,19... | collective-permute-start | bytes 983048 | tf_op jit(solution)/shard_map/ppermute | solution.py:24
  116.9 26.0 %collective-permute-start.23 = (bf16[64,2560]{1,0:T(8,128)(2,1)S(1)}, bf16[64,2560]{1,0:T(8,128)(2,1)S(1)}, u32[]{:S(2)}, u32[]{:S(2)}) collective-permute-start(bf16[64,2560]{1,0:T(8,128)(2,1)S(1)} %get-tuple-element.121), channel_id=1, source_target_pairs={{0,12},{1,13},{2,14},{3,15},{4,8},{5,9},{6,10},{7,11},{8,20},{9,21... | collective-permute-start | bytes 983048 | tf_op jit(solution)/shard_map/ppermute | solution.py:24
  159.8 33.0 %collective-permute-start.35 = (bf16[256,2560]{1,0:T(8,128)(2,1)S(1)}, bf16[256,2560]{1,0:T(8,128)(2,1)}, u32[]{:S(2)}, u32[]{:S(2)}) collective-permute-start(bf16[256,2560]{1,0:T(8,128)(2,1)S(1)} %maximum_maximum_fusion.1.refs_8_), channel_id=1, source_target_pairs={{0,1},{1,0},{2,3},{3,2},{4,5},{5,4},{6,7},{7,6},{8,9},{9,8},{10,11... | collective-permute-start | bytes 3932168 | tf_op jit(solution)/shard_map/ppermute | solution.py:28
  164.6 14.4 %collective-permute-start.28 = (bf16[128,1792]{1,0:T(8,128)(2,1)S(1)}, bf16[128,1792]{1,0:T(8,128)(2,1)S(1)}, u32[]{:S(2)}, u32[]{:S(2)}) collective-permute-start(bf16[128,1792]{1,0:T(8,128)(2,1)S(1)} %pad_maximum_fusion.11.refs_1_), channel_id=1, source_target_pairs={{0,6},{1,7},{2,0},{3,1},{4,2},{5,3},{6,4},{7,5},{8,14},{9,15},{10,... | collective-permute-start | bytes 1376264 | tf_op jit(solution)/shard_map/ppermute | solution.py:36
  168.4 14.3 %collective-permute-start.25 = (bf16[128,1792]{1,0:T(8,128)(2,1)S(1)}, bf16[128,1792]{1,0:T(8,128)(2,1)S(1)}, u32[]{:S(2)}, u32[]{:S(2)}) collective-permute-start(bf16[128,1792]{1,0:T(8,128)(2,1)S(1)} %pad_maximum_fusion.10.refs_0_), channel_id=1, source_target_pairs={{0,2},{1,3},{2,4},{3,5},{4,6},{5,7},{6,0},{7,1},{8,10},{9,11},{10,... | collective-permute-start | bytes 1376264 | tf_op jit(solution)/shard_map/ppermute | solution.py:32
  168.5 18.9 %collective-permute-start.26 = (bf16[128,1792]{1,0:T(8,128)(2,1)S(1)}, bf16[128,1792]{1,0:T(8,128)(2,1)}, u32[]{:S(2)}, u32[]{:S(2)}) collective-permute-start(bf16[128,1792]{1,0:T(8,128)(2,1)S(1)} %pad_maximum_fusion.11.refs_1_), channel_id=1, source_target_pairs={{0,2},{1,3},{2,4},{3,5},{4,6},{5,7},{6,0},{7,1},{8,10},{9,11},{10,... | collective-permute-start | bytes 1376264 | tf_op jit(solution)/shard_map/ppermute | solution.py:32
  168.6 18.8 %collective-permute-start.27 = (bf16[128,1792]{1,0:T(8,128)(2,1)S(1)}, bf16[128,1792]{1,0:T(8,128)(2,1)}, u32[]{:S(2)}, u32[]{:S(2)}) collective-permute-start(bf16[128,1792]{1,0:T(8,128)(2,1)S(1)} %pad_maximum_fusion.10.refs_0_), channel_id=1, source_target_pairs={{0,6},{1,7},{2,0},{3,1},{4,2},{5,3},{6,4},{7,5},{8,14},{9,15},{10,... | collective-permute-start | bytes 1376264 | tf_op jit(solution)/shard_map/ppermute | solution.py:36
  212.3 22.9 %collective-permute-start.36 = (bf16[128,1792]{1,0:T(8,128)(2,1)S(1)}, bf16[128,1792]{1,0:T(8,128)(2,1)S(1)}, u32[]{:S(2)}, u32[]{:S(2)}) collective-permute-start(bf16[128,1792]{1,0:T(8,128)(2,1)S(1)} %get-tuple-element.62), channel_id=1, source_target_pairs={{0,6},{1,7},{2,0},{3,1},{4,2},{5,3},{6,4},{7,5},{8,14},{9,15},{10,... | collective-permute-start | bytes 1376264 | tf_op jit(solution)/shard_map/ppermute | solution.py:36
  215.5 15.8 %collective-permute-start.40 = (bf16[128,1792]{1,0:T(8,128)(2,1)S(1)}, bf16[128,1792]{1,0:T(8,128)(2,1)S(1)}, u32[]{:S(2)}, u32[]{:S(2)}) collective-permute-start(bf16[128,1792]{1,0:T(8,128)(2,1)S(1)} %get-tuple-element.68), channel_id=1, source_target_pairs={{0,6},{1,7},{2,0},{3,1},{4,2},{5,3},{6,4},{7,5},{8,14},{9,15},{10,... | collective-permute-start | bytes 1376264 | tf_op jit(solution)/shard_map/ppermute | solution.py:36
  215.6 19.8 %collective-permute-start.39 = (bf16[128,1792]{1,0:T(8,128)(2,1)S(1)}, bf16[128,1792]{1,0:T(8,128)(2,1)S(1)}, u32[]{:S(2)}, u32[]{:S(2)}) collective-permute-start(bf16[128,1792]{1,0:T(8,128)(2,1)S(1)} %get-tuple-element.66), channel_id=1, source_target_pairs={{0,2},{1,3},{2,4},{3,5},{4,6},{5,7},{6,0},{7,1},{8,10},{9,11},{10,... | collective-permute-start | bytes 1376264 | tf_op jit(solution)/shard_map/ppermute | solution.py:32
  217.6 25.2 %collective-permute-start.42 = (bf16[256,2560]{1,0:T(8,128)(2,1)S(1)}, bf16[256,2560]{1,0:T(8,128)(2,1)S(1)}, u32[]{:S(2)}, u32[]{:S(2)}) collective-permute-start(bf16[256,2560]{1,0:T(8,128)(2,1)S(1)} %get-tuple-element.70), channel_id=1, source_target_pairs={{0,1},{1,0},{2,3},{3,2},{4,5},{5,4},{6,7},{7,6},{8,9},{9,8},{10,11... | collective-permute-start | bytes 3932168 | tf_op jit(solution)/shard_map/ppermute | solution.py:28
  241.5 17.8 %collective-permute-start.44 = (bf16[64,3584]{1,0:T(8,128)(2,1)S(1)}, bf16[64,3584]{1,0:T(8,128)(2,1)S(1)}, u32[]{:S(2)}, u32[]{:S(2)}) collective-permute-start(bf16[64,3584]{1,0:T(8,128)(2,1)S(1)} %fusion.22), channel_id=1, source_target_pairs={{0,9},{1,8},{2,11},{3,10},{4,13},{5,12},{6,15},{7,14},{8,17},{9,16... | collective-permute-start | bytes 1376264 | tf_op jit(solution)/shard_map/ppermute | solution.py:24
  243.9 19.8 %collective-permute-start.43 = (bf16[64,6144]{1,0:T(8,128)(2,1)S(1)}, bf16[64,6144]{1,0:T(8,128)(2,1)S(1)}, u32[]{:S(2)}, u32[]{:S(2)}) collective-permute-start(bf16[64,6144]{1,0:T(8,128)(2,1)S(1)} %pad_maximum_fusion.5), channel_id=1, source_target_pairs={{0,8},{1,9},{2,10},{3,11},{4,12},{5,13},{6,14},{7,15},{8,16},{9,17... | collective-permute-start | bytes 2359304 | tf_op jit(solution)/shard_map/ppermute | solution.py:24
  246.9 19.3 %collective-permute-start.45 = (bf16[64,2560]{1,0:T(8,128)(2,1)S(1)}, bf16[64,2560]{1,0:T(8,128)(2,1)S(1)}, u32[]{:S(2)}, u32[]{:S(2)}) collective-permute-start(bf16[64,2560]{1,0:T(8,128)(2,1)S(1)} %get-tuple-element.117), channel_id=1, source_target_pairs={{0,14},{1,15},{2,8},{3,9},{4,10},{5,11},{6,12},{7,13},{8,22},{9,23... | collective-permute-start | bytes 983048 | tf_op jit(solution)/shard_map/ppermute | solution.py:24
  250.3 23.8 %collective-permute-start.46 = (bf16[64,2560]{1,0:T(8,128)(2,1)S(1)}, bf16[64,2560]{1,0:T(8,128)(2,1)S(1)}, u32[]{:S(2)}, u32[]{:S(2)}) collective-permute-start(bf16[64,2560]{1,0:T(8,128)(2,1)S(1)} %get-tuple-element.119), channel_id=1, source_target_pairs={{0,10},{1,11},{2,12},{3,13},{4,14},{5,15},{6,8},{7,9},{8,18},{9,19... | collective-permute-start | bytes 983048 | tf_op jit(solution)/shard_map/ppermute | solution.py:24
  250.3 26.7 %collective-permute-start.47 = (bf16[64,2560]{1,0:T(8,128)(2,1)S(1)}, bf16[64,2560]{1,0:T(8,128)(2,1)S(1)}, u32[]{:S(2)}, u32[]{:S(2)}) collective-permute-start(bf16[64,2560]{1,0:T(8,128)(2,1)S(1)} %get-tuple-element.118), channel_id=1, source_target_pairs={{0,12},{1,13},{2,14},{3,15},{4,8},{5,9},{6,10},{7,11},{8,20},{9,21... | collective-permute-start | bytes 983048 | tf_op jit(solution)/shard_map/ppermute | solution.py:24
  295.6 29.1 %collective-permute-start.59 = (bf16[256,2560]{1,0:T(8,128)(2,1)S(1)}, bf16[256,2560]{1,0:T(8,128)(2,1)}, u32[]{:S(2)}, u32[]{:S(2)}) collective-permute-start(bf16[256,2560]{1,0:T(8,128)(2,1)S(1)} %maximum_maximum_fusion.2.refs_8_), channel_id=1, source_target_pairs={{0,1},{1,0},{2,3},{3,2},{4,5},{5,4},{6,7},{7,6},{8,9},{9,8},{10,11... | collective-permute-start | bytes 3932168 | tf_op jit(solution)/shard_map/ppermute | solution.py:28
  295.7 14.7 %collective-permute-start.52 = (bf16[128,1792]{1,0:T(8,128)(2,1)S(1)}, bf16[128,1792]{1,0:T(8,128)(2,1)S(1)}, u32[]{:S(2)}, u32[]{:S(2)}) collective-permute-start(bf16[128,1792]{1,0:T(8,128)(2,1)S(1)} %pad_maximum_fusion.13.refs_1_), channel_id=1, source_target_pairs={{0,6},{1,7},{2,0},{3,1},{4,2},{5,3},{6,4},{7,5},{8,14},{9,15},{10,... | collective-permute-start | bytes 1376264 | tf_op jit(solution)/shard_map/ppermute | solution.py:36
  299.5 14.7 %collective-permute-start.49 = (bf16[128,1792]{1,0:T(8,128)(2,1)S(1)}, bf16[128,1792]{1,0:T(8,128)(2,1)S(1)}, u32[]{:S(2)}, u32[]{:S(2)}) collective-permute-start(bf16[128,1792]{1,0:T(8,128)(2,1)S(1)} %pad_maximum_fusion.12.refs_0_), channel_id=1, source_target_pairs={{0,2},{1,3},{2,4},{3,5},{4,6},{5,7},{6,0},{7,1},{8,10},{9,11},{10,... | collective-permute-start | bytes 1376264 | tf_op jit(solution)/shard_map/ppermute | solution.py:32
  299.6 20.2 %collective-permute-start.50 = (bf16[128,1792]{1,0:T(8,128)(2,1)S(1)}, bf16[128,1792]{1,0:T(8,128)(2,1)}, u32[]{:S(2)}, u32[]{:S(2)}) collective-permute-start(bf16[128,1792]{1,0:T(8,128)(2,1)S(1)} %pad_maximum_fusion.13.refs_1_), channel_id=1, source_target_pairs={{0,2},{1,3},{2,4},{3,5},{4,6},{5,7},{6,0},{7,1},{8,10},{9,11},{10,... | collective-permute-start | bytes 1376264 | tf_op jit(solution)/shard_map/ppermute | solution.py:32
  299.7 20.1 %collective-permute-start.51 = (bf16[128,1792]{1,0:T(8,128)(2,1)S(1)}, bf16[128,1792]{1,0:T(8,128)(2,1)}, u32[]{:S(2)}, u32[]{:S(2)}) collective-permute-start(bf16[128,1792]{1,0:T(8,128)(2,1)S(1)} %pad_maximum_fusion.12.refs_0_), channel_id=1, source_target_pairs={{0,6},{1,7},{2,0},{3,1},{4,2},{5,3},{6,4},{7,5},{8,14},{9,15},{10,... | collective-permute-start | bytes 1376264 | tf_op jit(solution)/shard_map/ppermute | solution.py:36
  344.2 14.7 %collective-permute-start.61 = (bf16[128,1792]{1,0:T(8,128)(2,1)S(1)}, bf16[128,1792]{1,0:T(8,128)(2,1)S(1)}, u32[]{:S(2)}, u32[]{:S(2)}) collective-permute-start(bf16[128,1792]{1,0:T(8,128)(2,1)S(1)} %get-tuple-element.75), channel_id=1, source_target_pairs={{0,2},{1,3},{2,4},{3,5},{4,6},{5,7},{6,0},{7,1},{8,10},{9,11},{10,... | collective-permute-start | bytes 1376264 | tf_op jit(solution)/shard_map/ppermute | solution.py:32
  344.3 23.4 %collective-permute-start.60 = (bf16[128,1792]{1,0:T(8,128)(2,1)S(1)}, bf16[128,1792]{1,0:T(8,128)(2,1)S(1)}, u32[]{:S(2)}, u32[]{:S(2)}) collective-permute-start(bf16[128,1792]{1,0:T(8,128)(2,1)S(1)} %get-tuple-element.73), channel_id=1, source_target_pairs={{0,6},{1,7},{2,0},{3,1},{4,2},{5,3},{6,4},{7,5},{8,14},{9,15},{10,... | collective-permute-start | bytes 1376264 | tf_op jit(solution)/shard_map/ppermute | solution.py:36
  347.5 16.3 %collective-permute-start.64 = (bf16[128,1792]{1,0:T(8,128)(2,1)S(1)}, bf16[128,1792]{1,0:T(8,128)(2,1)S(1)}, u32[]{:S(2)}, u32[]{:S(2)}) collective-permute-start(bf16[128,1792]{1,0:T(8,128)(2,1)S(1)} %get-tuple-element.79), channel_id=1, source_target_pairs={{0,6},{1,7},{2,0},{3,1},{4,2},{5,3},{6,4},{7,5},{8,14},{9,15},{10,... | collective-permute-start | bytes 1376264 | tf_op jit(solution)/shard_map/ppermute | solution.py:36
  348.2 21.3 %collective-permute-start.63 = (bf16[128,1792]{1,0:T(8,128)(2,1)S(1)}, bf16[128,1792]{1,0:T(8,128)(2,1)S(1)}, u32[]{:S(2)}, u32[]{:S(2)}) collective-permute-start(bf16[128,1792]{1,0:T(8,128)(2,1)S(1)} %get-tuple-element.77), channel_id=1, source_target_pairs={{0,2},{1,3},{2,4},{3,5},{4,6},{5,7},{6,0},{7,1},{8,10},{9,11},{10,... | collective-permute-start | bytes 1376264 | tf_op jit(solution)/shard_map/ppermute | solution.py:32
  349.5 25.7 %collective-permute-start.66 = (bf16[256,2560]{1,0:T(8,128)(2,1)S(1)}, bf16[256,2560]{1,0:T(8,128)(2,1)S(1)}, u32[]{:S(2)}, u32[]{:S(2)}) collective-permute-start(bf16[256,2560]{1,0:T(8,128)(2,1)S(1)} %get-tuple-element.81), channel_id=1, source_target_pairs={{0,1},{1,0},{2,3},{3,2},{4,5},{5,4},{6,7},{7,6},{8,9},{9,8},{10,11... | collective-permute-start | bytes 3932168 | tf_op jit(solution)/shard_map/ppermute | solution.py:28
  373.9 18.7 %collective-permute-start.68 = (bf16[64,3584]{1,0:T(8,128)(2,1)S(1)}, bf16[64,3584]{1,0:T(8,128)(2,1)S(1)}, u32[]{:S(2)}, u32[]{:S(2)}) collective-permute-start(bf16[64,3584]{1,0:T(8,128)(2,1)S(1)} %fusion.21), channel_id=1, source_target_pairs={{0,9},{1,8},{2,11},{3,10},{4,13},{5,12},{6,15},{7,14},{8,17},{9,16... | collective-permute-start | bytes 1376264 | tf_op jit(solution)/shard_map/ppermute | solution.py:24
  376.4 19.5 %collective-permute-start.67 = (bf16[64,6144]{1,0:T(8,128)(2,1)S(1)}, bf16[64,6144]{1,0:T(8,128)(2,1)S(1)}, u32[]{:S(2)}, u32[]{:S(2)}) collective-permute-start(bf16[64,6144]{1,0:T(8,128)(2,1)S(1)} %pad_maximum_fusion.6), channel_id=1, source_target_pairs={{0,8},{1,9},{2,10},{3,11},{4,12},{5,13},{6,14},{7,15},{8,16},{9,17... | collective-permute-start | bytes 2359304 | tf_op jit(solution)/shard_map/ppermute | solution.py:24
  379.4 19.8 %collective-permute-start.69 = (bf16[64,2560]{1,0:T(8,128)(2,1)S(1)}, bf16[64,2560]{1,0:T(8,128)(2,1)S(1)}, u32[]{:S(2)}, u32[]{:S(2)}) collective-permute-start(bf16[64,2560]{1,0:T(8,128)(2,1)S(1)} %get-tuple-element.114), channel_id=1, source_target_pairs={{0,14},{1,15},{2,8},{3,9},{4,10},{5,11},{6,12},{7,13},{8,22},{9,23... | collective-permute-start | bytes 983048 | tf_op jit(solution)/shard_map/ppermute | solution.py:24
  382.8 23.8 %collective-permute-start.70 = (bf16[64,2560]{1,0:T(8,128)(2,1)S(1)}, bf16[64,2560]{1,0:T(8,128)(2,1)S(1)}, u32[]{:S(2)}, u32[]{:S(2)}) collective-permute-start(bf16[64,2560]{1,0:T(8,128)(2,1)S(1)} %get-tuple-element.116), channel_id=1, source_target_pairs={{0,10},{1,11},{2,12},{3,13},{4,14},{5,15},{6,8},{7,9},{8,18},{9,19... | collective-permute-start | bytes 983048 | tf_op jit(solution)/shard_map/ppermute | solution.py:24
  382.8 26.8 %collective-permute-start.71 = (bf16[64,2560]{1,0:T(8,128)(2,1)S(1)}, bf16[64,2560]{1,0:T(8,128)(2,1)S(1)}, u32[]{:S(2)}, u32[]{:S(2)}) collective-permute-start(bf16[64,2560]{1,0:T(8,128)(2,1)S(1)} %get-tuple-element.115), channel_id=1, source_target_pairs={{0,12},{1,13},{2,14},{3,15},{4,8},{5,9},{6,10},{7,11},{8,20},{9,21... | collective-permute-start | bytes 983048 | tf_op jit(solution)/shard_map/ppermute | solution.py:24
  428.2 29.7 %collective-permute-start.83 = (bf16[256,2560]{1,0:T(8,128)(2,1)S(1)}, bf16[256,2560]{1,0:T(8,128)(2,1)}, u32[]{:S(2)}, u32[]{:S(2)}) collective-permute-start(bf16[256,2560]{1,0:T(8,128)(2,1)S(1)} %maximum_maximum_fusion.3.refs_8_), channel_id=1, source_target_pairs={{0,1},{1,0},{2,3},{3,2},{4,5},{5,4},{6,7},{7,6},{8,9},{9,8},{10,11... | collective-permute-start | bytes 3932168 | tf_op jit(solution)/shard_map/ppermute | solution.py:28
  428.4 14.7 %collective-permute-start.76 = (bf16[128,1792]{1,0:T(8,128)(2,1)S(1)}, bf16[128,1792]{1,0:T(8,128)(2,1)S(1)}, u32[]{:S(2)}, u32[]{:S(2)}) collective-permute-start(bf16[128,1792]{1,0:T(8,128)(2,1)S(1)} %pad_maximum_fusion.15.refs_1_), channel_id=1, source_target_pairs={{0,6},{1,7},{2,0},{3,1},{4,2},{5,3},{6,4},{7,5},{8,14},{9,15},{10,... | collective-permute-start | bytes 1376264 | tf_op jit(solution)/shard_map/ppermute | solution.py:36
  432.1 14.7 %collective-permute-start.73 = (bf16[128,1792]{1,0:T(8,128)(2,1)S(1)}, bf16[128,1792]{1,0:T(8,128)(2,1)S(1)}, u32[]{:S(2)}, u32[]{:S(2)}) collective-permute-start(bf16[128,1792]{1,0:T(8,128)(2,1)S(1)} %pad_maximum_fusion.14.refs_0_), channel_id=1, source_target_pairs={{0,2},{1,3},{2,4},{3,5},{4,6},{5,7},{6,0},{7,1},{8,10},{9,11},{10,... | collective-permute-start | bytes 1376264 | tf_op jit(solution)/shard_map/ppermute | solution.py:32
  432.2 20.7 %collective-permute-start.74 = (bf16[128,1792]{1,0:T(8,128)(2,1)S(1)}, bf16[128,1792]{1,0:T(8,128)(2,1)}, u32[]{:S(2)}, u32[]{:S(2)}) collective-permute-start(bf16[128,1792]{1,0:T(8,128)(2,1)S(1)} %pad_maximum_fusion.15.refs_1_), channel_id=1, source_target_pairs={{0,2},{1,3},{2,4},{3,5},{4,6},{5,7},{6,0},{7,1},{8,10},{9,11},{10,... | collective-permute-start | bytes 1376264 | tf_op jit(solution)/shard_map/ppermute | solution.py:32
  432.3 20.7 %collective-permute-start.75 = (bf16[128,1792]{1,0:T(8,128)(2,1)S(1)}, bf16[128,1792]{1,0:T(8,128)(2,1)}, u32[]{:S(2)}, u32[]{:S(2)}) collective-permute-start(bf16[128,1792]{1,0:T(8,128)(2,1)S(1)} %pad_maximum_fusion.14.refs_0_), channel_id=1, source_target_pairs={{0,6},{1,7},{2,0},{3,1},{4,2},{5,3},{6,4},{7,5},{8,14},{9,15},{10,... | collective-permute-start | bytes 1376264 | tf_op jit(solution)/shard_map/ppermute | solution.py:36
  443.1 12.9 %collective-permute-start.78 = (bf16[128,1792]{1,0:T(8,128)(2,1)S(1)}, bf16[128,1792]{1,0:T(8,128)(2,1)}, u32[]{:S(2)}, u32[]{:S(2)}) collective-permute-start(bf16[128,1792]{1,0:T(8,128)(2,1)S(1)} %collective-permute-done.76.refs_5_), channel_id=1, source_target_pairs={{0,6},{1,7},{2,0},{3,1},{4,2},{5,3},{6,4},{7,5},{8,14},{9,15},{10,... | collective-permute-start | bytes 1376264 | tf_op jit(solution)/shard_map/ppermute | solution.py:36
  477.4 13.5 %collective-permute-start.88 = (bf16[128,1792]{1,0:T(8,128)(2,1)S(1)}, bf16[128,1792]{1,0:T(8,128)(2,1)S(1)}, u32[]{:S(2)}, u32[]{:S(2)}) collective-permute-start(bf16[128,1792]{1,0:T(8,128)(2,1)S(1)} %get-tuple-element.90), channel_id=1, source_target_pairs={{0,6},{1,7},{2,0},{3,1},{4,2},{5,3},{6,4},{7,5},{8,14},{9,15},{10,... | collective-permute-start | bytes 1376264 | tf_op jit(solution)/shard_map/ppermute | solution.py:36
  479.3 20.5 %collective-permute-start.87 = (bf16[128,1792]{1,0:T(8,128)(2,1)S(1)}, bf16[128,1792]{1,0:T(8,128)(2,1)S(1)}, u32[]{:S(2)}, u32[]{:S(2)}) collective-permute-start(bf16[128,1792]{1,0:T(8,128)(2,1)S(1)} %get-tuple-element.88), channel_id=1, source_target_pairs={{0,2},{1,3},{2,4},{3,5},{4,6},{5,7},{6,0},{7,1},{8,10},{9,11},{10,... | collective-permute-start | bytes 1376264 | tf_op jit(solution)/shard_map/ppermute | solution.py:32
  479.5 20.2 %collective-permute-start.85 = (bf16[128,1792]{1,0:T(8,128)(2,1)S(1)}, bf16[128,1792]{1,0:T(8,128)(2,1)S(1)}, u32[]{:S(2)}, u32[]{:S(2)}) collective-permute-start(bf16[128,1792]{1,0:T(8,128)(2,1)S(1)} %get-tuple-element.86), channel_id=1, source_target_pairs={{0,2},{1,3},{2,4},{3,5},{4,6},{5,7},{6,0},{7,1},{8,10},{9,11},{10,... | collective-permute-start | bytes 1376264 | tf_op jit(solution)/shard_map/ppermute | solution.py:32
  479.5 22.9 %collective-permute-start.84 = (bf16[128,1792]{1,0:T(8,128)(2,1)S(1)}, bf16[128,1792]{1,0:T(8,128)(2,1)S(1)}, u32[]{:S(2)}, u32[]{:S(2)}) collective-permute-start(bf16[128,1792]{1,0:T(8,128)(2,1)S(1)} %get-tuple-element.84), channel_id=1, source_target_pairs={{0,6},{1,7},{2,0},{3,1},{4,2},{5,3},{6,4},{7,5},{8,14},{9,15},{10,... | collective-permute-start | bytes 1376264 | tf_op jit(solution)/shard_map/ppermute | solution.py:36
  482.7 27.1 %collective-permute-start.90 = (bf16[256,2560]{1,0:T(8,128)(2,1)S(1)}, bf16[256,2560]{1,0:T(8,128)(2,1)S(1)}, u32[]{:S(2)}, u32[]{:S(2)}) collective-permute-start(bf16[256,2560]{1,0:T(8,128)(2,1)S(1)} %get-tuple-element.92), channel_id=1, source_target_pairs={{0,1},{1,0},{2,3},{3,2},{4,5},{5,4},{6,7},{7,6},{8,9},{9,8},{10,11... | collective-permute-start | bytes 3932168 | tf_op jit(solution)/shard_map/ppermute | solution.py:28
  510.9 20.1 %collective-permute-start.91 = (bf16[64,6144]{1,0:T(8,128)(2,1)S(1)}, bf16[64,6144]{1,0:T(8,128)(2,1)S(1)}, u32[]{:S(2)}, u32[]{:S(2)}) collective-permute-start(bf16[64,6144]{1,0:T(8,128)(2,1)S(1)} %pad_maximum_fusion.7), channel_id=1, source_target_pairs={{0,8},{1,9},{2,10},{3,11},{4,12},{5,13},{6,14},{7,15},{8,16},{9,17... | collective-permute-start | bytes 2359304 | tf_op jit(solution)/shard_map/ppermute | solution.py:24
  511.1 14.9 %collective-permute-start.92 = (bf16[64,3584]{1,0:T(8,128)(2,1)S(1)}, bf16[64,3584]{1,0:T(8,128)(2,1)S(1)}, u32[]{:S(2)}, u32[]{:S(2)}) collective-permute-start(bf16[64,3584]{1,0:T(8,128)(2,1)S(1)} %fusion.20), channel_id=1, source_target_pairs={{0,9},{1,8},{2,11},{3,10},{4,13},{5,12},{6,15},{7,14},{8,17},{9,16... | collective-permute-start | bytes 1376264 | tf_op jit(solution)/shard_map/ppermute | solution.py:24
  511.2 22.7 %collective-permute-start.93 = (bf16[64,2560]{1,0:T(8,128)(2,1)S(1)}, bf16[64,2560]{1,0:T(8,128)(2,1)S(1)}, u32[]{:S(2)}, u32[]{:S(2)}) collective-permute-start(bf16[64,2560]{1,0:T(8,128)(2,1)S(1)} %get-tuple-element.111), channel_id=1, source_target_pairs={{0,14},{1,15},{2,8},{3,9},{4,10},{5,11},{6,12},{7,13},{8,22},{9,23... | collective-permute-start | bytes 983048 | tf_op jit(solution)/shard_map/ppermute | solution.py:24
  511.3 25.1 %collective-permute-start.94 = (bf16[64,2560]{1,0:T(8,128)(2,1)S(1)}, bf16[64,2560]{1,0:T(8,128)(2,1)S(1)}, u32[]{:S(2)}, u32[]{:S(2)}) collective-permute-start(bf16[64,2560]{1,0:T(8,128)(2,1)S(1)} %get-tuple-element.113), channel_id=1, source_target_pairs={{0,10},{1,11},{2,12},{3,13},{4,14},{5,15},{6,8},{7,9},{8,18},{9,19... | collective-permute-start | bytes 983048 | tf_op jit(solution)/shard_map/ppermute | solution.py:24
  520.0 22.2 %collective-permute-start.95 = (bf16[64,2560]{1,0:T(8,128)(2,1)S(1)}, bf16[64,2560]{1,0:T(8,128)(2,1)S(1)}, u32[]{:S(2)}, u32[]{:S(2)}) collective-permute-start(bf16[64,2560]{1,0:T(8,128)(2,1)S(1)} %get-tuple-element.112), channel_id=1, source_target_pairs={{0,12},{1,13},{2,14},{3,15},{4,8},{5,9},{6,10},{7,11},{8,20},{9,21... | collective-permute-start | bytes 983048 | tf_op jit(solution)/shard_map/ppermute | solution.py:24
  (53 other events, 488.6 us)
